TPU v7x, 32 devices: a whole 2x2x4 slice. The times are simulated.
32 devices in a mesh: groups: 1, expert: 32 (over z, y, x, core).
Axes of the slice: x: 2, y: 2, z: 4, core: 2. Of those that a mesh axis runs over, the one named last changes fastest.
Arguments:
- gate_pre: bfloat16 [32, 3072, 640], P(('groups', 'expert')), may hold values from -6 to 6
- up_pre: bfloat16 [32, 3072, 640], P(('groups', 'expert')), may hold values from -6 to 6
- hidden_grad: bfloat16 [32, 3072, 640], P(('groups', 'expert')), may hold values from -6 to 6
- gate_weight: bfloat16 [32, 3584, 640], P('expert'), may hold values from -0.09375 to 0.09375
- up_weight: bfloat16 [32, 3584, 640], P('expert'), may hold values from -0.09375 to 0.09375
- routes: int32 [4096, 8], P(('groups', 'expert')), may hold values from 0 to 15, all different within a row; in each aligned block of 128 rows (0 to 127, 128 to 255, ...) at most 96 rows name the same one
Outputs:
- token_grad: bfloat16 [4096, 3584], P(('groups', 'expert'))
Inputs may be any that keep to these rules, and one draw needn't show every extreme that they name: `routes`: each row names 8 different experts. Among the rows of one device no expert is named more than 96 times, and in every draw some expert is named exactly 96 times by the rows of some device.
All inputs are finite; a program needn't handle non-finite values.
Results may differ from a plain program's by a relative error of at most 0.012.
Values may be sent and summed in bfloat16 or wider, within the bound.
No kernel may reach another device: no remote copies, remote signals or barrier semaphores. Data moves between devices by JAX's collectives and lax.ppermute only.
A program may use at most 192 MiB of HBM per device.

v0:
```python
import jax
import jax.numpy as jnp
from jax import lax
from jax.sharding import PartitionSpec as P


def swiglu_grads(gate_pre, up_pre, hidden_grad):
    gate_values = gate_pre.astype(jnp.float32)
    up_values = up_pre.astype(jnp.float32)
    grad_values = hidden_grad.astype(jnp.float32)
    sigmoid_gate = jax.nn.sigmoid(gate_values)
    grad_gate = grad_values * up_values * sigmoid_gate * (1.0 + gate_values * (1.0 - sigmoid_gate))
    grad_up = grad_values * gate_values * sigmoid_gate
    return (grad_gate.astype(jnp.bfloat16), grad_up.astype(jnp.bfloat16))


def local(gate_pre, up_pre, hidden_grad, gate_weight, up_weight, routes):
    model_width = gate_weight.shape[1]
    devices = lax.axis_size("expert")
    tok_rows = routes.shape[0]
    chosen = routes.shape[1]
    capacity = gate_pre.shape[1] // devices
    experts = devices // 2
    grad_gate, grad_up = swiglu_grads(gate_pre[0], up_pre[0], hidden_grad[0])
    dims = (((1,), (1,)), ((), ()))
    partial_value = lax.dot_general(
        grad_gate, gate_weight[0], dims, preferred_element_type=jnp.float32
    )
    partial_value = partial_value + lax.dot_general(
        grad_up, up_weight[0], dims, preferred_element_type=jnp.float32
    )
    partial_value = partial_value.astype(jnp.bfloat16)
    flat_routes = routes.reshape(-1)
    picked = (flat_routes[:, None] == jnp.arange(experts, dtype=jnp.int32)[None, :]).astype(
        jnp.int32
    )
    before = jnp.cumsum(picked, axis=0) - picked
    slot_ids = jnp.sum(before * picked, axis=1)
    arrived = lax.all_to_all(
        partial_value.reshape(devices, capacity, model_width),
        "expert",
        split_axis=0,
        concat_axis=0,
        tiled=True,
    )
    paired = arrived.reshape(experts, 2, capacity, model_width).astype(jnp.float32)
    row_table = (
        (paired[:, 0] + paired[:, 1]).astype(jnp.bfloat16).reshape(experts * capacity, model_width)
    )
    token_rows = jnp.take(row_table, flat_routes * capacity + slot_ids, axis=0)
    combined = jnp.sum(
        token_rows.reshape(tok_rows, chosen, model_width).astype(jnp.float32), axis=1
    )
    return combined.astype(jnp.bfloat16)


def solution(mesh):
    placed = (
        P(("groups", "expert"), None, None),
        P(("groups", "expert"), None, None),
        P(("groups", "expert"), None, None),
        P("expert", None, None),
        P("expert", None, None),
        P(("groups", "expert"), None),
    )
    return jax.shard_map(
        local, mesh=mesh, in_specs=placed, out_specs=P(("groups", "expert"), None), check_vma=False
    )
```

profile of v0, /device:TPU:0, one launch (start us, length us, event | category | flops | bytes accessed | tf_op | source)
XLA Modules:
  0.0 627.8 jit_solution(13943216948224893830)
XLA Ops:
  0.0 28.5 %fusion.13 = f32[3072,3584]{1,0:T(8,128)} fusion(bf16[1,3584,640]{2,1,0:T(8,128)(2,1)} %param.9, bf16[1,3072,640]{2,1,0:T(8,128)(2,1)} %param.8, bf16[1,3072,640]{2,1,0:T(8,128)(2,1)} %param.6, bf16[1,3072,640]{2,1,0:T(8,128)(2,1)} %param.7), kind=kOutput, calls=%fused_computation.22 | convolution fusion | flops 14118420480 | bytes 60424192 | tf_op jit(solution)/shard_map/dot_general | solution.py:26
  28.5 31.3 %add_convert_fusion = bf16[3072,3584]{1,0:T(8,128)(2,1)} fusion(f32[3072,3584]{1,0:T(8,128)} %fusion.13, bf16[1,3584,640]{2,1,0:T(8,128)(2,1)} %param.10, bf16[1,3072,640]{2,1,0:T(8,128)(2,1)} %param.6, bf16[1,3072,640]{2,1,0:T(8,128)(2,1)} %param.8), kind=kOutput, calls=%fused_computation.1 | convolution fusion | flops 14130610176 | bytes 78512128 | tf_op jit(solution)/shard_map/dot_general | solution.py:29
  59.8 0.0 copy-start
  59.8 7.6 %all-to-all-start = ((bf16[32,96,3584]{2,1,0:T(8,128)(2,1)}), bf16[32,96,3584]{2,1,0:T(8,128)(2,1)}, u32[]{:S(2)}, u32[]{:S(2)}) async-start(bf16[32,96,3584]{2,1,0:T(8,128)(2,1)} %bitcast.51), calls=%async_computation | async-start | bytes 44040192 | tf_op jit(solution)/shard_map/all_to_all | solution.py:39
  67.4 0.0 copy-done
  67.4 0.1 copy.19
  67.5 0.1 eq.26
  67.6 0.1 reshape.75
  67.7 0.1 copy.27
  67.8 0.1 mul.55
  67.9 4.5 reduce-window.6
  72.5 0.1 slice.18
  72.5 0.1 copy.21
  72.7 0.1 copy.22
  72.8 0.1 broadcast_add_fusion
  72.9 0.1 reduce_sum.26
  73.1 0.1 copy.24
  73.2 484.6 %all-to-all-done = bf16[32,96,3584]{2,1,0:T(8,128)(2,1)} async-done(((bf16[32,96,3584]{2,1,0:T(8,128)(2,1)}), bf16[32,96,3584]{2,1,0:T(8,128)(2,1)}, u32[]{:S(2)}, u32[]{:S(2)}) %all-to-all-start) | async-done | bytes 22020128 | tf_op jit(solution)/shard_map/all_to_all | solution.py:39
  557.9 24.2 %convert.2 = f32[16,2,96,3584]{3,2,1,0:T(8,128)} convert(bf16[16,2,96,3584]{3,2,1,0:T(8,128)(2,1)} %bitcast.8) | non-fusion elementwise | flops 11010048 | bytes 66060288 | tf_op jit(solution)/shard_map/convert_element_type | solution.py:46
  582.1 18.7 %fusion.1 = bf16[16,1,96,3584]{3,2,0,1:T(8,128)(2,1)} fusion(f32[16,2,96,3584]{3,2,1,0:T(8,128)} %convert.2), kind=kLoop, calls=%fused_computation.4 | loop fusion | flops 11010048 | bytes 55050240 | tf_op jit(solution)/shard_map/convert_element_type | solution.py:48
  600.8 19.3 %gather_fusion = bf16[1024,3584]{1,0:T(8,128)(2,1)} fusion(bf16[1536,3584]{1,0:T(8,128)(2,1)} %bitcast.50, s32[1024]{0:T(1024)S(1)} %broadcast_clamp_fusion), kind=kCustom, calls=%fused_computation | custom fusion | bytes 14684160 | tf_op jit(solution)/shard_map/jit(_take)/gather | solution.py:50
  620.1 7.7 %fusion.11 = bf16[128,3584]{1,0:T(8,128)(2,1)} fusion(bf16[1024,3584]{1,0:T(8,128)(2,1)} %gather_fusion, pred[128,8]{1,0:T(8,128)(4,1)S(1)} %copy.24), kind=kLoop, calls=%fused_computation.20 | loop fusion | flops 6881280 | bytes 8258560 | tf_op jit(solution)/shard_map/reduce_sum | solution.py:51
  (9 shorter events, 0.1 us)
Async XLA Ops:
  59.8 7.6 %copy-start = (s32[128,8]{0,1:T(8,128)S(1)}, s32[128,8]{0,1:T(8,128)}, u32[]{:S(2)}) copy-start(s32[128,8]{0,1:T(8,128)} %param.11) | copy-start | bytes 12292
  59.8 498.1 %all-to-all-start = ((bf16[32,96,3584]{2,1,0:T(8,128)(2,1)}), bf16[32,96,3584]{2,1,0:T(8,128)(2,1)}, u32[]{:S(2)}, u32[]{:S(2)}) async-start(bf16[32,96,3584]{2,1,0:T(8,128)(2,1)} %bitcast.51), calls=%async_computation | async-start | bytes 44040192 | tf_op jit(solution)/shard_map/all_to_all | solution.py:39
where the time goes:
time: 628 us
  waiting for transfers between devices  485 us (77%)
  matrix products  59.8 us (10%)
  other arithmetic  55.3 us (9%)
  local copies, waits for them, and re-layouts  20.4 us (3%)
  starting transfers between devices  7.59 us (1%)
    all_to_all x1, waiting for transfers between devices, local(): lax.all_to_all(partial_value.reshape(devices, capacity, model_width), 'ex...  485 us
    dot_general x1, matrix products, local(): lax.dot_general(grad_up, up_weight[0], dims, preferred_element_type=jnp.f...  31.3 us
    dot_general x1, matrix products, local(): lax.dot_general(grad_gate, gate_weight[0], dims, preferred_element_type=j...  28.5 us
    convert_element_type x1, other arithmetic, local(): arrived.reshape(experts, 2, capacity, model_width).astype(jnp.float32)  24.2 us
    gather x1, local copies, waits for them, and re-layouts, local(): token_rows = jnp.take(row_table, flat_routes * capacity + slot_ids, axis=0)  19.3 us
    convert_element_type x1, other arithmetic, local(): (paired[:, 0] + paired[:, 1]).astype(jnp.bfloat16)  18.7 us
  transfers between devices with their start and end apart: 1, of which 1 were waited for; matrix products, arithmetic and copies ran while one was open for 1% of the time, Pallas kernels for 0%

commit v1 on v0

v1 whole, which is shorter than its diff:
```python
import functools

import jax
import jax.numpy as jnp
from jax import lax
from jax.experimental import pallas as pl
from jax.experimental.pallas import tpu as pltpu
from jax.sharding import PartitionSpec as P

X, Y, Z0, Z1 = 8, 4, 2, 1
MASK = {X: 2, Y: 4, Z0: 8, Z1: 16}
WAVES = (
    (((X, Y, Z0, Z1), (Y, X, Z0, Z1)), 640),
    (((Z0, X, Y, Z1), (Z0, Y, X, Z1)), 512),
    (((X, Y, Z0, Z1), (Y, X, Z0, Z1)), 640),
)
UNIT = 128
VMEM = 60 * 1024 * 1024


def mask_of(position):
    return sum(MASK[bit] for bit in (X, Y, Z0, Z1) if position & bit)


def send(value, mask):
    count = lax.axis_size("expert")
    return lax.ppermute(value, "expert", [(i, i ^ mask) for i in range(count)])


def params(**more):
    return pltpu.CompilerParams(vmem_limit_bytes=VMEM, **more)


def slots_kernel(routes_ref, slot_ref):
    experts, tokens = slot_ref.shape
    chosen = routes_ref.shape[1]
    ids = lax.broadcasted_iota(jnp.int32, (tokens, experts), 1)
    picked = jnp.zeros((tokens, experts), jnp.float32)
    for k in range(chosen):
        picked = picked + (routes_ref[:, k : k + 1] == ids).astype(jnp.float32)
    picked = picked.astype(jnp.bfloat16)
    row = lax.broadcasted_iota(jnp.int32, (tokens, tokens), 0)
    column = lax.broadcasted_iota(jnp.int32, (tokens, tokens), 1)
    dims = (((0,), (0,)), ((), ()))
    before = lax.dot_general(
        picked, (row < column).astype(jnp.bfloat16), dims, preferred_element_type=jnp.float32
    )
    here = lax.dot_general(
        picked, (row == column).astype(jnp.bfloat16), dims, preferred_element_type=jnp.float32
    )
    slot_ref[...] = jnp.where(here > 0.5, before, -1.0).astype(jnp.int32)


def swiglu_kernel(group, table_ref, *refs):
    out_ref = refs[-1]
    width = refs[0].shape[2]
    for i in range(group):
        gate = refs[i][0].astype(jnp.float32)
        up = refs[group + i][0].astype(jnp.float32)
        grad = refs[2 * group + i][0].astype(jnp.float32)
        sigmoid_gate = 0.5 * jnp.tanh(0.5 * gate) + 0.5
        common = grad * sigmoid_gate
        linear = common * gate
        out_ref[i, :, :width] = (up * (common + linear * (1.0 - sigmoid_gate))).astype(
            jnp.bfloat16
        )
        out_ref[i, :, width:] = linear.astype(jnp.bfloat16)


def swiglu(table, gate_pre, up_pre, hidden_grad, group=2):
    count = table.shape[0]
    _, capacity, width = gate_pre.shape
    spec = [
        pl.BlockSpec((1, capacity, width), lambda n, table, i=i: (table[n * group + i], 0, 0))
        for i in range(group)
    ]
    return pl.pallas_call(
        functools.partial(swiglu_kernel, group),
        grid_spec=pltpu.PrefetchScalarGridSpec(
            num_scalar_prefetch=1,
            grid=(count // group,),
            in_specs=spec * 3,
            out_specs=pl.BlockSpec((group, capacity, 2 * width), lambda n, table: (n, 0, 0)),
        ),
        out_shape=jax.ShapeDtypeStruct((count, capacity, 2 * width), jnp.bfloat16),
        compiler_params=params(),
        cost_estimate=pl.CostEstimate(
            flops=20 * count * capacity * width,
            bytes_accessed=10 * count * capacity * width,
            transcendentals=2 * count * capacity * width,
        ),
    )(table, *([gate_pre] * group), *([up_pre] * group), *([hidden_grad] * group))


def rows_kernel(sets, quads, places, steps, *refs):
    count = len(quads)
    own, other, weights = refs[:count], refs[count : 2 * count], refs[2 * count : 2 * count + 4]
    outs, rows = refs[2 * count + 4 : -1], refs[-1]
    pairs, capacity, depth = own[0].shape
    block = pairs * capacity
    n = pl.program_id(0)

    for which in range(2):
        if which and sets[0] == sets[1]:
            continue

        @pl.when(n == which * steps)
        def _():
            for i, q in enumerate(sets[which]):
                at = quads.index(q)
                rows[i * block : (i + 1) * block, :depth] = own[at][...].reshape(block, depth)
                rows[i * block : (i + 1) * block, depth:] = other[at][...].reshape(block, depth)

    dims = (((1,), (1,)), ((), ()))
    width = depth // 2
    total = None
    for i in range(4):
        part = lax.dot_general(
            rows[:, i * width : (i + 1) * width],
            weights[i][...],
            dims,
            preferred_element_type=jnp.float32,
        )
        total = part if total is None else total + part
    total = total.astype(jnp.bfloat16)
    for which in range(2):

        @pl.when((n >= steps) == bool(which))
        def _():
            for i, place in enumerate(places[which]):
                outs[which][place] = total[i * capacity : (i + 1) * capacity]


def expert_rows(own, other, weights, orders, sent, start, columns):
    _, capacity, depth = own.shape
    tile = next(t for t in (640, 512, 384, 256, 128) if columns % t == 0 and start % t == 0 and t <= 320)
    steps = columns // tile
    sets = [[q for q in range(8) if bool(2 * q & order[0]) == sent] for order in orders]
    places = [
        [
            sum(4 >> k for k in range(3) if position & order[k + 1])
            for q in chosen
            for position in (2 * q, 2 * q + 1)
        ]
        for order, chosen in zip(orders, sets)
    ]
    quads = sorted(set(sets[0]) | set(sets[1]))
    spec = [pl.BlockSpec((2, capacity, depth), lambda n, q=q: (q, 0, 0)) for q in quads]
    first = start // tile
    weight = pl.BlockSpec((tile, depth // 2), lambda n: (first + n, 0))
    return pl.pallas_call(
        functools.partial(rows_kernel, sets, quads, places, steps),
        grid=(2 * steps,),
        in_specs=spec * 2 + [weight] * 4,
        out_specs=[
            pl.BlockSpec((8, capacity, tile), lambda n: (0, 0, jnp.minimum(n, steps - 1))),
            pl.BlockSpec((8, capacity, tile), lambda n: (0, 0, jnp.maximum(n - steps, 0))),
        ],
        out_shape=[jax.ShapeDtypeStruct((8, capacity, columns), jnp.bfloat16)] * 2,
        scratch_shapes=[pltpu.VMEM((8 * capacity, 2 * depth), jnp.bfloat16)],
        compiler_params=params(),
        cost_estimate=pl.CostEstimate(
            flops=2 * 8 * capacity * 2 * depth * 2 * columns,
            bytes_accessed=2 * (8 * capacity * (2 * depth + columns) + 2 * depth * columns),
            transcendentals=0,
        ),
    )(*([own] * len(quads)), *([other] * len(quads)), *weights)


def spread_kernel(places, with_arrived, ids_ref, slot_ref, *refs):
    per = 3 if with_arrived else 2
    outs = refs[2 * per :]
    _, capacity, columns = refs[0].shape
    tokens = slot_ref.shape[2]
    ids = lax.broadcasted_iota(jnp.int32, (capacity, tokens), 0)
    dims = (((0,), (0,)), ((), ()))
    for which in range(2):
        for i, place in enumerate(places[which]):
            total = None
            for side in range(2):
                slot = slot_ref[place, pl.ds(ids_ref[2 * which + side], 1), :]
                pick = (ids == slot).astype(jnp.bfloat16)
                part = lax.dot_general(
                    pick, refs[per * which + side][i], dims, preferred_element_type=jnp.float32
                )
                total = part if total is None else total + part
            if with_arrived:
                total = total + refs[per * which + 2][i].astype(jnp.float32)
            total = total.astype(jnp.bfloat16)
            if with_arrived:
                outs[2 * which + (i >= 2)][i % 2] = total
            else:
                outs[which][i] = total


def token_rows(ids, slots, orders, rows, arrived):
    _, capacity, columns = rows[0].shape
    _, experts, tokens = slots.shape
    half = 0 if arrived else 1
    places = [
        [
            sum(order[k + 1] for k in range(3) if (i + 4 * half) & (4 >> k))
            for i in range(4)
        ]
        for order in orders
    ]
    steps = 1 if columns % 256 else 2
    tile = columns // steps
    block = pl.BlockSpec((4, capacity, tile), lambda n, ids: (half, 0, n))
    specs, arguments = [], []
    for which in range(2):
        specs += [block, block]
        arguments += rows[2 * which : 2 * which + 2]
        if arrived:
            specs.append(pl.BlockSpec((4, tokens, tile), lambda n, ids: (0, 0, n)))
            arguments.append(arrived[which])
    blocks, outs = (2, 4) if arrived else (4, 2)
    return pl.pallas_call(
        functools.partial(spread_kernel, places, bool(arrived)),
        grid_spec=pltpu.PrefetchScalarGridSpec(
            num_scalar_prefetch=1,
            grid=(steps,),
            in_specs=[pl.BlockSpec(slots.shape, lambda n, ids: (0, 0, 0))] + specs,
            out_specs=[pl.BlockSpec((blocks, tokens, tile), lambda n, ids: (0, 0, n))] * outs,
        ),
        out_shape=[jax.ShapeDtypeStruct((blocks, tokens, columns), jnp.bfloat16)] * outs,
        compiler_params=params(),
        cost_estimate=pl.CostEstimate(
            flops=32 * capacity * tokens * columns,
            bytes_accessed=64 * tokens * columns,
            transcendentals=0,
        ),
    )(ids, slots, *arguments)


def local(gate_pre, up_pre, hidden_grad, gate_weight, up_weight, routes):
    devices = lax.axis_size("expert")
    experts = devices // 2
    tokens = routes.shape[0]
    capacity = gate_pre.shape[1] // devices
    hidden = gate_pre.shape[2]
    me = lax.axis_index("expert").astype(jnp.int32)

    slots = pl.pallas_call(
        slots_kernel, out_shape=jax.ShapeDtypeStruct((experts, tokens), jnp.int32)
    )(routes)[None]
    for bit in (Z1, Z0, Y, X):
        slots = jnp.concatenate([slots, send(slots, MASK[bit])], axis=0)

    inputs = [v.reshape(devices, capacity, hidden) for v in (gate_pre, up_pre, hidden_grad)]
    masks = jnp.array([mask_of(p) for p in range(16)], jnp.int32)
    weights = [gate_weight[0], up_weight[0]]
    other_weights = [send(w, 1) for w in weights]
    other = send(swiglu((me ^ 1) ^ masks, *inputs), 1)
    own = swiglu(me ^ masks, *inputs)
    weights = weights + other_weights

    waves = []
    start = 0
    for orders, columns in WAVES:
        sent = expert_rows(own, other, weights, orders, True, start, columns)
        waves.append((start, [send(v, MASK[order[0]]) for v, order in zip(sent, orders)]))
        start += 2 * columns
    sums = []
    for (orders, columns), (start, arrived) in zip(WAVES, waves):
        kept = expert_rows(own, other, weights, orders, False, start, columns)
        rows = [kept[0], arrived[0], kept[1], arrived[1]]
        ids = jnp.stack([(me ^ m) // 2 for order in orders for m in (0, MASK[order[0]])])
        upper = token_rows(ids, slots, orders, rows, None)
        sums.append((ids, rows, [send(v, MASK[order[1]]) for v, order in zip(upper, orders)]))
    results = []
    for (orders, columns), (ids, rows, arrived) in zip(WAVES, sums):
        lower = token_rows(ids, slots, orders, rows, arrived)
        for which, order in enumerate(orders):
            third = send(lower[2 * which + 1], MASK[order[2]])
            rest = lower[2 * which].astype(jnp.float32) + third.astype(jnp.float32)
            fourth = send(rest[1].astype(jnp.bfloat16), MASK[order[3]])
            results.append((rest[0] + fourth.astype(jnp.float32)).astype(jnp.bfloat16))
    return jnp.concatenate(results, axis=1)


def solution(mesh):
    placed = (
        P(("groups", "expert"), None, None),
        P(("groups", "expert"), None, None),
        P(("groups", "expert"), None, None),
        P("expert", None, None),
        P("expert", None, None),
        P(("groups", "expert"), None),
    )
    return jax.shard_map(
        local, mesh=mesh, in_specs=placed, out_specs=P(("groups", "expert"), None), check_vma=False
    )
```

time: 628 us -> 224 us (0.36)
  waiting for transfers between devices: 485 us -> 42.9 us
  Pallas kernels: 0 us -> 133 us
  matrix products: 59.8 us -> 0 us
  other arithmetic: 55.3 us -> 5.6 us
  starting transfers between devices: 7.59 us -> 35.4 us
  local copies, waits for them, and re-layouts: 20.4 us -> 6.67 us
    all_to_all x1 -> x0, waiting for transfers between devices: 485 us -> none  [local(): lax.all_to_all(partial_value.reshape(devices, capacity, model_width), 'ex...]
    pallas_call x0 -> x15, Pallas kernels: none -> 133 us  [the longest x6 89 us: expert_rows(): pl.pallas_call(functools.partial(rows_kernel, sets, quads, places, steps)...]
    dot_general x2 -> x0, matrix products: 59.8 us -> none  [the longest x1 31.3 us: local(): lax.dot_general(grad_up, up_weight[0], dims, preferred_element_type=jnp.f...]
    ppermute x0 -> x31, waiting for transfers between devices: none -> 42.9 us  [send(): return lax.ppermute(value, 'expert', [(i, i ^ mask) for i in range(count)])]
    convert_element_type x3 -> x0, other arithmetic: 42.9 us -> none  [the longest x1 24.2 us: local(): arrived.reshape(experts, 2, capacity, model_width).astype(jnp.float32)]
    ppermute x0 -> x31, starting transfers between devices: none -> 35.4 us  [send(): return lax.ppermute(value, 'expert', [(i, i ^ mask) for i in range(count)])]
    gather x1 -> x0, local copies, waits for them, and re-layouts: 19.3 us -> none  [local(): token_rows = jnp.take(row_table, flat_routes * capacity + slot_ids, axis=0)]
    reduce_sum x2 -> x0, other arithmetic: 7.71 us -> none  [the longest x1 7.68 us: local(): jnp.sum(token_rows.reshape(tok_rows, chosen, model_width).astype(jnp.floa...]
  transfers between devices with their start and end apart: 1 -> 31, of which waited for: 1 -> 10; matrix products, arithmetic and copies ran while one was open for 1% -> 3% of each run, Pallas kernels for 0% -> 59%
where the time goes in v1:
time: 224 us; the launch traced here: 223 us
  Pallas kernels  133 us (59%)
  waiting for transfers between devices  42.9 us (19%)
  starting transfers between devices  35.4 us (16%)
  local copies, waits for them, and re-layouts  6.67 us (3%)
  other arithmetic  5.6 us (2%)
    pallas_call x6, Pallas kernels, expert_rows(): pl.pallas_call(functools.partial(rows_kernel, sets, quads, places, steps)...  89 us
    ppermute x31, waiting for transfers between devices, send(): return lax.ppermute(value, 'expert', [(i, i ^ mask) for i in range(count)])  42.9 us
    ppermute x31, starting transfers between devices, send(): return lax.ppermute(value, 'expert', [(i, i ^ mask) for i in range(count)])  35.4 us
    pallas_call x6, Pallas kernels, token_rows(): pl.pallas_call(functools.partial(spread_kernel, places, bool(arrived)), g...  24 us
    pallas_call x2, Pallas kernels, swiglu(): pl.pallas_call(functools.partial(swiglu_kernel, group), grid_spec=pltpu.P...  17.7 us
    unnamed x41, local copies, waits for them, and re-layouts  5.89 us
  transfers between devices with their start and end apart: 31, of which 10 were waited for; matrix products, arithmetic and copies ran while one was open for 3% of the time, Pallas kernels for 59%

profile of v1, /device:TPU:0, one launch (start us, length us, event | category | flops | bytes accessed | tf_op | source)
XLA Modules:
  0.0 223.4 jit_solution(16209251600575421030)
XLA Ops:
  1.8 8.8 %shard_map.75 = bf16[16,96,1280]{2,1,0:T(8,128)(2,1)} custom-call(s32[16]{0:T(128)} %get-tuple-element.65.table_ref, bf16[32,96,640]{2,1,0:T(8,128)(2,1)} %bitcast.85, bf16[32,96,640]{2,1,0:T(8,128)(2,1)} %bitcast.86, bf16[32,96,640]{2,1,0:T(8,128)(2,1)} %bitcast.89, bf16[32,96,640]{2,1,0:T(8,128)(2,1)} %bitcast.90, bf16[32,96,640]{2,1,0:T(8,128)(2,1)} %bitcast.93, ...), custom_call_target="tpu_custom_call" | custom-call | flops 19660800 | bytes 9830400 | tf_op jit(solution)/shard_map/pallas_call | solution.py:77
  11.8 1.8 shard_map.73
  13.6 3.6 %collective-permute-start = (s32[1,16,128]{2,1,0:T(8,128)}, s32[1,16,128]{2,1,0:T(8,128)S(1)}, u32[]{:S(2)}, u32[]{:S(2)}) collective-permute-start(s32[1,16,128]{2,1,0:T(8,128)} %bitcast.97), channel_id=1, source_target_pairs={{0,16},{1,17},{2,18},{3,19},{4,20},{5,21},{6,22},{7,23},{8,24},{9,... | collective-permute-start | bytes 24584 | tf_op jit(solution)/shard_map/ppermute | solution.py:27
  19.1 8.9 %shard_map.74.refs_0_.refs_1_.refs_2_.refs_3_.refs_4_.refs_5_ = bf16[16,96,1280]{2,1,0:T(8,128)(2,1)} custom-call(s32[16]{0:T(128)} %get-tuple-element.66.table_ref, bf16[32,96,640]{2,1,0:T(8,128)(2,1)} %bitcast.87, bf16[32,96,640]{2,1,0:T(8,128)(2,1)} %bitcast.88, bf16[32,96,640]{2,1,0:T(8,128)(2,1)} %bitcast.91, bf16[32,96,640]{2,1,0:T(8,128)(2,1)} %bitcast.92, ...), custom_call_target="tpu_custom_call" | custom-call | flops 19660800 | bytes 9830400 | tf_op jit(solution)/shard_map/pallas_call | solution.py:77
  28.0 1.6 collective-permute-start.1
  29.7 2.2 collective-permute-done.1
  33.3 2.4 %collective-permute-done.2 = s32[4,16,128]{2,1,0:T(8,128)S(1)} collective-permute-done((s32[4,16,128]{2,1,0:T(8,128)S(1)}, s32[4,16,128]{2,1,0:T(8,128)S(1)}, u32[]{:S(2)}, u32[]{:S(2)}) %collective-permute-start.2) | collective-permute-done | bytes 32800 | tf_op jit(solution)/shard_map/ppermute | solution.py:27
  37.2 9.7 %shard_map.81 = (bf16[8,96,512]{2,1,0:T(8,128)(2,1)}, bf16[8,96,512]{2,1,0:T(8,128)(2,1)}) custom-call(bf16[16,96,1280]{2,1,0:T(8,128)(2,1)} %shard_map.74.refs_0_.refs_1_.refs_2_.refs_3_.refs_4_.refs_5_, bf16[16,96,1280]{2,1,0:T(8,128)(2,1)} %shard_map.74.refs_0_.refs_1_.refs_2_.refs_3_.refs_4_.refs_5_, ...), custom_call_target="tpu_custom_call" | custom-call | flops 4026531840 | bytes 7340032 | tf_op jit(solution)/shard_map/pallas_call | solution.py:151
  47.0 1.6 collective-permute-start.15
  49.1 17.4 %shard_map.77 = (bf16[8,96,640]{2,1,0:T(8,128)(2,1)}, bf16[8,96,640]{2,1,0:T(8,128)(2,1)}) custom-call(bf16[16,96,1280]{2,1,0:T(8,128)(2,1)} %shard_map.74.refs_0_.refs_1_.refs_2_.refs_3_.refs_4_.refs_5_, bf16[16,96,1280]{2,1,0:T(8,128)(2,1)} %shard_map.74.refs_0_.refs_1_.refs_2_.refs_3_.refs_4_.refs_5_, ...), custom_call_target="tpu_custom_call" | custom-call | flops 5033164800 | bytes 8192000 | tf_op jit(solution)/shard_map/pallas_call | solution.py:151
  67.0 1.6 collective-permute-start.8
  68.6 9.7 %shard_map.80 = (bf16[8,96,512]{2,1,0:T(8,128)(2,1)}, bf16[8,96,512]{2,1,0:T(8,128)(2,1)}) custom-call(bf16[16,96,1280]{2,1,0:T(8,128)(2,1)} %shard_map.74.refs_0_.refs_1_.refs_2_.refs_3_.refs_4_.refs_5_, bf16[16,96,1280]{2,1,0:T(8,128)(2,1)} %shard_map.74.refs_0_.refs_1_.refs_2_.refs_3_.refs_4_.refs_5_, ...), custom_call_target="tpu_custom_call" | custom-call | flops 4026531840 | bytes 7340032 | tf_op jit(solution)/shard_map/pallas_call | solution.py:151
  78.4 2.8 %collective-permute-done.16.refs_3_.refs_4_ = bf16[8,96,512]{2,1,0:T(8,128)(2,1)S(1)} collective-permute-done((bf16[8,96,512]{2,1,0:T(8,128)(2,1)}, bf16[8,96,512]{2,1,0:T(8,128)(2,1)S(1)}, u32[]{:S(2)}, u32[]{:S(2)}) %collective-permute-start.16) | collective-permute-done | bytes 786464 | tf_op jit(solution)/shard_map/ppermute | solution.py:27
  82.1 3.8 %shard_map.82 = (bf16[4,128,512]{2,1,0:T(8,128)(2,1)}, bf16[4,128,512]{2,1,0:T(8,128)(2,1)}) custom-call(s32[4]{0:T(128)} %pad_add_fusion.4.ids_ref, s32[16,16,128]{2,1,0:T(8,128)} %copy-done, bf16[8,96,512]{2,1,0:T(8,128)(2,1)} %get-tuple-element.45.refs_0_, bf16[8,96,512]{2,1,0:T(8,128)(2,1)} %copy-done.5, ...), custom_call_target="tpu_custom_call" | custom-call | flops 201326592 | bytes 4194304 | tf_op jit(solution)/shard_map/pallas_call | solution.py:218
  87.9 17.3 %shard_map.85 = (bf16[8,96,640]{2,1,0:T(8,128)(2,1)}, bf16[8,96,640]{2,1,0:T(8,128)(2,1)}) custom-call(bf16[16,96,1280]{2,1,0:T(8,128)(2,1)} %shard_map.74.refs_0_.refs_1_.refs_2_.refs_3_.refs_4_.refs_5_, bf16[16,96,1280]{2,1,0:T(8,128)(2,1)} %shard_map.74.refs_0_.refs_1_.refs_2_.refs_3_.refs_4_.refs_5_, ...), custom_call_target="tpu_custom_call" | custom-call | flops 5033164800 | bytes 8192000 | tf_op jit(solution)/shard_map/pallas_call | solution.py:151
  105.2 1.5 collective-permute-start.23
  107.3 17.3 %shard_map.76 = (bf16[8,96,640]{2,1,0:T(8,128)(2,1)}, bf16[8,96,640]{2,1,0:T(8,128)(2,1)}) custom-call(bf16[16,96,1280]{2,1,0:T(8,128)(2,1)} %shard_map.74.refs_0_.refs_1_.refs_2_.refs_3_.refs_4_.refs_5_, bf16[16,96,1280]{2,1,0:T(8,128)(2,1)} %shard_map.74.refs_0_.refs_1_.refs_2_.refs_3_.refs_4_.refs_5_, ...), custom_call_target="tpu_custom_call" | custom-call | flops 5033164800 | bytes 8192000 | tf_op jit(solution)/shard_map/pallas_call | solution.py:151
  125.6 3.9 %shard_map.78 = (bf16[4,128,640]{2,1,0:T(8,128)(2,1)}, bf16[4,128,640]{2,1,0:T(8,128)(2,1)}) custom-call(s32[4]{0:T(128)} %pad_add_fusion.3.ids_ref, s32[16,16,128]{2,1,0:T(8,128)} %copy-done, bf16[8,96,640]{2,1,0:T(8,128)(2,1)} %get-tuple-element.35.refs_0_, bf16[8,96,640]{2,1,0:T(8,128)(2,1)} %copy-done.1, ...), custom_call_target="tpu_custom_call" | custom-call | flops 251658240 | bytes 5242880 | tf_op jit(solution)/shard_map/pallas_call | solution.py:218
  131.6 4.0 %shard_map.83 = (bf16[2,128,512]{2,1,0:T(8,128)(2,1)}, bf16[2,128,512]{2,1,0:T(8,128)(2,1)}, bf16[2,128,512]{2,1,0:T(8,128)(2,1)}, bf16[2,128,512]{2,1,0:T(8,128)(2,1)}) custom-call(s32[4]{0:T(128)} %pad_add_fusion.4.ids_ref, s32[16,16,128]{2,1,0:T(8,128)} %copy-done, bf16[8,96,512]{2,1,0:T(8,128)(2,1)} %get-tuple-element.45.refs_0_, ...), custom_call_target="tpu_custom_call" | custom-call | flops 201326592 | bytes 4194304 | tf_op jit(solution)/shard_map/pallas_call | solution.py:218
  136.1 17.5 %shard_map.84 = (bf16[8,96,640]{2,1,0:T(8,128)(2,1)}, bf16[8,96,640]{2,1,0:T(8,128)(2,1)}) custom-call(bf16[16,96,1280]{2,1,0:T(8,128)(2,1)} %shard_map.74.refs_0_.refs_1_.refs_2_.refs_3_.refs_4_.refs_5_, bf16[16,96,1280]{2,1,0:T(8,128)(2,1)} %shard_map.74.refs_0_.refs_1_.refs_2_.refs_3_.refs_4_.refs_5_, ...), custom_call_target="tpu_custom_call" | custom-call | flops 5033164800 | bytes 8192000 | tf_op jit(solution)/shard_map/pallas_call | solution.py:151
  154.9 3.9 %shard_map.86 = (bf16[4,128,640]{2,1,0:T(8,128)(2,1)}, bf16[4,128,640]{2,1,0:T(8,128)(2,1)}) custom-call(s32[4]{0:T(128)} %pad_add_fusion.3.ids_ref, s32[16,16,128]{2,1,0:T(8,128)} %copy-done, bf16[8,96,640]{2,1,0:T(8,128)(2,1)} %get-tuple-element.55.refs_0_, bf16[8,96,640]{2,1,0:T(8,128)(2,1)} %copy-done.2, ...), custom_call_target="tpu_custom_call" | custom-call | flops 251658240 | bytes 5242880 | tf_op jit(solution)/shard_map/pallas_call | solution.py:218
  164.0 4.2 %shard_map.79 = (bf16[2,128,640]{2,1,0:T(8,128)(2,1)}, bf16[2,128,640]{2,1,0:T(8,128)(2,1)}, bf16[2,128,640]{2,1,0:T(8,128)(2,1)}, bf16[2,128,640]{2,1,0:T(8,128)(2,1)}) custom-call(s32[4]{0:T(128)} %pad_add_fusion.3.ids_ref, s32[16,16,128]{2,1,0:T(8,128)} %copy-done, bf16[8,96,640]{2,1,0:T(8,128)(2,1)} %get-tuple-element.35.refs_0_, ...), custom_call_target="tpu_custom_call" | custom-call | flops 251658240 | bytes 5242880 | tf_op jit(solution)/shard_map/pallas_call | solution.py:218
  168.2 1.6 collective-permute-start.11
  169.7 7.6 %collective-permute-done.21 = bf16[2,128,512]{2,1,0:T(8,128)(2,1)S(1)} collective-permute-done((bf16[2,128,512]{2,1,0:T(8,128)(2,1)}, bf16[2,128,512]{2,1,0:T(8,128)(2,1)S(1)}, u32[]{:S(2)}, u32[]{:S(2)}) %collective-permute-start.21) | collective-permute-done | bytes 262176 | tf_op jit(solution)/shard_map/ppermute | solution.py:27
  177.8 1.6 collective-permute-start.13
  180.3 4.2 %shard_map.87 = (bf16[2,128,640]{2,1,0:T(8,128)(2,1)}, bf16[2,128,640]{2,1,0:T(8,128)(2,1)}, bf16[2,128,640]{2,1,0:T(8,128)(2,1)}, bf16[2,128,640]{2,1,0:T(8,128)(2,1)}) custom-call(s32[4]{0:T(128)} %pad_add_fusion.3.ids_ref, s32[16,16,128]{2,1,0:T(8,128)} %copy-done, bf16[8,96,640]{2,1,0:T(8,128)(2,1)} %get-tuple-element.55.refs_0_, ...), custom_call_target="tpu_custom_call" | custom-call | flops 251658240 | bytes 5242880 | tf_op jit(solution)/shard_map/pallas_call | solution.py:218
  186.6 5.2 %collective-permute-done.13 = bf16[2,128,640]{2,1,0:T(8,128)(2,1)S(1)} collective-permute-done((bf16[2,128,640]{2,1,0:T(8,128)(2,1)}, bf16[2,128,640]{2,1,0:T(8,128)(2,1)S(1)}, u32[]{:S(2)}, u32[]{:S(2)}) %collective-permute-start.13) | collective-permute-done | bytes 327712 | tf_op jit(solution)/shard_map/ppermute | solution.py:27
  193.4 7.7 %collective-permute-done.27 = bf16[2,128,640]{2,1,0:T(8,128)(2,1)S(1)} collective-permute-done((bf16[2,128,640]{2,1,0:T(8,128)(2,1)}, bf16[2,128,640]{2,1,0:T(8,128)(2,1)S(1)}, u32[]{:S(2)}, u32[]{:S(2)}) %collective-permute-start.27) | collective-permute-done | bytes 327712 | tf_op jit(solution)/shard_map/ppermute | solution.py:27
  203.4 2.5 %collective-permute-done.29 = bf16[2,128,640]{2,1,0:T(8,128)(2,1)S(1)} collective-permute-done((bf16[2,128,640]{2,1,0:T(8,128)(2,1)}, bf16[2,128,640]{2,1,0:T(8,128)(2,1)S(1)}, u32[]{:S(2)}, u32[]{:S(2)}) %collective-permute-start.29) | collective-permute-done | bytes 327712 | tf_op jit(solution)/shard_map/ppermute | solution.py:27
  206.1 2.9 %collective-permute-start.30 = (bf16[128,640]{1,0:T(8,128)(2,1)S(1)}, bf16[128,640]{1,0:T(8,128)(2,1)S(1)}, u32[]{:S(2)}, u32[]{:S(2)}) collective-permute-start(bf16[128,640]{1,0:T(8,128)(2,1)S(1)} %fusion.19), channel_id=1, source_target_pairs={{0,16},{1,17},{2,18},{3,19},{4,20},{5,21},{6,22},{7,23},{8,24},{9,... | collective-permute-start | bytes 491528 | tf_op jit(solution)/shard_map/ppermute | solution.py:27
  209.1 9.8 %collective-permute-done.14 = bf16[128,640]{1,0:T(8,128)(2,1)S(1)} collective-permute-done((bf16[128,640]{1,0:T(8,128)(2,1)S(1)}, bf16[128,640]{1,0:T(8,128)(2,1)S(1)}, u32[]{:S(2)}, u32[]{:S(2)}) %collective-permute-start.14) | collective-permute-done | bytes 163872 | tf_op jit(solution)/shard_map/ppermute | solution.py:27
  221.0 1.7 collective-permute-done.30
  (111 shorter events, 32.7 us)
Async XLA Ops:
  0.0 37.2 %collective-permute-start.5 = (bf16[3584,640]{1,0:T(8,128)(2,1)}, bf16[3584,640]{1,0:T(8,128)(2,1)}, u32[]{:S(2)}, u32[]{:S(2)}) collective-permute-start(bf16[3584,640]{1,0:T(8,128)(2,1)} %bitcast.71), channel_id=1, source_target_pairs={{0,1},{1,0},{2,3},{3,2},{4,5},{5,4},{6,7},{7,6},{8,9},{9,8},{10,11... | collective-permute-start | bytes 13762568 | tf_op jit(solution)/shard_map/ppermute | solution.py:27
  0.5 36.8 %collective-permute-start.6 = (bf16[3584,640]{1,0:T(8,128)(2,1)}, bf16[3584,640]{1,0:T(8,128)(2,1)}, u32[]{:S(2)}, u32[]{:S(2)}) collective-permute-start(bf16[3584,640]{1,0:T(8,128)(2,1)} %bitcast.78), channel_id=1, source_target_pairs={{0,1},{1,0},{2,3},{3,2},{4,5},{5,4},{6,7},{7,6},{8,9},{9,8},{10,11... | collective-permute-start | bytes 13762568 | tf_op jit(solution)/shard_map/ppermute | solution.py:27
  10.6 26.6 %collective-permute-start.4 = (bf16[16,96,1280]{2,1,0:T(8,128)(2,1)}, bf16[16,96,1280]{2,1,0:T(8,128)(2,1)}, u32[]{:S(2)}, u32[]{:S(2)}) collective-permute-start(bf16[16,96,1280]{2,1,0:T(8,128)(2,1)} %shard_map.75), channel_id=1, source_target_pairs={{0,1},{1,0},{2,3},{3,2},{4,5},{5,4},{6,7},{7,6},{8,9},{9,8},{10,11... | collective-permute-start | bytes 11796488 | tf_op jit(solution)/shard_map/ppermute | solution.py:27
  13.6 14.4 %collective-permute-start = (s32[1,16,128]{2,1,0:T(8,128)}, s32[1,16,128]{2,1,0:T(8,128)S(1)}, u32[]{:S(2)}, u32[]{:S(2)}) collective-permute-start(s32[1,16,128]{2,1,0:T(8,128)} %bitcast.97), channel_id=1, source_target_pairs={{0,16},{1,17},{2,18},{3,19},{4,20},{5,21},{6,22},{7,23},{8,24},{9,... | collective-permute-start | bytes 24584 | tf_op jit(solution)/shard_map/ppermute | solution.py:27
  28.0 3.8 %collective-permute-start.1 = (s32[2,16,128]{2,1,0:T(8,128)S(1)}, s32[2,16,128]{2,1,0:T(8,128)S(1)}, u32[]{:S(2)}, u32[]{:S(2)}) collective-permute-start(s32[2,16,128]{2,1,0:T(8,128)S(1)} %pad_add_fusion.2), channel_id=1, source_target_pairs={{0,8},{1,9},{2,10},{3,11},{4,12},{5,13},{6,14},{7,15},{8,0},{9,1},... | collective-permute-start | bytes 49160 | tf_op jit(solution)/shard_map/ppermute | solution.py:27
  31.8 3.9 %collective-permute-start.2 = (s32[4,16,128]{2,1,0:T(8,128)S(1)}, s32[4,16,128]{2,1,0:T(8,128)S(1)}, u32[]{:S(2)}, u32[]{:S(2)}) collective-permute-start(s32[4,16,128]{2,1,0:T(8,128)S(1)} %pad_add_fusion.1), channel_id=1, source_target_pairs={{0,4},{1,5},{2,6},{3,7},{4,0},{5,1},{6,2},{7,3},{8,12},{9,13},{10,... | collective-permute-start | bytes 98312 | tf_op jit(solution)/shard_map/ppermute | solution.py:27
  35.7 31.3 %collective-permute-start.3 = (s32[8,16,128]{2,1,0:T(8,128)S(1)}, s32[8,16,128]{2,1,0:T(8,128)S(1)}, u32[]{:S(2)}, u32[]{:S(2)}) collective-permute-start(s32[8,16,128]{2,1,0:T(8,128)S(1)} %pad_add_fusion), channel_id=1, source_target_pairs={{0,2},{1,3},{2,0},{3,1},{4,6},{5,7},{6,4},{7,5},{8,10},{9,11},{10,... | collective-permute-start | bytes 196616 | tf_op jit(solution)/shard_map/ppermute | solution.py:27
  47.0 31.4 %collective-permute-start.15 = (bf16[8,96,512]{2,1,0:T(8,128)(2,1)}, bf16[8,96,512]{2,1,0:T(8,128)(2,1)S(1)}, u32[]{:S(2)}, u32[]{:S(2)}) collective-permute-start(bf16[8,96,512]{2,1,0:T(8,128)(2,1)} %get-tuple-element.46), channel_id=1, source_target_pairs={{0,8},{1,9},{2,10},{3,11},{4,12},{5,13},{6,14},{7,15},{8,0},{9,1},... | collective-permute-start | bytes 2359304 | tf_op jit(solution)/shard_map/ppermute | solution.py:27
  48.6 32.6 %collective-permute-start.16 = (bf16[8,96,512]{2,1,0:T(8,128)(2,1)}, bf16[8,96,512]{2,1,0:T(8,128)(2,1)S(1)}, u32[]{:S(2)}, u32[]{:S(2)}) collective-permute-start(bf16[8,96,512]{2,1,0:T(8,128)(2,1)} %get-tuple-element.48), channel_id=1, source_target_pairs={{0,8},{1,9},{2,10},{3,11},{4,12},{5,13},{6,14},{7,15},{8,0},{9,1},... | collective-permute-start | bytes 2359304 | tf_op jit(solution)/shard_map/ppermute | solution.py:27
  66.4 40.4 %collective-permute-start.7 = (bf16[8,96,640]{2,1,0:T(8,128)(2,1)}, bf16[8,96,640]{2,1,0:T(8,128)(2,1)S(1)}, u32[]{:S(2)}, u32[]{:S(2)}) collective-permute-start(bf16[8,96,640]{2,1,0:T(8,128)(2,1)} %get-tuple-element.36), channel_id=1, source_target_pairs={{0,2},{1,3},{2,0},{3,1},{4,6},{5,7},{6,4},{7,5},{8,10},{9,11},{10,... | collective-permute-start | bytes 2949128 | tf_op jit(solution)/shard_map/ppermute | solution.py:27
  67.0 57.6 %collective-permute-start.8 = (bf16[8,96,640]{2,1,0:T(8,128)(2,1)}, bf16[8,96,640]{2,1,0:T(8,128)(2,1)S(1)}, u32[]{:S(2)}, u32[]{:S(2)}) collective-permute-start(bf16[8,96,640]{2,1,0:T(8,128)(2,1)} %get-tuple-element.38), channel_id=1, source_target_pairs={{0,4},{1,5},{2,6},{3,7},{4,0},{5,1},{6,2},{7,3},{8,12},{9,13},{10,... | collective-permute-start | bytes 2949128 | tf_op jit(solution)/shard_map/ppermute | solution.py:27
  85.9 45.2 %collective-permute-start.17 = (bf16[4,128,512]{2,1,0:T(8,128)(2,1)}, bf16[4,128,512]{2,1,0:T(8,128)(2,1)}, u32[]{:S(2)}, u32[]{:S(2)}) collective-permute-start(bf16[4,128,512]{2,1,0:T(8,128)(2,1)} %get-tuple-element.49), channel_id=1, source_target_pairs={{0,2},{1,3},{2,0},{3,1},{4,6},{5,7},{6,4},{7,5},{8,10},{9,11},{10,... | collective-permute-start | bytes 1572872 | tf_op jit(solution)/shard_map/ppermute | solution.py:27
  86.4 45.2 %collective-permute-start.18 = (bf16[4,128,512]{2,1,0:T(8,128)(2,1)}, bf16[4,128,512]{2,1,0:T(8,128)(2,1)}, u32[]{:S(2)}, u32[]{:S(2)}) collective-permute-start(bf16[4,128,512]{2,1,0:T(8,128)(2,1)} %get-tuple-element.50), channel_id=1, source_target_pairs={{0,4},{1,5},{2,6},{3,7},{4,0},{5,1},{6,2},{7,3},{8,12},{9,13},{10,... | collective-permute-start | bytes 1572872 | tf_op jit(solution)/shard_map/ppermute | solution.py:27
  105.2 48.4 %collective-permute-start.23 = (bf16[8,96,640]{2,1,0:T(8,128)(2,1)}, bf16[8,96,640]{2,1,0:T(8,128)(2,1)S(1)}, u32[]{:S(2)}, u32[]{:S(2)}) collective-permute-start(bf16[8,96,640]{2,1,0:T(8,128)(2,1)} %get-tuple-element.56), channel_id=1, source_target_pairs={{0,2},{1,3},{2,0},{3,1},{4,6},{5,7},{6,4},{7,5},{8,10},{9,11},{10,... | collective-permute-start | bytes 2949128 | tf_op jit(solution)/shard_map/ppermute | solution.py:27
  106.8 46.9 %collective-permute-start.24 = (bf16[8,96,640]{2,1,0:T(8,128)(2,1)}, bf16[8,96,640]{2,1,0:T(8,128)(2,1)S(1)}, u32[]{:S(2)}, u32[]{:S(2)}) collective-permute-start(bf16[8,96,640]{2,1,0:T(8,128)(2,1)} %get-tuple-element.58), channel_id=1, source_target_pairs={{0,4},{1,5},{2,6},{3,7},{4,0},{5,1},{6,2},{7,3},{8,12},{9,13},{10,... | collective-permute-start | bytes 2949128 | tf_op jit(solution)/shard_map/ppermute | solution.py:27
  129.5 33.6 %collective-permute-start.9 = (bf16[4,128,640]{2,1,0:T(8,128)(2,1)}, bf16[4,128,640]{2,1,0:T(8,128)(2,1)S(1)}, u32[]{:S(2)}, u32[]{:S(2)}) collective-permute-start(bf16[4,128,640]{2,1,0:T(8,128)(2,1)} %get-tuple-element.39), channel_id=1, source_target_pairs={{0,4},{1,5},{2,6},{3,7},{4,0},{5,1},{6,2},{7,3},{8,12},{9,13},{10,... | collective-permute-start | bytes 1966088 | tf_op jit(solution)/shard_map/ppermute | solution.py:27
  131.1 32.4 %collective-permute-start.10 = (bf16[4,128,640]{2,1,0:T(8,128)(2,1)}, bf16[4,128,640]{2,1,0:T(8,128)(2,1)}, u32[]{:S(2)}, u32[]{:S(2)}) collective-permute-start(bf16[4,128,640]{2,1,0:T(8,128)(2,1)} %get-tuple-element.40), channel_id=1, source_target_pairs={{0,2},{1,3},{2,0},{3,1},{4,6},{5,7},{6,4},{7,5},{8,10},{9,11},{10,... | collective-permute-start | bytes 1966088 | tf_op jit(solution)/shard_map/ppermute | solution.py:27
  135.6 26.3 %collective-permute-start.19 = (bf16[2,128,512]{2,1,0:T(8,128)(2,1)}, bf16[2,128,512]{2,1,0:T(8,128)(2,1)S(1)}, u32[]{:S(2)}, u32[]{:S(2)}) collective-permute-start(bf16[2,128,512]{2,1,0:T(8,128)(2,1)} %get-tuple-element.52), channel_id=1, source_target_pairs={{0,4},{1,5},{2,6},{3,7},{4,0},{5,1},{6,2},{7,3},{8,12},{9,13},{10,... | collective-permute-start | bytes 786440 | tf_op jit(solution)/shard_map/ppermute | solution.py:27
  158.8 19.0 %collective-permute-start.25 = (bf16[4,128,640]{2,1,0:T(8,128)(2,1)}, bf16[4,128,640]{2,1,0:T(8,128)(2,1)S(1)}, u32[]{:S(2)}, u32[]{:S(2)}) collective-permute-start(bf16[4,128,640]{2,1,0:T(8,128)(2,1)} %get-tuple-element.59), channel_id=1, source_target_pairs={{0,4},{1,5},{2,6},{3,7},{4,0},{5,1},{6,2},{7,3},{8,12},{9,13},{10,... | collective-permute-start | bytes 1966088 | tf_op jit(solution)/shard_map/ppermute | solution.py:27
  160.3 19.1 %collective-permute-start.26 = (bf16[4,128,640]{2,1,0:T(8,128)(2,1)}, bf16[4,128,640]{2,1,0:T(8,128)(2,1)S(1)}, u32[]{:S(2)}, u32[]{:S(2)}) collective-permute-start(bf16[4,128,640]{2,1,0:T(8,128)(2,1)} %get-tuple-element.60), channel_id=1, source_target_pairs={{0,2},{1,3},{2,0},{3,1},{4,6},{5,7},{6,4},{7,5},{8,10},{9,11},{10,... | collective-permute-start | bytes 1966088 | tf_op jit(solution)/shard_map/ppermute | solution.py:27
  161.8 15.5 %collective-permute-start.21 = (bf16[2,128,512]{2,1,0:T(8,128)(2,1)}, bf16[2,128,512]{2,1,0:T(8,128)(2,1)S(1)}, u32[]{:S(2)}, u32[]{:S(2)}) collective-permute-start(bf16[2,128,512]{2,1,0:T(8,128)(2,1)} %get-tuple-element.54), channel_id=1, source_target_pairs={{0,2},{1,3},{2,0},{3,1},{4,6},{5,7},{6,4},{7,5},{8,10},{9,11},{10,... | collective-permute-start | bytes 786440 | tf_op jit(solution)/shard_map/ppermute | solution.py:27
  163.1 55.8 %collective-permute-start.20 = (bf16[128,512]{1,0:T(8,128)(2,1)}, bf16[128,512]{1,0:T(8,128)(2,1)}, u32[]{:S(2)}, u32[]{:S(2)}) collective-permute-start(bf16[128,512]{1,0:T(8,128)(2,1)} %fusion.21), channel_id=1, source_target_pairs={{0,16},{1,17},{2,18},{3,19},{4,20},{5,21},{6,22},{7,23},{8,24},{9,... | collective-permute-start | bytes 393224 | tf_op jit(solution)/shard_map/ppermute | solution.py:27
  168.2 17.1 %collective-permute-start.11 = (bf16[2,128,640]{2,1,0:T(8,128)(2,1)}, bf16[2,128,640]{2,1,0:T(8,128)(2,1)S(1)}, u32[]{:S(2)}, u32[]{:S(2)}) collective-permute-start(bf16[2,128,640]{2,1,0:T(8,128)(2,1)} %get-tuple-element.42), channel_id=1, source_target_pairs={{0,8},{1,9},{2,10},{3,11},{4,12},{5,13},{6,14},{7,15},{8,0},{9,1},... | collective-permute-start | bytes 983048 | tf_op jit(solution)/shard_map/ppermute | solution.py:27
  177.4 42.4 %collective-permute-start.22 = (bf16[128,512]{1,0:T(8,128)(2,1)S(1)}, bf16[128,512]{1,0:T(8,128)(2,1)S(1)}, u32[]{:S(2)}, u32[]{:S(2)}) collective-permute-start(bf16[128,512]{1,0:T(8,128)(2,1)S(1)} %fusion.23), channel_id=1, source_target_pairs={{0,16},{1,17},{2,18},{3,19},{4,20},{5,21},{6,22},{7,23},{8,24},{9,... | collective-permute-start | bytes 393224 | tf_op jit(solution)/shard_map/ppermute | solution.py:27
  177.8 14.0 %collective-permute-start.13 = (bf16[2,128,640]{2,1,0:T(8,128)(2,1)}, bf16[2,128,640]{2,1,0:T(8,128)(2,1)S(1)}, u32[]{:S(2)}, u32[]{:S(2)}) collective-permute-start(bf16[2,128,640]{2,1,0:T(8,128)(2,1)} %get-tuple-element.44), channel_id=1, source_target_pairs={{0,8},{1,9},{2,10},{3,11},{4,12},{5,13},{6,14},{7,15},{8,0},{9,1},... | collective-permute-start | bytes 983048 | tf_op jit(solution)/shard_map/ppermute | solution.py:27
  184.4 21.5 %copy-start.12 = (bf16[2,128,640]{2,1,0:T(8,128)(2,1)S(1)}, bf16[2,128,640]{2,1,0:T(8,128)(2,1)}, u32[]{:S(2)}) copy-start(bf16[2,128,640]{2,1,0:T(8,128)(2,1)} %get-tuple-element.63) | copy-start | bytes 983044
  184.5 16.6 %collective-permute-start.27 = (bf16[2,128,640]{2,1,0:T(8,128)(2,1)}, bf16[2,128,640]{2,1,0:T(8,128)(2,1)S(1)}, u32[]{:S(2)}, u32[]{:S(2)}) collective-permute-start(bf16[2,128,640]{2,1,0:T(8,128)(2,1)} %get-tuple-element.62), channel_id=1, source_target_pairs={{0,8},{1,9},{2,10},{3,11},{4,12},{5,13},{6,14},{7,15},{8,0},{9,1},... | collective-permute-start | bytes 983048 | tf_op jit(solution)/shard_map/ppermute | solution.py:27
  185.3 20.6 %collective-permute-start.29 = (bf16[2,128,640]{2,1,0:T(8,128)(2,1)}, bf16[2,128,640]{2,1,0:T(8,128)(2,1)S(1)}, u32[]{:S(2)}, u32[]{:S(2)}) collective-permute-start(bf16[2,128,640]{2,1,0:T(8,128)(2,1)} %get-tuple-element.64), channel_id=1, source_target_pairs={{0,8},{1,9},{2,10},{3,11},{4,12},{5,13},{6,14},{7,15},{8,0},{9,1},... | collective-permute-start | bytes 983048 | tf_op jit(solution)/shard_map/ppermute | solution.py:27
  191.8 14.3 %collective-permute-start.12 = (bf16[128,640]{1,0:T(8,128)(2,1)S(1)}, bf16[128,640]{1,0:T(8,128)(2,1)S(1)}, u32[]{:S(2)}, u32[]{:S(2)}) collective-permute-start(bf16[128,640]{1,0:T(8,128)(2,1)S(1)} %fusion.13), channel_id=1, source_target_pairs={{0,16},{1,17},{2,18},{3,19},{4,20},{5,21},{6,22},{7,23},{8,24},{9,... | collective-permute-start | bytes 491528 | tf_op jit(solution)/shard_map/ppermute | solution.py:27
  201.1 17.8 %collective-permute-start.14 = (bf16[128,640]{1,0:T(8,128)(2,1)S(1)}, bf16[128,640]{1,0:T(8,128)(2,1)S(1)}, u32[]{:S(2)}, u32[]{:S(2)}) collective-permute-start(bf16[128,640]{1,0:T(8,128)(2,1)S(1)} %fusion.15), channel_id=1, source_target_pairs={{0,16},{1,17},{2,18},{3,19},{4,20},{5,21},{6,22},{7,23},{8,24},{9,... | collective-permute-start | bytes 491528 | tf_op jit(solution)/shard_map/ppermute | solution.py:27
  205.9 15.0 %collective-permute-start.28 = (bf16[128,640]{1,0:T(8,128)(2,1)S(1)}, bf16[128,640]{1,0:T(8,128)(2,1)S(1)}, u32[]{:S(2)}, u32[]{:S(2)}) collective-permute-start(bf16[128,640]{1,0:T(8,128)(2,1)S(1)} %fusion.17), channel_id=1, source_target_pairs={{0,16},{1,17},{2,18},{3,19},{4,20},{5,21},{6,22},{7,23},{8,24},{9,... | collective-permute-start | bytes 491528 | tf_op jit(solution)/shard_map/ppermute | solution.py:27
  206.1 16.6 %collective-permute-start.30 = (bf16[128,640]{1,0:T(8,128)(2,1)S(1)}, bf16[128,640]{1,0:T(8,128)(2,1)S(1)}, u32[]{:S(2)}, u32[]{:S(2)}) collective-permute-start(bf16[128,640]{1,0:T(8,128)(2,1)S(1)} %fusion.19), channel_id=1, source_target_pairs={{0,16},{1,17},{2,18},{3,19},{4,20},{5,21},{6,22},{7,23},{8,24},{9,... | collective-permute-start | bytes 491528 | tf_op jit(solution)/shard_map/ppermute | solution.py:27
  (17 other events, 120.8 us)

commit v2 on v0

v2 whole, which is shorter than its diff:
```python
import functools

import jax
import jax.numpy as jnp
from jax import lax
from jax.experimental import pallas as pl
from jax.experimental.pallas import tpu as pltpu
from jax.sharding import PartitionSpec as P

X, Y, Z0, Z1 = 8, 4, 2, 1
MASK = {X: 2, Y: 4, Z0: 8, Z1: 16}
TABLE = {X: 1, Y: 2, Z0: 4, Z1: 8}
AM = (X, Y, Z0, Z1), (Y, X, Z1, Z0)
AH = (X, Y, Z0, Z1), (Y, X, Z0, Z1)
BH = (Z0, X, Y, Z1), (Z0, Y, X, Z1)
BZ = (Z0, X, Z1, Y), (Z0, Y, Z1, X)
D = (X, Z0, Y, Z1), (Y, Z0, X, Z1)
E = (X, Z0, Z1, Y), (Y, Z0, Z1, X)
WAVES = ((AH, 512), (BZ, 256), (AH, 512), (BH, 256), (D, 256))
SCHEDULE = (
    *("A0", "S0", "A1", "S1", "S2", "B0", "S3", "B3", "B2", "C0", "B1", "C3", "D0", "B4", "C1", "C2"),
    *("E0", "C4", "D1", "F0", "D3", "D4", "D2", "E1", "E3", "E4", "E2", "F3", "F4", "F2", "F1"),
)
TILE = 256


def mask_of(position):
    return sum(MASK[bit] for bit in (X, Y, Z0, Z1) if position & bit)


def send(value, mask):
    count = lax.axis_size("expert")
    return lax.ppermute(value, "expert", [(i, i ^ mask) for i in range(count)])


def params(mebibytes):
    return pltpu.CompilerParams(vmem_limit_bytes=mebibytes * 1024 * 1024)


HBM, INSIDE = pl.BlockSpec(memory_space=pltpu.HBM), pl.BlockSpec(memory_space=pltpu.VMEM)


def inside(*shape):
    return pltpu.VMEM(shape, jnp.bfloat16)


def slots_kernel(routes_ref, slot_ref):
    experts, tokens = slot_ref.shape
    chosen = routes_ref.shape[1]
    ids = lax.broadcasted_iota(jnp.int32, (tokens, experts), 1)
    picked = jnp.zeros((tokens, experts), jnp.float32)
    for k in range(chosen):
        picked = picked + (routes_ref[:, k : k + 1] == ids).astype(jnp.float32)
    picked = picked.astype(jnp.bfloat16)
    row = lax.broadcasted_iota(jnp.int32, (tokens, tokens), 0)
    column = lax.broadcasted_iota(jnp.int32, (tokens, tokens), 1)
    dims = (((0,), (0,)), ((), ()))
    before = lax.dot_general(
        picked, (row < column).astype(jnp.bfloat16), dims, preferred_element_type=jnp.float32
    )
    here = lax.dot_general(
        picked, (row == column).astype(jnp.bfloat16), dims, preferred_element_type=jnp.float32
    )
    slot_ref[...] = jnp.where(here > 0.5, before, -1.0).astype(jnp.int32)


def swiglu_kernel(side, gate_pre, up_pre, hidden_grad, result, values, ready, *refs):
    capacity, width = values.shape[3:]
    out, out_ready = refs if side else (result, None)
    me = lax.axis_index("expert").astype(jnp.int32)
    core, plane, layer = (me & 1) ^ side, (me >> 1) & 3, me >> 3

    def in_copies(group):
        chip = plane ^ (group >> 1) ^ ((group & 1) << 1)
        for k, source in enumerate((gate_pre, up_pre, hidden_grad)):
            yield pltpu.make_async_copy(
                source.at[:, chip, core], values.at[k, group], ready.at[k, group]
            )

    def out_copy(group):
        rows = pl.ds(4 * group * capacity, 4 * capacity)
        return pltpu.make_async_copy(out.at[rows], result.at[rows], out_ready.at[group])

    for group in range(4):
        for copy in in_copies(group):
            copy.start()
    for group in range(4):
        for copy in in_copies(group):
            copy.wait()

        @pl.loop(0, 4)
        def _(i):
            at = layer ^ (i >> 1) ^ ((i & 1) << 1)
            gate, up, grad = (values[k, group, at].astype(jnp.float32) for k in range(3))
            sigmoid_gate = 0.5 * jnp.tanh(0.5 * gate) + 0.5
            common = grad * sigmoid_gate
            linear = common * gate
            full = up * (common + linear * (1.0 - sigmoid_gate))
            rows = pl.ds(pl.multiple_of((4 * group + i) * capacity, capacity), capacity)
            out[rows, :width] = full.astype(jnp.bfloat16)
            out[rows, width:] = linear.astype(jnp.bfloat16)

        if side:
            out_copy(group).start()
    if side:
        for group in range(4):
            out_copy(group).wait()


def swiglu(side, gate_pre, up_pre, hidden_grad):
    layers, chips, _, capacity, width = gate_pre.shape
    rows = layers * chips * capacity
    scratch_shapes = [
        pltpu.VMEM((3, chips, layers, capacity, width), jnp.bfloat16),
        pltpu.SemaphoreType.DMA((3, chips)),
    ]
    if side:
        scratch_shapes += [
            pltpu.VMEM((rows, 2 * width), jnp.bfloat16),
            pltpu.SemaphoreType.DMA((chips,)),
        ]
    return pl.pallas_call(
        functools.partial(swiglu_kernel, side),
        in_specs=[HBM] * 3,
        out_specs=HBM if side else INSIDE,
        out_shape=jax.ShapeDtypeStruct((rows, 2 * width), jnp.bfloat16) if side else inside(rows, 2 * width),
        scratch_shapes=scratch_shapes,
        compiler_params=params(62 if side else 57),
        cost_estimate=pl.CostEstimate(
            flops=10 * rows * 2 * width,
            bytes_accessed=5 * rows * 2 * width,
            transcendentals=rows * width,
        ),
    )(gate_pre, up_pre, hidden_grad)


def rows_kernel(orders, first, load, _, own, other, *refs):
    if load:
        weights, (kept, loaded, weight, *sent, weight_ready, other_ready) = refs[:4], refs[4:]
        other_copy = pltpu.make_async_copy(other, loaded, other_ready)
        other = loaded
    else:
        weight, kept, *sent = refs
    depth = own.shape[1]
    width = depth // 2
    tile = weight.shape[1]
    capacity, columns = kept.shape[2:]
    steps = columns // tile

    def weight_copy(t, i):
        return pltpu.make_async_copy(
            weights[i].at[pl.ds(pl.multiple_of(t * tile, tile), tile), :],
            weight.at[t, :, pl.ds(i * width, width)],
            weight_ready.at[t, i],
        )

    def part(t, side):
        at = slice(side * depth, (side + 1) * depth)
        return lax.dot_general(
            (own, other)[side][...],
            weight[first + t, :, at],
            (((1,), (1,)), ((), ())),
            preferred_element_type=jnp.float32,
        )

    def place(order, position):
        return sum(4 >> k for k in range(3) if position & order[k + 1])

    if load:
        other_copy.start()

        @pl.loop(0, weight.shape[0])
        def _(t):
            for i in range(4):
                weight_copy(t, i).start()

    @pl.loop(0, 2 * steps)
    def _(t):
        second = t // steps
        if load:
            for i in range(4):
                weight_copy(t, i).wait()
        total = part(t, 0)
        if load:
            pl.when(t == 0)(other_copy.wait)
        total = (total + part(t, 1)).astype(jnp.bfloat16)
        at = pl.ds(pl.multiple_of((t - second * steps) * tile, tile), tile)
        for which, order in enumerate(orders):

            @pl.when(second == which)
            def _():
                for position in range(16):
                    rows = total[position * capacity : (position + 1) * capacity]
                    if not position & order[0]:
                        kept[which, place(order, position), :, at] = rows
                    elif len(sent) == 1:
                        sent[0][which, place(order, position), :, at] = rows
                    else:
                        sent[which][0, place(order, position), :, at] = rows

    if load:

        @pl.loop(2 * steps, weight.shape[0])
        def _(t):
            for i in range(4):
                weight_copy(t, i).wait()


def expert_rows(token, own, other, weights, orders, start, columns, load):
    rows, depth = own.shape
    capacity = rows // 16
    count = 1 if orders[0][0] == orders[1][0] else 2
    out_shape = [inside(2, 8, capacity, columns)]
    scratch_shapes = []
    if load:
        tiles = weights[0].shape[0] // TILE
        out_shape += [inside(rows, depth), inside(tiles, TILE, 2 * depth)]
        scratch_shapes = [pltpu.SemaphoreType.DMA((tiles, 4)), pltpu.SemaphoreType.DMA]
    out_shape += [inside(3 - count, 8, capacity, columns)] * count
    out = pl.pallas_call(
        functools.partial(rows_kernel, orders, start // TILE, load),
        in_specs=[pl.BlockSpec(memory_space=pl.ANY), INSIDE] + ([HBM] * 5 if load else [INSIDE] * 2),
        out_specs=[INSIDE] * len(out_shape),
        out_shape=out_shape,
        scratch_shapes=scratch_shapes,
        compiler_params=params(33 if load else 10),
        cost_estimate=pl.CostEstimate(
            flops=4 * rows * 2 * depth * columns,
            bytes_accessed=2 * (rows * 2 * columns + 4 * depth * columns),
            transcendentals=0,
        ),
    )(token, own, other, *weights)
    if load:
        return out[0], out[3:], out[1], [out[2]]
    return out[0], out[1:], other, weights


def spread_kernel(orders, half, counts, slots, kept, *refs):
    firsts, refs = refs[: counts[0]], refs[counts[0] :]
    arrived, outs = refs[: counts[1]], refs[counts[1] :]
    capacity = kept.shape[2]
    tokens = slots.shape[2]
    me = lax.axis_index("expert").astype(jnp.int32)
    ids = lax.broadcasted_iota(jnp.int32, (capacity, tokens), 0)
    dims = (((0,), (0,)), ((), ()))

    for which, order in enumerate(orders):
        for i in range(4):
            block = i + 4 * half
            place = sum(TABLE[order[k + 1]] for k in range(3) if block & (4 >> k))
            total = None
            for mask, rows in ((0, kept.at[which]), (MASK[order[0]], stream(firsts, which))):
                slot = slots[place, pl.ds((me ^ mask) // 2, 1), :]
                part = lax.dot_general(
                    (ids == slot).astype(jnp.bfloat16),
                    rows[block],
                    dims,
                    preferred_element_type=jnp.float32,
                )
                total = part if total is None else total + part
            if half == 0:
                total = total + stream(arrived, which)[i].astype(jnp.float32)
            total = total.astype(jnp.bfloat16)
            if half:
                stream(outs, which)[i] = total
            elif i < 2:
                outs[0][which, i] = total
            else:
                stream(outs[1:], which)[i - 2] = total


def token_rows(slots, orders, kept, firsts, arrived):
    capacity, columns = kept.shape[2:]
    tokens = slots.shape[2]
    half = 0 if arrived else 1
    counts = len(firsts), len(arrived or ())
    bit = 2 if arrived else 1
    count = 1 if orders[0][bit] == orders[1][bit] else 2
    blocks = 2 if arrived else 4
    shapes = [inside(3 - count, blocks, tokens, columns)] * count
    if arrived:
        shapes = [inside(2, 2, tokens, columns)] + shapes
    arguments = [slots, kept, *firsts, *(arrived or ())]
    out = pl.pallas_call(
        functools.partial(spread_kernel, orders, half, counts),
        in_specs=[INSIDE] * len(arguments),
        out_specs=[INSIDE] * len(shapes),
        out_shape=shapes,
        compiler_params=params(8),
        cost_estimate=pl.CostEstimate(
            flops=32 * capacity * tokens * columns,
            bytes_accessed=64 * tokens * columns,
            transcendentals=0,
        ),
    )(*arguments)
    return (out[0], out[1:]) if arrived else out


def join_kernel(*refs):
    *parts, out = refs
    first = 0
    for part in parts:
        out[first : first + part.shape[0]] = part[...]
        first += part.shape[0]


def join(*parts):
    shape = (sum(part.shape[0] for part in parts), *parts[0].shape[1:])
    return pl.pallas_call(
        join_kernel,
        in_specs=[INSIDE] * len(parts),
        out_specs=INSIDE,
        out_shape=pltpu.VMEM(shape, parts[0].dtype),
        compiler_params=params(4),
    )(*parts)


def stream(values, which):
    return values[0].at[which] if len(values) == 1 else values[which].at[0]


def add_kernel(counts, _, kept, *refs):
    third, refs = refs[: counts[0]], refs[counts[0] :]
    fourth, outs = refs[: counts[1]], refs[counts[1] :]
    for which in range(2):
        block = 0 if fourth else 1
        total = kept[which, block].astype(jnp.float32)
        total = total + stream(third, which)[block].astype(jnp.float32)
        if fourth:
            total = total + stream(fourth, which)[...].astype(jnp.float32)
        stream(outs, which)[...] = total.astype(jnp.bfloat16)


def add(token, kept, third, fourth, merged):
    _, _, tokens, columns = kept.shape
    shapes = [inside(2, tokens, columns)] if merged else [inside(1, tokens, columns)] * 2
    arguments = [kept, *third, *fourth]
    return pl.pallas_call(
        functools.partial(add_kernel, (len(third), len(fourth))),
        in_specs=[pl.BlockSpec(memory_space=pl.ANY)] + [INSIDE] * len(arguments),
        out_specs=[INSIDE] * len(shapes),
        out_shape=shapes,
        compiler_params=params(4),
    )(token, *arguments)


def after(value, last):
    return value if last is None else lax.optimization_barrier((value, last))[0]


def send_all(values, orders, k):
    if len(values) == 1:
        return [send(values[0], MASK[orders[0][k]])]
    return [send(v, MASK[order[k]]) for v, order in zip(values, orders)]


def local(gate_pre, up_pre, hidden_grad, gate_weight, up_weight, routes):
    devices = lax.axis_size("expert")
    experts = devices // 2
    tokens = routes.shape[0]
    capacity = gate_pre.shape[1] // devices
    hidden = gate_pre.shape[2]

    inputs = [
        v.reshape(devices // 8, 4, 2, capacity, hidden) for v in (gate_pre, up_pre, hidden_grad)
    ]
    weights = [gate_weight[0], up_weight[0]]
    weights = weights + [send(w, 1) for w in weights]
    starts = [2 * sum(columns for _, columns in WAVES[:w]) for w in range(len(WAVES))]
    state = {}
    last = None
    for step in SCHEDULE:
        kind, number = step[0], int(step[1])
        if kind not in "AS":
            orders, columns = WAVES[number]
        if step == "A0":
            last = swiglu(1, after(inputs[0], last), *inputs[1:])
            state["other"] = send(last, 1)
        elif step == "A1":
            last = swiglu(0, after(inputs[0], last), *inputs[1:])
            state["own"] = last
        elif step == "S0":
            last = pl.pallas_call(
                slots_kernel,
                out_shape=jax.ShapeDtypeStruct((experts, tokens), jnp.int32),
                compiler_params=params(4),
            )(after(routes, last))[None]
            state["token"] = last
            state["slots"] = [last, send(last, MASK[X])]
        elif kind == "S":
            here, *arrived = state["slots"]
            last = join(after(here, last), *arrived)
            masks = [(MASK[Y],), (MASK[Z0], MASK[Z1], MASK[Z0] + MASK[Z1]), ()][number - 1]
            state["slots"] = [last] + [send(last, mask) for mask in masks]
        elif kind == "B":
            load = "loaded" not in state
            kept, last, state["other"], weights = expert_rows(
                after(state["token"], last), state["own"], state["other"], weights, orders,
                starts[number], columns, load,
            )
            state["loaded"] = True
            state["rows", number] = kept, send_all(last, orders, 0)
        elif kind == "C":
            last = token_rows(after(state["slots"][0], last), orders, *state["rows", number], None)
            state["second", number] = send_all(last, orders, 1)
        elif kind == "D":
            last = token_rows(
                after(state["slots"][0], last), orders, *state["rows", number], state["second", number]
            )
            state["third", number] = last[0], send_all(last[1], orders, 2)
        elif kind == "E":
            kept, third = state["third", number]
            last = add(after(state["token"], last), kept, third, [], orders[0][3] == orders[1][3])
            state["fourth", number] = kept, third, send_all(last, orders, 3)
        elif kind == "F":
            last = add(after(state["token"], last), *state["fourth", number], True)
            state["result", number] = [last[0][0], last[0][1]]
    return jnp.concatenate([v for w in range(len(WAVES)) for v in state["result", w]], axis=1)


def solution(mesh):
    placed = (
        P(("groups", "expert"), None, None),
        P(("groups", "expert"), None, None),
        P(("groups", "expert"), None, None),
        P("expert", None, None),
        P("expert", None, None),
        P(("groups", "expert"), None),
    )
    return jax.shard_map(
        local, mesh=mesh, in_specs=placed, out_specs=P(("groups", "expert"), None), check_vma=False
    )
```

time: 628 us -> 170 us (0.27)
  waiting for transfers between devices: 485 us -> 68.1 us
  matrix products: 59.8 us -> 0 us
  other arithmetic: 55.3 us -> 0 us
  Pallas kernels: 0 us -> 54.2 us
  starting transfers between devices: 7.59 us -> 39.5 us
  local copies, waits for them, and re-layouts: 20.4 us -> 7.72 us
    all_to_all x1 -> x0, waiting for transfers between devices: 485 us -> none  [local(): lax.all_to_all(partial_value.reshape(devices, capacity, model_width), 'ex...]
    ppermute x0 -> x38, waiting for transfers between devices: none -> 68.1 us  [send(): return lax.ppermute(value, 'expert', [(i, i ^ mask) for i in range(count)])]
    dot_general x2 -> x0, matrix products: 59.8 us -> none  [the longest x1 31.3 us: local(): lax.dot_general(grad_up, up_weight[0], dims, preferred_element_type=jnp.f...]
    pallas_call x0 -> x31, Pallas kernels: none -> 54.2 us  [the longest x5 39.4 us: expert_rows(): pl.pallas_call(functools.partial(rows_kernel, orders, start // TILE, load...]
    convert_element_type x3 -> x0, other arithmetic: 42.9 us -> none  [the longest x1 24.2 us: local(): arrived.reshape(experts, 2, capacity, model_width).astype(jnp.float32)]
    ppermute x0 -> x38, starting transfers between devices: none -> 39.5 us  [send(): return lax.ppermute(value, 'expert', [(i, i ^ mask) for i in range(count)])]
    gather x1 -> x0, local copies, waits for them, and re-layouts: 19.3 us -> none  [local(): token_rows = jnp.take(row_table, flat_routes * capacity + slot_ids, axis=0)]
    reduce_sum x2 -> x0, other arithmetic: 7.71 us -> none  [the longest x1 7.68 us: local(): jnp.sum(token_rows.reshape(tok_rows, chosen, model_width).astype(jnp.floa...]
  transfers between devices with their start and end apart: 1 -> 38, of which waited for: 1 -> 16; matrix products, arithmetic and copies ran while one was open for 1% -> 0% of each run, Pallas kernels for 0% -> 31%
where the time goes in v2:
time: 170 us
  waiting for transfers between devices  68.1 us (40%)
  Pallas kernels  54.2 us (32%)
  starting transfers between devices  39.5 us (23%)
  local copies, waits for them, and re-layouts  7.72 us (5%)
    ppermute x38, waiting for transfers between devices, send(): return lax.ppermute(value, 'expert', [(i, i ^ mask) for i in range(count)])  68.1 us
    ppermute x38, starting transfers between devices, send(): return lax.ppermute(value, 'expert', [(i, i ^ mask) for i in range(count)])  39.5 us
    pallas_call x5, Pallas kernels, expert_rows(): pl.pallas_call(functools.partial(rows_kernel, orders, start // TILE, load...  39.4 us
    pallas_call x2, Pallas kernels, swiglu(): pl.pallas_call(functools.partial(swiglu_kernel, side), in_specs=[HBM] * 3...  7.9 us
    unnamed x27, local copies, waits for them, and re-layouts  6.99 us
    pallas_call x10, Pallas kernels, token_rows(): pl.pallas_call(functools.partial(spread_kernel, orders, half, counts), in...  5.87 us
  transfers between devices with their start and end apart: 38, of which 16 were waited for; matrix products, arithmetic and copies ran while one was open for 0% of the time, Pallas kernels for 31%

profile of v2, /device:TPU:0, one launch (start us, length us, event | category | flops | bytes accessed | tf_op | source)
XLA Modules:
  0.0 169.9 jit_solution(5521959469464855823)
XLA Ops:
  0.5 4.4 %shard_map.64 = bf16[1536,1280]{1,0:T(8,128)(2,1)} custom-call(bf16[4,4,2,96,640]{4,3,2,1,0:T(8,128)(2,1)} %bitcast.63, bf16[4,4,2,96,640]{4,3,2,1,0:T(8,128)(2,1)} %bitcast.65, bf16[4,4,2,96,640]{4,3,2,1,0:T(8,128)(2,1)} %bitcast.67), custom_call_target="tpu_custom_call" | custom-call | flops 19660800 | bytes 9830400 | tf_op jit(solution)/shard_map/pallas_call | solution.py:122
  6.0 2.5 %collective-permute-start = (s32[1,16,128]{2,1,0:T(8,128)S(1)}, s32[1,16,128]{2,1,0:T(8,128)S(1)}, u32[]{:S(2)}, u32[]{:S(2)}) collective-permute-start(s32[1,16,128]{2,1,0:T(8,128)S(1)} %bitcast.46), channel_id=1, source_target_pairs={{0,2},{1,3},{2,0},{3,1},{4,6},{5,7},{6,4},{7,5},{8,10},{9,11},{10,... | collective-permute-start | bytes 24584 | tf_op jit(solution)/shard_map/ppermute | solution.py:33
  8.5 3.5 %shard_map.66.own = bf16[1536,1280]{1,0:T(8,128)(2,1)S(1)} custom-call(bf16[4,4,2,96,640]{4,3,2,1,0:T(8,128)(2,1)} %bitcast.64, bf16[4,4,2,96,640]{4,3,2,1,0:T(8,128)(2,1)} %bitcast.66, bf16[4,4,2,96,640]{4,3,2,1,0:T(8,128)(2,1)} %bitcast.68), custom_call_target="tpu_custom_call" | custom-call | flops 19660800 | bytes 9830400 | tf_op jit(solution)/shard_map/pallas_call | solution.py:122
  12.0 2.0 %copy-done = bf16[1536,1280]{1,0:T(8,128)(2,1)} copy-done((bf16[1536,1280]{1,0:T(8,128)(2,1)}, bf16[1536,1280]{1,0:T(8,128)(2,1)S(1)}, u32[]{:S(2)}) %copy-start) | copy-done | bytes 3932184
  14.0 1.6 collective-permute-start.1
  15.6 2.2 %collective-permute-done.1.refs_1_ = s32[2,16,128]{2,1,0:T(8,128)S(1)} collective-permute-done((s32[2,16,128]{2,1,0:T(8,128)S(1)}, s32[2,16,128]{2,1,0:T(8,128)S(1)}, u32[]{:S(2)}, u32[]{:S(2)}) %collective-permute-start.1) | collective-permute-done | bytes 16416 | tf_op jit(solution)/shard_map/ppermute | solution.py:33
  17.8 1.6 collective-permute-start.5
  19.5 2.6 %collective-permute-start.6 = (s32[4,16,128]{2,1,0:T(8,128)S(1)}, s32[4,16,128]{2,1,0:T(8,128)S(1)}, u32[]{:S(2)}, u32[]{:S(2)}) collective-permute-start(s32[4,16,128]{2,1,0:T(8,128)S(1)} %shard_map.68.refs_0_), channel_id=1, source_target_pairs={{0,16},{1,17},{2,18},{3,19},{4,20},{5,21},{6,22},{7,23},{8,24},{9,... | collective-permute-start | bytes 98312 | tf_op jit(solution)/shard_map/ppermute | solution.py:33
  22.0 3.3 %collective-permute-start.7 = (s32[4,16,128]{2,1,0:T(8,128)S(1)}, s32[4,16,128]{2,1,0:T(8,128)S(1)}, u32[]{:S(2)}, u32[]{:S(2)}) collective-permute-start(s32[4,16,128]{2,1,0:T(8,128)S(1)} %shard_map.68.refs_0_), channel_id=1, source_target_pairs={{0,24},{1,25},{2,26},{3,27},{4,28},{5,29},{6,30},{7,31},{8,16},{9,... | collective-permute-start | bytes 98312 | tf_op jit(solution)/shard_map/ppermute | solution.py:33
  25.3 15.6 %shard_map.69 = (bf16[2,8,96,512]{3,2,1,0:T(8,128)(2,1)S(1)}, bf16[1536,1280]{1,0:T(8,128)(2,1)S(1)}, bf16[14,256,2560]{2,1,0:T(8,128)(2,1)S(1)}, bf16[1,8,96,51...) custom-call(s32[1,16,128]{2,1,0:T(8,128)} %bitcast.48, bf16[1536,1280]{1,0:T(8,128)(2,1)} %copy-done, ...), custom_call_target="tpu_custom_call" | custom-call | flops 8053063680 | bytes 8388608 | tf_op jit(solution)/shard_map/pallas_call | solution.py:220
  41.0 1.9 %copy-done.2 = bf16[1536,1280]{1,0:T(8,128)(2,1)} copy-done((bf16[1536,1280]{1,0:T(8,128)(2,1)}, bf16[1536,1280]{1,0:T(8,128)(2,1)S(1)}, u32[]{:S(2)}) %copy-start.2) | copy-done | bytes 3932184
  44.3 1.5 collective-permute-start.9
  45.9 2.1 %copy-done.3 = bf16[1536,1280]{1,0:T(8,128)(2,1)S(1)} copy-done((bf16[1536,1280]{1,0:T(8,128)(2,1)S(1)}, bf16[1536,1280]{1,0:T(8,128)(2,1)}, u32[]{:S(2)}) %copy-start.3) | copy-done | bytes 3932184
  48.0 4.7 %shard_map.71 = (bf16[2,8,96,256]{3,2,1,0:T(8,128)(2,1)S(1)}, bf16[2,8,96,256]{3,2,1,0:T(8,128)(2,1)S(1)}) custom-call(s32[1,16,128]{2,1,0:T(8,128)S(1)} %bitcast.49, bf16[1536,1280]{1,0:T(8,128)(2,1)S(1)} %copy-done.1, bf16[1536,1280]{1,0:T(8,128)(2,1)S(1)} %copy-done.3, bf16[14,256,2560]{2,1,0:T(8,128)(2,1)S(1)} %get-tuple-element.82.refs_0_), custom_call_target="tpu_custom_call" | custom-call | flops 4026531840 | bytes 4194304 | tf_op jit(solution)/shard_map/pallas_call | solution.py:220
  52.8 9.4 %shard_map.72 = (bf16[2,8,96,512]{3,2,1,0:T(8,128)(2,1)S(1)}, bf16[1,8,96,512]{3,2,1,0:T(8,128)(2,1)S(1)}, bf16[1,8,96,512]{3,2,1,0:T(8,128)(2,1)S(1)}) custom-call(s32[1,16,128]{2,1,0:T(8,128)S(1)} %bitcast.50, bf16[1536,1280]{1,0:T(8,128)(2,1)S(1)} %copy-done.1, bf16[1536,1280]{1,0:T(8,128)(2,1)S(1)} %copy-done.3, ...), custom_call_target="tpu_custom_call" | custom-call | flops 8053063680 | bytes 8388608 | tf_op jit(solution)/shard_map/pallas_call | solution.py:220
  64.1 1.6 collective-permute-start.11
  66.2 4.7 %shard_map.74 = (bf16[2,8,96,256]{3,2,1,0:T(8,128)(2,1)S(1)}, bf16[2,8,96,256]{3,2,1,0:T(8,128)(2,1)S(1)}) custom-call(s32[1,16,128]{2,1,0:T(8,128)S(1)} %bitcast.51, bf16[1536,1280]{1,0:T(8,128)(2,1)S(1)} %copy-done.1, bf16[1536,1280]{1,0:T(8,128)(2,1)S(1)} %copy-done.4, bf16[14,256,2560]{2,1,0:T(8,128)(2,1)S(1)} %get-tuple-element.82.refs_0_), custom_call_target="tpu_custom_call" | custom-call | flops 4026531840 | bytes 4194304 | tf_op jit(solution)/shard_map/pallas_call | solution.py:220
  71.0 1.6 collective-permute-start.14
  74.4 4.6 %collective-permute-done.11.refs_2_ = bf16[1,4,128,512]{3,2,1,0:T(8,128)(2,1)S(1)} collective-permute-done((bf16[1,4,128,512]{3,2,1,0:T(8,128)(2,1)S(1)}, bf16[1,4,128,512]{3,2,1,0:T(8,128)(2,1)S(1)}, u32[]{:S(2)}, u32[]{:S(2)}) %collective-permute-start.11) | collective-permute-done | bytes 524320 | tf_op jit(solution)/shard_map/ppermute | solution.py:33
  79.0 1.5 collective-permute-done.12.refs_3_
  81.4 4.9 %shard_map.77 = (bf16[2,8,96,256]{3,2,1,0:T(8,128)(2,1)S(1)}, bf16[1,8,96,256]{3,2,1,0:T(8,128)(2,1)S(1)}, bf16[1,8,96,256]{3,2,1,0:T(8,128)(2,1)S(1)}) custom-call(s32[1,16,128]{2,1,0:T(8,128)S(1)} %bitcast.52, bf16[1536,1280]{1,0:T(8,128)(2,1)S(1)} %copy-done.1, bf16[1536,1280]{1,0:T(8,128)(2,1)S(1)} %copy-done.4, ...), custom_call_target="tpu_custom_call" | custom-call | flops 4026531840 | bytes 4194304 | tf_op jit(solution)/shard_map/pallas_call | solution.py:220
  86.9 4.6 %collective-permute-done.13.refs_0_ = bf16[2,8,96,256]{3,2,1,0:T(8,128)(2,1)S(1)} collective-permute-done((bf16[2,8,96,256]{3,2,1,0:T(8,128)(2,1)S(1)}, bf16[2,8,96,256]{3,2,1,0:T(8,128)(2,1)S(1)}, u32[]{:S(2)}, u32[]{:S(2)}) %collective-permute-start.13) | collective-permute-done | bytes 786464 | tf_op jit(solution)/shard_map/ppermute | solution.py:33
  92.5 4.9 %collective-permute-done.14.refs_0_ = bf16[1,8,96,512]{3,2,1,0:T(8,128)(2,1)S(1)} collective-permute-done((bf16[1,8,96,512]{3,2,1,0:T(8,128)(2,1)S(1)}, bf16[1,8,96,512]{3,2,1,0:T(8,128)(2,1)S(1)}, u32[]{:S(2)}, u32[]{:S(2)}) %collective-permute-start.14) | collective-permute-done | bytes 786464 | tf_op jit(solution)/shard_map/ppermute | solution.py:33
  100.0 5.8 %collective-permute-done.17.refs_0_ = bf16[1,8,96,256]{3,2,1,0:T(8,128)(2,1)S(1)} collective-permute-done((bf16[1,8,96,256]{3,2,1,0:T(8,128)(2,1)S(1)}, bf16[1,8,96,256]{3,2,1,0:T(8,128)(2,1)S(1)}, u32[]{:S(2)}, u32[]{:S(2)}) %collective-permute-start.17) | collective-permute-done | bytes 393248 | tf_op jit(solution)/shard_map/ppermute | solution.py:33
  113.1 12.6 %collective-permute-done.22.refs_1_ = bf16[1,4,128,256]{3,2,1,0:T(8,128)(2,1)S(1)} collective-permute-done((bf16[1,4,128,256]{3,2,1,0:T(8,128)(2,1)S(1)}, bf16[1,4,128,256]{3,2,1,0:T(8,128)(2,1)S(1)}, u32[]{:S(2)}, u32[]{:S(2)}) %collective-permute-start.22) | collective-permute-done | bytes 262176 | tf_op jit(solution)/shard_map/ppermute | solution.py:33
  131.3 10.8 %collective-permute-done.27.refs_0_ = bf16[2,2,128,256]{3,2,1,0:T(8,128)(2,1)S(1)} collective-permute-done((bf16[2,2,128,256]{3,2,1,0:T(8,128)(2,1)S(1)}, bf16[2,2,128,256]{3,2,1,0:T(8,128)(2,1)S(1)}, u32[]{:S(2)}, u32[]{:S(2)}) %collective-permute-start.27) | collective-permute-done | bytes 262176 | tf_op jit(solution)/shard_map/ppermute | solution.py:33
  142.7 4.3 %collective-permute-done.31.refs_1_ = bf16[1,2,128,256]{3,2,1,0:T(8,128)(2,1)S(1)} collective-permute-done((bf16[1,2,128,256]{3,2,1,0:T(8,128)(2,1)S(1)}, bf16[1,2,128,256]{3,2,1,0:T(8,128)(2,1)S(1)}, u32[]{:S(2)}, u32[]{:S(2)}) %collective-permute-start.31) | collective-permute-done | bytes 131104 | tf_op jit(solution)/shard_map/ppermute | solution.py:33
  147.1 3.5 %collective-permute-start.35 = (bf16[2,128,512]{2,1,0:T(8,128)(2,1)S(1)}, bf16[2,128,512]{2,1,0:T(8,128)(2,1)S(1)}, u32[]{:S(2)}, u32[]{:S(2)}) collective-permute-start(bf16[2,128,512]{2,1,0:T(8,128)(2,1)S(1)} %shard_map.90), channel_id=1, source_target_pairs={{0,16},{1,17},{2,18},{3,19},{4,20},{5,21},{6,22},{7,23},{8,24},{9,... | collective-permute-start | bytes 786440 | tf_op jit(solution)/shard_map/ppermute | solution.py:33
  150.7 1.5 collective-permute-start.36
  152.8 2.8 %collective-permute-start.34 = (bf16[2,128,256]{2,1,0:T(8,128)(2,1)S(1)}, bf16[2,128,256]{2,1,0:T(8,128)(2,1)S(1)}, u32[]{:S(2)}, u32[]{:S(2)}) collective-permute-start(bf16[2,128,256]{2,1,0:T(8,128)(2,1)S(1)} %shard_map.89), channel_id=1, source_target_pairs={{0,16},{1,17},{2,18},{3,19},{4,20},{5,21},{6,22},{7,23},{8,24},{9,... | collective-permute-start | bytes 393224 | tf_op jit(solution)/shard_map/ppermute | solution.py:33
  155.7 10.6 %collective-permute-done.33.refs_2_ = bf16[2,128,256]{2,1,0:T(8,128)(2,1)S(1)} collective-permute-done((bf16[2,128,256]{2,1,0:T(8,128)(2,1)S(1)}, bf16[2,128,256]{2,1,0:T(8,128)(2,1)S(1)}, u32[]{:S(2)}, u32[]{:S(2)}) %collective-permute-start.33) | collective-permute-done | bytes 131104 | tf_op jit(solution)/shard_map/ppermute | solution.py:33
  166.3 1.7 %collective-permute-done.34.refs_2_ = bf16[2,128,256]{2,1,0:T(8,128)(2,1)S(1)} collective-permute-done((bf16[2,128,256]{2,1,0:T(8,128)(2,1)S(1)}, bf16[2,128,256]{2,1,0:T(8,128)(2,1)S(1)}, u32[]{:S(2)}, u32[]{:S(2)}) %collective-permute-start.34) | collective-permute-done | bytes 131104 | tf_op jit(solution)/shard_map/ppermute | solution.py:33
  (104 shorter events, 28.5 us)
Async XLA Ops:
  0.0 25.3 %collective-permute-start.3 = (bf16[3584,640]{1,0:T(8,128)(2,1)}, bf16[3584,640]{1,0:T(8,128)(2,1)}, u32[]{:S(2)}, u32[]{:S(2)}) collective-permute-start(bf16[3584,640]{1,0:T(8,128)(2,1)} %bitcast.69), channel_id=1, source_target_pairs={{0,1},{1,0},{2,3},{3,2},{4,5},{5,4},{6,7},{7,6},{8,9},{9,8},{10,11... | collective-permute-start | bytes 13762568 | tf_op jit(solution)/shard_map/ppermute | solution.py:33
  0.5 24.9 %collective-permute-start.4 = (bf16[3584,640]{1,0:T(8,128)(2,1)}, bf16[3584,640]{1,0:T(8,128)(2,1)}, u32[]{:S(2)}, u32[]{:S(2)}) collective-permute-start(bf16[3584,640]{1,0:T(8,128)(2,1)} %bitcast.71), channel_id=1, source_target_pairs={{0,1},{1,0},{2,3},{3,2},{4,5},{5,4},{6,7},{7,6},{8,9},{9,8},{10,11... | collective-permute-start | bytes 13762568 | tf_op jit(solution)/shard_map/ppermute | solution.py:33
  4.9 17.1 %collective-permute-start.2 = (bf16[1536,1280]{1,0:T(8,128)(2,1)}, bf16[1536,1280]{1,0:T(8,128)(2,1)}, u32[]{:S(2)}, u32[]{:S(2)}) collective-permute-start(bf16[1536,1280]{1,0:T(8,128)(2,1)} %shard_map.64), channel_id=1, source_target_pairs={{0,1},{1,0},{2,3},{3,2},{4,5},{5,4},{6,7},{7,6},{8,9},{9,8},{10,11... | collective-permute-start | bytes 11796488 | tf_op jit(solution)/shard_map/ppermute | solution.py:33
  17.8 28.0 %collective-permute-start.5 = (s32[4,16,128]{2,1,0:T(8,128)S(1)}, s32[4,16,128]{2,1,0:T(8,128)S(1)}, u32[]{:S(2)}, u32[]{:S(2)}) collective-permute-start(s32[4,16,128]{2,1,0:T(8,128)S(1)} %shard_map.68.refs_0_), channel_id=1, source_target_pairs={{0,8},{1,9},{2,10},{3,11},{4,12},{5,13},{6,14},{7,15},{8,0},{9,1},... | collective-permute-start | bytes 98312 | tf_op jit(solution)/shard_map/ppermute | solution.py:33
  19.5 26.4 %collective-permute-start.6 = (s32[4,16,128]{2,1,0:T(8,128)S(1)}, s32[4,16,128]{2,1,0:T(8,128)S(1)}, u32[]{:S(2)}, u32[]{:S(2)}) collective-permute-start(s32[4,16,128]{2,1,0:T(8,128)S(1)} %shard_map.68.refs_0_), channel_id=1, source_target_pairs={{0,16},{1,17},{2,18},{3,19},{4,20},{5,21},{6,22},{7,23},{8,24},{9,... | collective-permute-start | bytes 98312 | tf_op jit(solution)/shard_map/ppermute | solution.py:33
  22.0 23.8 %collective-permute-start.7 = (s32[4,16,128]{2,1,0:T(8,128)S(1)}, s32[4,16,128]{2,1,0:T(8,128)S(1)}, u32[]{:S(2)}, u32[]{:S(2)}) collective-permute-start(s32[4,16,128]{2,1,0:T(8,128)S(1)} %shard_map.68.refs_0_), channel_id=1, source_target_pairs={{0,24},{1,25},{2,26},{3,27},{4,28},{5,29},{6,30},{7,31},{8,16},{9,... | collective-permute-start | bytes 98312 | tf_op jit(solution)/shard_map/ppermute | solution.py:33
  42.8 19.4 %collective-permute-start.8 = (bf16[1,8,96,512]{3,2,1,0:T(8,128)(2,1)S(1)}, bf16[1,8,96,512]{3,2,1,0:T(8,128)(2,1)S(1)}, u32[]{:S(2)}, u32[]{:S(2)}) collective-permute-start(bf16[1,8,96,512]{3,2,1,0:T(8,128)(2,1)S(1)} %get-tuple-element.77), channel_id=1, source_target_pairs={{0,2},{1,3},{2,0},{3,1},{4,6},{5,7},{6,4},{7,5},{8,10},{9,11},{10,... | collective-permute-start | bytes 2359304 | tf_op jit(solution)/shard_map/ppermute | solution.py:33
  44.3 19.0 %collective-permute-start.9 = (bf16[1,8,96,512]{3,2,1,0:T(8,128)(2,1)S(1)}, bf16[1,8,96,512]{3,2,1,0:T(8,128)(2,1)S(1)}, u32[]{:S(2)}, u32[]{:S(2)}) collective-permute-start(bf16[1,8,96,512]{3,2,1,0:T(8,128)(2,1)S(1)} %get-tuple-element.78), channel_id=1, source_target_pairs={{0,4},{1,5},{2,6},{3,7},{4,0},{5,1},{6,2},{7,3},{8,12},{9,13},{10,... | collective-permute-start | bytes 2359304 | tf_op jit(solution)/shard_map/ppermute | solution.py:33
  52.7 19.8 %collective-permute-start.10 = (bf16[2,8,96,256]{3,2,1,0:T(8,128)(2,1)S(1)}, bf16[2,8,96,256]{3,2,1,0:T(8,128)(2,1)S(1)}, u32[]{:S(2)}, u32[]{:S(2)}) collective-permute-start(bf16[2,8,96,256]{3,2,1,0:T(8,128)(2,1)S(1)} %get-tuple-element.83), channel_id=1, source_target_pairs={{0,8},{1,9},{2,10},{3,11},{4,12},{5,13},{6,14},{7,15},{8,0},{9,1},... | collective-permute-start | bytes 2359304 | tf_op jit(solution)/shard_map/ppermute | solution.py:33
  64.1 14.9 %collective-permute-start.11 = (bf16[1,4,128,512]{3,2,1,0:T(8,128)(2,1)S(1)}, bf16[1,4,128,512]{3,2,1,0:T(8,128)(2,1)S(1)}, u32[]{:S(2)}, u32[]{:S(2)}) collective-permute-start(bf16[1,4,128,512]{3,2,1,0:T(8,128)(2,1)S(1)} %get-tuple-element.89), channel_id=1, source_target_pairs={{0,4},{1,5},{2,6},{3,7},{4,0},{5,1},{6,2},{7,3},{8,12},{9,13},{10,... | collective-permute-start | bytes 1572872 | tf_op jit(solution)/shard_map/ppermute | solution.py:33
  65.7 14.9 %collective-permute-start.12 = (bf16[1,4,128,512]{3,2,1,0:T(8,128)(2,1)S(1)}, bf16[1,4,128,512]{3,2,1,0:T(8,128)(2,1)S(1)}, u32[]{:S(2)}, u32[]{:S(2)}) collective-permute-start(bf16[1,4,128,512]{3,2,1,0:T(8,128)(2,1)S(1)} %get-tuple-element.90), channel_id=1, source_target_pairs={{0,2},{1,3},{2,0},{3,1},{4,6},{5,7},{6,4},{7,5},{8,10},{9,11},{10,... | collective-permute-start | bytes 1572872 | tf_op jit(solution)/shard_map/ppermute | solution.py:33
  70.9 20.5 %collective-permute-start.13 = (bf16[2,8,96,256]{3,2,1,0:T(8,128)(2,1)S(1)}, bf16[2,8,96,256]{3,2,1,0:T(8,128)(2,1)S(1)}, u32[]{:S(2)}, u32[]{:S(2)}) collective-permute-start(bf16[2,8,96,256]{3,2,1,0:T(8,128)(2,1)S(1)} %get-tuple-element.92), channel_id=1, source_target_pairs={{0,8},{1,9},{2,10},{3,11},{4,12},{5,13},{6,14},{7,15},{8,0},{9,1},... | collective-permute-start | bytes 2359304 | tf_op jit(solution)/shard_map/ppermute | solution.py:33
  71.0 26.4 %collective-permute-start.14 = (bf16[1,8,96,512]{3,2,1,0:T(8,128)(2,1)S(1)}, bf16[1,8,96,512]{3,2,1,0:T(8,128)(2,1)S(1)}, u32[]{:S(2)}, u32[]{:S(2)}) collective-permute-start(bf16[1,8,96,512]{3,2,1,0:T(8,128)(2,1)S(1)} %get-tuple-element.85), channel_id=1, source_target_pairs={{0,2},{1,3},{2,0},{3,1},{4,6},{5,7},{6,4},{7,5},{8,10},{9,11},{10,... | collective-permute-start | bytes 2359304 | tf_op jit(solution)/shard_map/ppermute | solution.py:33
  72.6 25.4 %collective-permute-start.15 = (bf16[1,8,96,512]{3,2,1,0:T(8,128)(2,1)S(1)}, bf16[1,8,96,512]{3,2,1,0:T(8,128)(2,1)S(1)}, u32[]{:S(2)}, u32[]{:S(2)}) collective-permute-start(bf16[1,8,96,512]{3,2,1,0:T(8,128)(2,1)S(1)} %get-tuple-element.86), channel_id=1, source_target_pairs={{0,4},{1,5},{2,6},{3,7},{4,0},{5,1},{6,2},{7,3},{8,12},{9,13},{10,... | collective-permute-start | bytes 2359304 | tf_op jit(solution)/shard_map/ppermute | solution.py:33
  81.3 18.6 %collective-permute-start.16 = (bf16[2,2,128,512]{3,2,1,0:T(8,128)(2,1)S(1)}, bf16[2,2,128,512]{3,2,1,0:T(8,128)(2,1)S(1)}, u32[]{:S(2)}, u32[]{:S(2)}) collective-permute-start(bf16[2,2,128,512]{3,2,1,0:T(8,128)(2,1)S(1)} %get-tuple-element.99), channel_id=1, source_target_pairs={{0,8},{1,9},{2,10},{3,11},{4,12},{5,13},{6,14},{7,15},{8,0},{9,1},... | collective-permute-start | bytes 1572872 | tf_op jit(solution)/shard_map/ppermute | solution.py:33
  86.3 19.5 %collective-permute-start.17 = (bf16[1,8,96,256]{3,2,1,0:T(8,128)(2,1)S(1)}, bf16[1,8,96,256]{3,2,1,0:T(8,128)(2,1)S(1)}, u32[]{:S(2)}, u32[]{:S(2)}) collective-permute-start(bf16[1,8,96,256]{3,2,1,0:T(8,128)(2,1)S(1)} %get-tuple-element.101), channel_id=1, source_target_pairs={{0,2},{1,3},{2,0},{3,1},{4,6},{5,7},{6,4},{7,5},{8,10},{9,11},{10,... | collective-permute-start | bytes 1179656 | tf_op jit(solution)/shard_map/ppermute | solution.py:33
  91.5 14.4 %collective-permute-start.18 = (bf16[1,8,96,256]{3,2,1,0:T(8,128)(2,1)S(1)}, bf16[1,8,96,256]{3,2,1,0:T(8,128)(2,1)S(1)}, u32[]{:S(2)}, u32[]{:S(2)}) collective-permute-start(bf16[1,8,96,256]{3,2,1,0:T(8,128)(2,1)S(1)} %get-tuple-element.102), channel_id=1, source_target_pairs={{0,4},{1,5},{2,6},{3,7},{4,0},{5,1},{6,2},{7,3},{8,12},{9,13},{10,... | collective-permute-start | bytes 1179656 | tf_op jit(solution)/shard_map/ppermute | solution.py:33
  106.3 19.9 %collective-permute-start.24 = (bf16[2,4,128,256]{3,2,1,0:T(8,128)(2,1)S(1)}, bf16[2,4,128,256]{3,2,1,0:T(8,128)(2,1)S(1)}, u32[]{:S(2)}, u32[]{:S(2)}) collective-permute-start(bf16[2,4,128,256]{3,2,1,0:T(8,128)(2,1)S(1)} %shard_map.81), channel_id=1, source_target_pairs={{0,8},{1,9},{2,10},{3,11},{4,12},{5,13},{6,14},{7,15},{8,0},{9,1},... | collective-permute-start | bytes 1572872 | tf_op jit(solution)/shard_map/ppermute | solution.py:33
  106.4 20.3 %collective-permute-start.25 = (bf16[1,4,128,512]{3,2,1,0:T(8,128)(2,1)S(1)}, bf16[1,4,128,512]{3,2,1,0:T(8,128)(2,1)S(1)}, u32[]{:S(2)}, u32[]{:S(2)}) collective-permute-start(bf16[1,4,128,512]{3,2,1,0:T(8,128)(2,1)S(1)} %get-tuple-element.109), channel_id=1, source_target_pairs={{0,4},{1,5},{2,6},{3,7},{4,0},{5,1},{6,2},{7,3},{8,12},{9,13},{10,... | collective-permute-start | bytes 1572872 | tf_op jit(solution)/shard_map/ppermute | solution.py:33
  108.8 17.9 %collective-permute-start.26 = (bf16[1,4,128,512]{3,2,1,0:T(8,128)(2,1)S(1)}, bf16[1,4,128,512]{3,2,1,0:T(8,128)(2,1)S(1)}, u32[]{:S(2)}, u32[]{:S(2)}) collective-permute-start(bf16[1,4,128,512]{3,2,1,0:T(8,128)(2,1)S(1)} %get-tuple-element.110), channel_id=1, source_target_pairs={{0,2},{1,3},{2,0},{3,1},{4,6},{5,7},{6,4},{7,5},{8,10},{9,11},{10,... | collective-permute-start | bytes 1572872 | tf_op jit(solution)/shard_map/ppermute | solution.py:33
  109.9 15.8 %collective-permute-start.22 = (bf16[1,4,128,256]{3,2,1,0:T(8,128)(2,1)S(1)}, bf16[1,4,128,256]{3,2,1,0:T(8,128)(2,1)S(1)}, u32[]{:S(2)}, u32[]{:S(2)}) collective-permute-start(bf16[1,4,128,256]{3,2,1,0:T(8,128)(2,1)S(1)} %get-tuple-element.95), channel_id=1, source_target_pairs={{0,2},{1,3},{2,0},{3,1},{4,6},{5,7},{6,4},{7,5},{8,10},{9,11},{10,... | collective-permute-start | bytes 786440 | tf_op jit(solution)/shard_map/ppermute | solution.py:33
  112.0 13.7 %collective-permute-start.23 = (bf16[1,4,128,256]{3,2,1,0:T(8,128)(2,1)S(1)}, bf16[1,4,128,256]{3,2,1,0:T(8,128)(2,1)S(1)}, u32[]{:S(2)}, u32[]{:S(2)}) collective-permute-start(bf16[1,4,128,256]{3,2,1,0:T(8,128)(2,1)S(1)} %get-tuple-element.96), channel_id=1, source_target_pairs={{0,4},{1,5},{2,6},{3,7},{4,0},{5,1},{6,2},{7,3},{8,12},{9,13},{10,... | collective-permute-start | bytes 786440 | tf_op jit(solution)/shard_map/ppermute | solution.py:33
  127.5 19.6 %collective-permute-start.32 = (bf16[2,2,128,512]{3,2,1,0:T(8,128)(2,1)S(1)}, bf16[2,2,128,512]{3,2,1,0:T(8,128)(2,1)S(1)}, u32[]{:S(2)}, u32[]{:S(2)}) collective-permute-start(bf16[2,2,128,512]{3,2,1,0:T(8,128)(2,1)S(1)} %get-tuple-element.128), channel_id=1, source_target_pairs={{0,8},{1,9},{2,10},{3,11},{4,12},{5,13},{6,14},{7,15},{8,0},{9,1},... | collective-permute-start | bytes 1572872 | tf_op jit(solution)/shard_map/ppermute | solution.py:33
  128.2 13.9 %collective-permute-start.27 = (bf16[2,2,128,256]{3,2,1,0:T(8,128)(2,1)S(1)}, bf16[2,2,128,256]{3,2,1,0:T(8,128)(2,1)S(1)}, u32[]{:S(2)}, u32[]{:S(2)}) collective-permute-start(bf16[2,2,128,256]{3,2,1,0:T(8,128)(2,1)S(1)} %get-tuple-element.116), channel_id=1, source_target_pairs={{0,16},{1,17},{2,18},{3,19},{4,20},{5,21},{6,22},{7,23},{8,24},{9,... | collective-permute-start | bytes 786440 | tf_op jit(solution)/shard_map/ppermute | solution.py:33
  128.6 14.0 %collective-permute-start.28 = (bf16[1,2,128,256]{3,2,1,0:T(8,128)(2,1)S(1)}, bf16[1,2,128,256]{3,2,1,0:T(8,128)(2,1)S(1)}, u32[]{:S(2)}, u32[]{:S(2)}) collective-permute-start(bf16[1,2,128,256]{3,2,1,0:T(8,128)(2,1)S(1)} %get-tuple-element.120), channel_id=1, source_target_pairs={{0,4},{1,5},{2,6},{3,7},{4,0},{5,1},{6,2},{7,3},{8,12},{9,13},{10,... | collective-permute-start | bytes 393224 | tf_op jit(solution)/shard_map/ppermute | solution.py:33
  129.7 12.9 %collective-permute-start.29 = (bf16[1,2,128,256]{3,2,1,0:T(8,128)(2,1)S(1)}, bf16[1,2,128,256]{3,2,1,0:T(8,128)(2,1)S(1)}, u32[]{:S(2)}, u32[]{:S(2)}) collective-permute-start(bf16[1,2,128,256]{3,2,1,0:T(8,128)(2,1)S(1)} %get-tuple-element.121), channel_id=1, source_target_pairs={{0,2},{1,3},{2,0},{3,1},{4,6},{5,7},{6,4},{7,5},{8,10},{9,11},{10,... | collective-permute-start | bytes 393224 | tf_op jit(solution)/shard_map/ppermute | solution.py:33
  130.3 12.4 %collective-permute-start.30 = (bf16[1,2,128,256]{3,2,1,0:T(8,128)(2,1)S(1)}, bf16[1,2,128,256]{3,2,1,0:T(8,128)(2,1)S(1)}, u32[]{:S(2)}, u32[]{:S(2)}) collective-permute-start(bf16[1,2,128,256]{3,2,1,0:T(8,128)(2,1)S(1)} %get-tuple-element.124), channel_id=1, source_target_pairs={{0,4},{1,5},{2,6},{3,7},{4,0},{5,1},{6,2},{7,3},{8,12},{9,13},{10,... | collective-permute-start | bytes 393224 | tf_op jit(solution)/shard_map/ppermute | solution.py:33
  147.1 20.9 %collective-permute-start.35 = (bf16[2,128,512]{2,1,0:T(8,128)(2,1)S(1)}, bf16[2,128,512]{2,1,0:T(8,128)(2,1)S(1)}, u32[]{:S(2)}, u32[]{:S(2)}) collective-permute-start(bf16[2,128,512]{2,1,0:T(8,128)(2,1)S(1)} %shard_map.90), channel_id=1, source_target_pairs={{0,16},{1,17},{2,18},{3,19},{4,20},{5,21},{6,22},{7,23},{8,24},{9,... | collective-permute-start | bytes 786440 | tf_op jit(solution)/shard_map/ppermute | solution.py:33
  150.6 15.6 %collective-permute-start.33 = (bf16[2,128,256]{2,1,0:T(8,128)(2,1)S(1)}, bf16[2,128,256]{2,1,0:T(8,128)(2,1)S(1)}, u32[]{:S(2)}, u32[]{:S(2)}) collective-permute-start(bf16[2,128,256]{2,1,0:T(8,128)(2,1)S(1)} %shard_map.88), channel_id=1, source_target_pairs={{0,16},{1,17},{2,18},{3,19},{4,20},{5,21},{6,22},{7,23},{8,24},{9,... | collective-permute-start | bytes 393224 | tf_op jit(solution)/shard_map/ppermute | solution.py:33
  150.7 17.5 %collective-permute-start.36 = (bf16[1,128,256]{2,1,0:T(8,128)(2,1)S(1)}, bf16[1,128,256]{2,1,0:T(8,128)(2,1)S(1)}, u32[]{:S(2)}, u32[]{:S(2)}) collective-permute-start(bf16[1,128,256]{2,1,0:T(8,128)(2,1)S(1)} %get-tuple-element.130), channel_id=1, source_target_pairs={{0,4},{1,5},{2,6},{3,7},{4,0},{5,1},{6,2},{7,3},{8,12},{9,13},{10,... | collective-permute-start | bytes 196616 | tf_op jit(solution)/shard_map/ppermute | solution.py:33
  152.2 16.0 %collective-permute-start.37 = (bf16[1,128,256]{2,1,0:T(8,128)(2,1)S(1)}, bf16[1,128,256]{2,1,0:T(8,128)(2,1)S(1)}, u32[]{:S(2)}, u32[]{:S(2)}) collective-permute-start(bf16[1,128,256]{2,1,0:T(8,128)(2,1)S(1)} %get-tuple-element.131), channel_id=1, source_target_pairs={{0,2},{1,3},{2,0},{3,1},{4,6},{5,7},{6,4},{7,5},{8,10},{9,11},{10,... | collective-permute-start | bytes 196616 | tf_op jit(solution)/shard_map/ppermute | solution.py:33
  152.8 15.2 %collective-permute-start.34 = (bf16[2,128,256]{2,1,0:T(8,128)(2,1)S(1)}, bf16[2,128,256]{2,1,0:T(8,128)(2,1)S(1)}, u32[]{:S(2)}, u32[]{:S(2)}) collective-permute-start(bf16[2,128,256]{2,1,0:T(8,128)(2,1)S(1)} %shard_map.89), channel_id=1, source_target_pairs={{0,16},{1,17},{2,18},{3,19},{4,20},{5,21},{6,22},{7,23},{8,24},{9,... | collective-permute-start | bytes 393224 | tf_op jit(solution)/shard_map/ppermute | solution.py:33
  (15 other events, 141.8 us)

commit v3 on v2

--- a/solution.py
+++ b/solution.py
@@ -16,12 +16,13 @@
 BZ = (Z0, X, Z1, Y), (Z0, Y, Z1, X)
 D = (X, Z0, Y, Z1), (Y, Z0, X, Z1)
 E = (X, Z0, Z1, Y), (Y, Z0, Z1, X)
-WAVES = ((AH, 512), (BZ, 256), (AH, 512), (BH, 256), (D, 256))
+WAVES = ((AH, 512), (BH, 256), (E, 256), (AM, 512), (AH, 256))
 SCHEDULE = (
-    *("A0", "S0", "A1", "S1", "S2", "B0", "S3", "B3", "B2", "C0", "B1", "C3", "D0", "B4", "C1", "C2"),
-    *("E0", "C4", "D1", "F0", "D3", "D4", "D2", "E1", "E3", "E4", "E2", "F3", "F4", "F2", "F1"),
+    *("A0", "S0", "A1", "S1", "S2", "B0", "S3", "B1", "B2", "C0", "B3", "C2", "C1", "D0", "D2", "C3"),
+    *("E0", "E2", "B4", "D3", "F0", "C4", "E3", "D1", "D4", "E1", "F3", "E4", "F1", "F2", "F4"),
 )
 TILE = 256
+LIMITS = 26, 6
 
 
 def mask_of(position):
@@ -66,7 +67,7 @@
 
 def swiglu_kernel(side, gate_pre, up_pre, hidden_grad, result, values, ready, *refs):
     capacity, width = values.shape[3:]
-    out, out_ready = refs if side else (result, None)
+    out, out_ready = refs
     me = lax.axis_index("expert").astype(jnp.int32)
     core, plane, layer = (me & 1) ^ side, (me >> 1) & 3, me >> 3
 
@@ -100,11 +101,9 @@
             out[rows, :width] = full.astype(jnp.bfloat16)
             out[rows, width:] = linear.astype(jnp.bfloat16)
 
-        if side:
-            out_copy(group).start()
-    if side:
-        for group in range(4):
-            out_copy(group).wait()
+        out_copy(group).start()
+    for group in range(4):
+        out_copy(group).wait()
 
 
 def swiglu(side, gate_pre, up_pre, hidden_grad):
@@ -113,19 +112,16 @@
     scratch_shapes = [
         pltpu.VMEM((3, chips, layers, capacity, width), jnp.bfloat16),
         pltpu.SemaphoreType.DMA((3, chips)),
+        pltpu.VMEM((rows, 2 * width), jnp.bfloat16),
+        pltpu.SemaphoreType.DMA((chips,)),
     ]
-    if side:
-        scratch_shapes += [
-            pltpu.VMEM((rows, 2 * width), jnp.bfloat16),
-            pltpu.SemaphoreType.DMA((chips,)),
-        ]
     return pl.pallas_call(
         functools.partial(swiglu_kernel, side),
         in_specs=[HBM] * 3,
-        out_specs=HBM if side else INSIDE,
-        out_shape=jax.ShapeDtypeStruct((rows, 2 * width), jnp.bfloat16) if side else inside(rows, 2 * width),
+        out_specs=HBM,
+        out_shape=jax.ShapeDtypeStruct((rows, 2 * width), jnp.bfloat16),
         scratch_shapes=scratch_shapes,
-        compiler_params=params(62 if side else 57),
+        compiler_params=params(62),
         cost_estimate=pl.CostEstimate(
             flops=10 * rows * 2 * width,
             bytes_accessed=5 * rows * 2 * width,
@@ -134,14 +130,13 @@
     )(gate_pre, up_pre, hidden_grad)
 
 
-def rows_kernel(orders, first, load, _, own, other, *refs):
+def rows_kernel(orders, first, load, _, *refs):
     if load:
-        weights, (kept, loaded, weight, *sent, weight_ready, other_ready) = refs[:4], refs[4:]
-        other_copy = pltpu.make_async_copy(other, loaded, other_ready)
-        other = loaded
+        sources, weights, refs = refs[:2], refs[2:6], refs[6:]
+        kept, grads, weight, *sent, weight_ready, grads_ready = refs
     else:
-        weight, kept, *sent = refs
-    depth = own.shape[1]
+        grads, weight, kept, *sent = refs
+    depth = grads.shape[2]
     width = depth // 2
     tile = weight.shape[1]
     capacity, columns = kept.shape[2:]
@@ -157,7 +152,7 @@
     def part(t, side):
         at = slice(side * depth, (side + 1) * depth)
         return lax.dot_general(
-            (own, other)[side][...],
+            grads[side],
             weight[first + t, :, at],
             (((1,), (1,)), ((), ())),
             preferred_element_type=jnp.float32,
@@ -166,10 +161,27 @@
     def place(order, position):
         return sum(4 >> k for k in range(3) if position & order[k + 1])
 
+    def grads_copy(side, i):
+        rows = pl.ds(pl.multiple_of(i * capacity, capacity), capacity)
+        return pltpu.make_async_copy(
+            sources[side].at[rows], grads.at[side, rows], grads_ready.at[side, i]
+        )
+
+    def wait_grads(side):
+        @pl.loop(0, 16)
+        def _(i):
+            grads_copy(side, i).wait()
+
     if load:
-        other_copy.start()
-
-        @pl.loop(0, weight.shape[0])
+        for side in range(2):
+            for i in range(2 * side, 2 * side + 2):
+                weight_copy(0, i).start()
+
+            @pl.loop(0, 16)
+            def _(i):
+                grads_copy(side, i).start()
+
+        @pl.loop(1, weight.shape[0])
         def _(t):
             for i in range(4):
                 weight_copy(t, i).start()
@@ -180,9 +192,11 @@
         if load:
             for i in range(4):
                 weight_copy(t, i).wait()
+        if load:
+            pl.when(t == 0)(lambda: wait_grads(0))
         total = part(t, 0)
         if load:
-            pl.when(t == 0)(other_copy.wait)
+            pl.when(t == 0)(lambda: wait_grads(1))
         total = (total + part(t, 1)).astype(jnp.bfloat16)
         at = pl.ds(pl.multiple_of((t - second * steps) * tile, tile), tile)
         for which, order in enumerate(orders):
@@ -206,33 +220,35 @@
                 weight_copy(t, i).wait()
 
 
-def expert_rows(token, own, other, weights, orders, start, columns, load):
-    rows, depth = own.shape
+def expert_rows(token, grads, weights, orders, start, columns):
+    load = len(weights) == 4
+    rows, depth = grads[0].shape[-2:]
     capacity = rows // 16
     count = 1 if orders[0][0] == orders[1][0] else 2
     out_shape = [inside(2, 8, capacity, columns)]
     scratch_shapes = []
     if load:
         tiles = weights[0].shape[0] // TILE
-        out_shape += [inside(rows, depth), inside(tiles, TILE, 2 * depth)]
-        scratch_shapes = [pltpu.SemaphoreType.DMA((tiles, 4)), pltpu.SemaphoreType.DMA]
+        out_shape += [inside(2, rows, depth), inside(tiles, TILE, 2 * depth)]
+        scratch_shapes = [pltpu.SemaphoreType.DMA((tiles, 4)), pltpu.SemaphoreType.DMA((2, 16))]
     out_shape += [inside(3 - count, 8, capacity, columns)] * count
+    arguments = [*grads, *weights]
     out = pl.pallas_call(
         functools.partial(rows_kernel, orders, start // TILE, load),
-        in_specs=[pl.BlockSpec(memory_space=pl.ANY), INSIDE] + ([HBM] * 5 if load else [INSIDE] * 2),
+        in_specs=[pl.BlockSpec(memory_space=pl.ANY)] + [HBM if load else INSIDE] * len(arguments),
         out_specs=[INSIDE] * len(out_shape),
         out_shape=out_shape,
         scratch_shapes=scratch_shapes,
-        compiler_params=params(33 if load else 10),
+        compiler_params=params(LIMITS[0] if load else LIMITS[1]),
         cost_estimate=pl.CostEstimate(
             flops=4 * rows * 2 * depth * columns,
             bytes_accessed=2 * (rows * 2 * columns + 4 * depth * columns),
             transcendentals=0,
         ),
-    )(token, own, other, *weights)
+    )(token, *arguments)
     if load:
-        return out[0], out[3:], out[1], [out[2]]
-    return out[0], out[1:], other, weights
+        return out[0], out[3:], [out[1]], [out[2]]
+    return out[0], out[1:], grads, weights
 
 
 def spread_kernel(orders, half, counts, slots, kept, *refs):
@@ -393,12 +409,10 @@
             masks = [(MASK[Y],), (MASK[Z0], MASK[Z1], MASK[Z0] + MASK[Z1]), ()][number - 1]
             state["slots"] = [last] + [send(last, mask) for mask in masks]
         elif kind == "B":
-            load = "loaded" not in state
-            kept, last, state["other"], weights = expert_rows(
-                after(state["token"], last), state["own"], state["other"], weights, orders,
-                starts[number], columns, load,
+            grads = state.get("grads") or [state["own"], state["other"]]
+            kept, last, state["grads"], weights = expert_rows(
+                after(state["token"], last), grads, weights, orders, starts[number], columns
             )
-            state["loaded"] = True
             state["rows", number] = kept, send_all(last, orders, 0)
         elif kind == "C":
             last = token_rows(after(state["slots"][0], last), orders, *state["rows", number], None)

time: 170 us -> 158 us (0.929)
  local copies, waits for them, and re-layouts: 7.72 us -> 1.74 us
  starting transfers between devices: 39.5 us -> 36.1 us
  waiting for transfers between devices: 68.1 us -> 65.3 us
    unnamed x27 -> x17, local copies, waits for them, and re-layouts: 6.99 us -> 1 us
    ppermute x38 -> x40, starting transfers between devices: 39.5 us -> 36.1 us  [send(): return lax.ppermute(value, 'expert', [(i, i ^ mask) for i in range(count)])]
    ppermute x38 -> x40, waiting for transfers between devices: 68.1 us -> 65.3 us  [send(): return lax.ppermute(value, 'expert', [(i, i ^ mask) for i in range(count)])]
  transfers between devices with their start and end apart: 38 -> 40, of which waited for: 16 -> 19; matrix products, arithmetic and copies ran while one was open for 0% -> 0% of each run, Pallas kernels for 31% -> 35%
where the time goes in v3:
time: 158 us
  waiting for transfers between devices  65.3 us (41%)
  Pallas kernels  54.7 us (35%)
  starting transfers between devices  36.1 us (23%)
  local copies, waits for them, and re-layouts  1.74 us (1%)
    ppermute x40, waiting for transfers between devices, send(): return lax.ppermute(value, 'expert', [(i, i ^ mask) for i in range(count)])  65.3 us
    pallas_call x5, Pallas kernels, expert_rows(): pl.pallas_call(functools.partial(rows_kernel, orders, start // TILE, load...  39 us
    ppermute x40, starting transfers between devices, send(): return lax.ppermute(value, 'expert', [(i, i ^ mask) for i in range(count)])  36.1 us
    pallas_call x2, Pallas kernels, swiglu(): pl.pallas_call(functools.partial(swiglu_kernel, side), in_specs=[HBM] * 3...  8.82 us
    pallas_call x10, Pallas kernels, token_rows(): pl.pallas_call(functools.partial(spread_kernel, orders, half, counts), in...  5.88 us
  transfers between devices with their start and end apart: 40, of which 19 were waited for; matrix products, arithmetic and copies ran while one was open for 0% of the time, Pallas kernels for 35%

profile of v3, /device:TPU:0, one launch (start us, length us, event | category | flops | bytes accessed | tf_op | source)
XLA Modules:
  0.0 158.2 jit_solution(12646088038747807659)
XLA Ops:
  0.5 4.4 %shard_map.64 = bf16[1536,1280]{1,0:T(8,128)(2,1)} custom-call(bf16[4,4,2,96,640]{4,3,2,1,0:T(8,128)(2,1)} %bitcast.63, bf16[4,4,2,96,640]{4,3,2,1,0:T(8,128)(2,1)} %bitcast.65, bf16[4,4,2,96,640]{4,3,2,1,0:T(8,128)(2,1)} %bitcast.67), custom_call_target="tpu_custom_call" | custom-call | flops 19660800 | bytes 9830400 | tf_op jit(solution)/shard_map/pallas_call | solution.py:118
  5.9 2.5 %collective-permute-start = (s32[1,16,128]{2,1,0:T(8,128)S(1)}, s32[1,16,128]{2,1,0:T(8,128)S(1)}, u32[]{:S(2)}, u32[]{:S(2)}) collective-permute-start(s32[1,16,128]{2,1,0:T(8,128)S(1)} %bitcast.46), channel_id=1, source_target_pairs={{0,2},{1,3},{2,0},{3,1},{4,6},{5,7},{6,4},{7,5},{8,10},{9,11},{10,... | collective-permute-start | bytes 24584 | tf_op jit(solution)/shard_map/ppermute | solution.py:34
  8.5 4.4 %shard_map.66.refs_0_ = bf16[1536,1280]{1,0:T(8,128)(2,1)} custom-call(bf16[4,4,2,96,640]{4,3,2,1,0:T(8,128)(2,1)} %bitcast.64, bf16[4,4,2,96,640]{4,3,2,1,0:T(8,128)(2,1)} %bitcast.66, bf16[4,4,2,96,640]{4,3,2,1,0:T(8,128)(2,1)} %bitcast.68), custom_call_target="tpu_custom_call" | custom-call | flops 19660800 | bytes 9830400 | tf_op jit(solution)/shard_map/pallas_call | solution.py:118
  12.9 1.6 %collective-permute-start.1 = (s32[2,16,128]{2,1,0:T(8,128)S(1)}, s32[2,16,128]{2,1,0:T(8,128)S(1)}, u32[]{:S(2)}, u32[]{:S(2)}) collective-permute-start(s32[2,16,128]{2,1,0:T(8,128)S(1)} %shard_map.67.refs_0_), channel_id=1, source_target_pairs={{0,4},{1,5},{2,6},{3,7},{4,0},{5,1},{6,2},{7,3},{8,12},{9,13},{10,... | collective-permute-start | bytes 49160 | tf_op jit(solution)/shard_map/ppermute | solution.py:34
  14.5 2.2 %collective-permute-done.1.refs_1_ = s32[2,16,128]{2,1,0:T(8,128)S(1)} collective-permute-done((s32[2,16,128]{2,1,0:T(8,128)S(1)}, s32[2,16,128]{2,1,0:T(8,128)S(1)}, u32[]{:S(2)}, u32[]{:S(2)}) %collective-permute-start.1) | collective-permute-done | bytes 16416 | tf_op jit(solution)/shard_map/ppermute | solution.py:34
  16.7 1.6 collective-permute-start.5
  18.3 2.6 %collective-permute-start.6 = (s32[4,16,128]{2,1,0:T(8,128)S(1)}, s32[4,16,128]{2,1,0:T(8,128)S(1)}, u32[]{:S(2)}, u32[]{:S(2)}) collective-permute-start(s32[4,16,128]{2,1,0:T(8,128)S(1)} %shard_map.68.refs_0_), channel_id=1, source_target_pairs={{0,16},{1,17},{2,18},{3,19},{4,20},{5,21},{6,22},{7,23},{8,24},{9,... | collective-permute-start | bytes 98312 | tf_op jit(solution)/shard_map/ppermute | solution.py:34
  20.9 4.4 %collective-permute-start.7 = (s32[4,16,128]{2,1,0:T(8,128)S(1)}, s32[4,16,128]{2,1,0:T(8,128)S(1)}, u32[]{:S(2)}, u32[]{:S(2)}) collective-permute-start(s32[4,16,128]{2,1,0:T(8,128)S(1)} %shard_map.68.refs_0_), channel_id=1, source_target_pairs={{0,24},{1,25},{2,26},{3,27},{4,28},{5,29},{6,30},{7,31},{8,16},{9,... | collective-permute-start | bytes 98312 | tf_op jit(solution)/shard_map/ppermute | solution.py:34
  25.3 14.9 %shard_map.69 = (bf16[2,8,96,512]{3,2,1,0:T(8,128)(2,1)S(1)}, bf16[2,1536,1280]{2,1,0:T(8,128)(2,1)S(1)}, bf16[14,256,2560]{2,1,0:T(8,128)(2,1)S(1)}, bf16[1,8,9...) custom-call(s32[1,16,128]{2,1,0:T(8,128)} %bitcast.48, bf16[1536,1280]{1,0:T(8,128)(2,1)} %shard_map.66.refs_0_, ...), custom_call_target="tpu_custom_call" | custom-call | flops 8053063680 | bytes 8388608 | tf_op jit(solution)/shard_map/pallas_call | solution.py:236
  40.2 1.6 collective-permute-start.8
  43.4 4.8 %shard_map.71 = (bf16[2,8,96,256]{3,2,1,0:T(8,128)(2,1)S(1)}, bf16[2,8,96,256]{3,2,1,0:T(8,128)(2,1)S(1)}) custom-call(s32[1,16,128]{2,1,0:T(8,128)S(1)} %bitcast.49, bf16[2,1536,1280]{2,1,0:T(8,128)(2,1)S(1)} %get-tuple-element.84.refs_0_, bf16[14,256,2560]{2,1,0:T(8,128)(2,1)S(1)} %get-tuple-element.85.refs_1_), custom_call_target="tpu_custom_call" | custom-call | flops 4026531840 | bytes 4194304 | tf_op jit(solution)/shard_map/pallas_call | solution.py:236
  48.1 4.8 %shard_map.72 = (bf16[2,8,96,256]{3,2,1,0:T(8,128)(2,1)S(1)}, bf16[1,8,96,256]{3,2,1,0:T(8,128)(2,1)S(1)}, bf16[1,8,96,256]{3,2,1,0:T(8,128)(2,1)S(1)}) custom-call(s32[1,16,128]{2,1,0:T(8,128)S(1)} %bitcast.50, bf16[2,1536,1280]{2,1,0:T(8,128)(2,1)S(1)} %get-tuple-element.84.refs_0_, bf16[14,256,2560]{2,1,0:T(8,128)(2,1)S(1)} %get-tuple-element.85.refs_1_), custom_call_target="tpu_custom_call" | custom-call | flops 4026531840 | bytes 4194304 | tf_op jit(solution)/shard_map/pallas_call | solution.py:236
  54.0 6.7 %collective-permute-done.8.refs_0_ = bf16[1,8,96,512]{3,2,1,0:T(8,128)(2,1)S(1)} collective-permute-done((bf16[1,8,96,512]{3,2,1,0:T(8,128)(2,1)S(1)}, bf16[1,8,96,512]{3,2,1,0:T(8,128)(2,1)S(1)}, u32[]{:S(2)}, u32[]{:S(2)}) %collective-permute-start.8) | collective-permute-done | bytes 786464 | tf_op jit(solution)/shard_map/ppermute | solution.py:34
  60.7 1.5 collective-permute-done.9.refs_1_
  63.0 1.6 %collective-permute-start.13 = (bf16[1,4,128,512]{3,2,1,0:T(8,128)(2,1)S(1)}, bf16[1,4,128,512]{3,2,1,0:T(8,128)(2,1)S(1)}, u32[]{:S(2)}, u32[]{:S(2)}) collective-permute-start(bf16[1,4,128,512]{3,2,1,0:T(8,128)(2,1)S(1)} %get-tuple-element.92), channel_id=1, source_target_pairs={{0,4},{1,5},{2,6},{3,7},{4,0},{5,1},{6,2},{7,3},{8,12},{9,13},{10,... | collective-permute-start | bytes 1572872 | tf_op jit(solution)/shard_map/ppermute | solution.py:34
  65.1 9.8 %shard_map.74 = (bf16[2,8,96,512]{3,2,1,0:T(8,128)(2,1)S(1)}, bf16[1,8,96,512]{3,2,1,0:T(8,128)(2,1)S(1)}, bf16[1,8,96,512]{3,2,1,0:T(8,128)(2,1)S(1)}) custom-call(s32[1,16,128]{2,1,0:T(8,128)S(1)} %bitcast.51, bf16[2,1536,1280]{2,1,0:T(8,128)(2,1)S(1)} %get-tuple-element.84.refs_0_, bf16[14,256,2560]{2,1,0:T(8,128)(2,1)S(1)} %get-tuple-element.85.refs_1_), custom_call_target="tpu_custom_call" | custom-call | flops 8053063680 | bytes 8388608 | tf_op jit(solution)/shard_map/pallas_call | solution.py:236
  74.9 1.6 collective-permute-start.16
  78.0 3.9 %collective-permute-done.13.refs_2_ = bf16[1,4,128,512]{3,2,1,0:T(8,128)(2,1)S(1)} collective-permute-done((bf16[1,4,128,512]{3,2,1,0:T(8,128)(2,1)S(1)}, bf16[1,4,128,512]{3,2,1,0:T(8,128)(2,1)S(1)}, u32[]{:S(2)}, u32[]{:S(2)}) %collective-permute-start.13) | collective-permute-done | bytes 524320 | tf_op jit(solution)/shard_map/ppermute | solution.py:34
  82.8 12.4 %collective-permute-done.15.refs_2_ = bf16[2,4,128,256]{3,2,1,0:T(8,128)(2,1)S(1)} collective-permute-done((bf16[2,4,128,256]{3,2,1,0:T(8,128)(2,1)S(1)}, bf16[2,4,128,256]{3,2,1,0:T(8,128)(2,1)S(1)}, u32[]{:S(2)}, u32[]{:S(2)}) %collective-permute-start.15) | collective-permute-done | bytes 524320 | tf_op jit(solution)/shard_map/ppermute | solution.py:34
  98.1 1.6 %collective-permute-start.20 = (bf16[1,4,128,512]{3,2,1,0:T(8,128)(2,1)S(1)}, bf16[1,4,128,512]{3,2,1,0:T(8,128)(2,1)S(1)}, u32[]{:S(2)}, u32[]{:S(2)}) collective-permute-start(bf16[1,4,128,512]{3,2,1,0:T(8,128)(2,1)S(1)} %get-tuple-element.111), channel_id=1, source_target_pairs={{0,4},{1,5},{2,6},{3,7},{4,0},{5,1},{6,2},{7,3},{8,12},{9,13},{10,... | collective-permute-start | bytes 1572872 | tf_op jit(solution)/shard_map/ppermute | solution.py:34
  100.2 1.7 %collective-permute-done.18.refs_0_ = bf16[2,2,128,512]{3,2,1,0:T(8,128)(2,1)S(1)} collective-permute-done((bf16[2,2,128,512]{3,2,1,0:T(8,128)(2,1)S(1)}, bf16[2,2,128,512]{3,2,1,0:T(8,128)(2,1)S(1)}, u32[]{:S(2)}, u32[]{:S(2)}) %collective-permute-start.18) | collective-permute-done | bytes 524320 | tf_op jit(solution)/shard_map/ppermute | solution.py:34
  101.9 3.8 %collective-permute-done.19.refs_0_ = bf16[2,2,128,256]{3,2,1,0:T(8,128)(2,1)S(1)} collective-permute-done((bf16[2,2,128,256]{3,2,1,0:T(8,128)(2,1)S(1)}, bf16[2,2,128,256]{3,2,1,0:T(8,128)(2,1)S(1)}, u32[]{:S(2)}, u32[]{:S(2)}) %collective-permute-start.19) | collective-permute-done | bytes 262176 | tf_op jit(solution)/shard_map/ppermute | solution.py:34
  105.8 4.8 %shard_map.82 = (bf16[2,8,96,256]{3,2,1,0:T(8,128)(2,1)S(1)}, bf16[1,8,96,256]{3,2,1,0:T(8,128)(2,1)S(1)}, bf16[1,8,96,256]{3,2,1,0:T(8,128)(2,1)S(1)}) custom-call(s32[1,16,128]{2,1,0:T(8,128)S(1)} %bitcast.54, bf16[2,1536,1280]{2,1,0:T(8,128)(2,1)S(1)} %get-tuple-element.84.refs_0_, bf16[14,256,2560]{2,1,0:T(8,128)(2,1)S(1)} %get-tuple-element.85.refs_1_), custom_call_target="tpu_custom_call" | custom-call | flops 4026531840 | bytes 4194304 | tf_op jit(solution)/shard_map/pallas_call | solution.py:236
  113.0 1.5 collective-permute-done.21.refs_3_
  116.6 11.3 %collective-permute-done.22.refs_1_ = bf16[2,128,512]{2,1,0:T(8,128)(2,1)S(1)} collective-permute-done((bf16[2,128,512]{2,1,0:T(8,128)(2,1)S(1)}, bf16[2,128,512]{2,1,0:T(8,128)(2,1)S(1)}, u32[]{:S(2)}, u32[]{:S(2)}) %collective-permute-start.22) | collective-permute-done | bytes 262176 | tf_op jit(solution)/shard_map/ppermute | solution.py:34
  133.3 3.0 %collective-permute-done.27.refs_1_ = bf16[1,4,128,256]{3,2,1,0:T(8,128)(2,1)S(1)} collective-permute-done((bf16[1,4,128,256]{3,2,1,0:T(8,128)(2,1)S(1)}, bf16[1,4,128,256]{3,2,1,0:T(8,128)(2,1)S(1)}, u32[]{:S(2)}, u32[]{:S(2)}) %collective-permute-start.27) | collective-permute-done | bytes 262176 | tf_op jit(solution)/shard_map/ppermute | solution.py:34
  136.8 1.6 %collective-permute-start.32 = (bf16[1,2,128,256]{3,2,1,0:T(8,128)(2,1)S(1)}, bf16[1,2,128,256]{3,2,1,0:T(8,128)(2,1)S(1)}, u32[]{:S(2)}, u32[]{:S(2)}) collective-permute-start(bf16[1,2,128,256]{3,2,1,0:T(8,128)(2,1)S(1)} %get-tuple-element.135), channel_id=1, source_target_pairs={{0,2},{1,3},{2,0},{3,1},{4,6},{5,7},{6,4},{7,5},{8,10},{9,11},{10,... | collective-permute-start | bytes 393224 | tf_op jit(solution)/shard_map/ppermute | solution.py:34
  139.9 1.9 %collective-permute-done.31.refs_0_ = bf16[1,2,128,256]{3,2,1,0:T(8,128)(2,1)S(1)} collective-permute-done((bf16[1,2,128,256]{3,2,1,0:T(8,128)(2,1)S(1)}, bf16[1,2,128,256]{3,2,1,0:T(8,128)(2,1)S(1)}, u32[]{:S(2)}, u32[]{:S(2)}) %collective-permute-start.31) | collective-permute-done | bytes 131104 | tf_op jit(solution)/shard_map/ppermute | solution.py:34
  143.2 4.0 %collective-permute-done.33.refs_2_ = bf16[1,128,512]{2,1,0:T(8,128)(2,1)S(1)} collective-permute-done((bf16[1,128,512]{2,1,0:T(8,128)(2,1)S(1)}, bf16[1,128,512]{2,1,0:T(8,128)(2,1)S(1)}, u32[]{:S(2)}, u32[]{:S(2)}) %collective-permute-start.33) | collective-permute-done | bytes 131104 | tf_op jit(solution)/shard_map/ppermute | solution.py:34
  147.2 2.9 %collective-permute-done.34.refs_3_ = bf16[1,128,512]{2,1,0:T(8,128)(2,1)S(1)} collective-permute-done((bf16[1,128,512]{2,1,0:T(8,128)(2,1)S(1)}, bf16[1,128,512]{2,1,0:T(8,128)(2,1)S(1)}, u32[]{:S(2)}, u32[]{:S(2)}) %collective-permute-start.34) | collective-permute-done | bytes 131104 | tf_op jit(solution)/shard_map/ppermute | solution.py:34
  150.4 2.7 %collective-permute-done.36.refs_2_ = bf16[2,128,256]{2,1,0:T(8,128)(2,1)S(1)} collective-permute-done((bf16[2,128,256]{2,1,0:T(8,128)(2,1)S(1)}, bf16[2,128,256]{2,1,0:T(8,128)(2,1)S(1)}, u32[]{:S(2)}, u32[]{:S(2)}) %collective-permute-start.36) | collective-permute-done | bytes 131104 | tf_op jit(solution)/shard_map/ppermute | solution.py:34
  153.3 3.3 %collective-permute-done.39.refs_1_ = bf16[2,128,256]{2,1,0:T(8,128)(2,1)S(1)} collective-permute-done((bf16[2,128,256]{2,1,0:T(8,128)(2,1)S(1)}, bf16[2,128,256]{2,1,0:T(8,128)(2,1)S(1)}, u32[]{:S(2)}, u32[]{:S(2)}) %collective-permute-start.39) | collective-permute-done | bytes 131104 | tf_op jit(solution)/shard_map/ppermute | solution.py:34
  (98 shorter events, 26.7 us)
Async XLA Ops:
  0.0 25.3 %collective-permute-start.3 = (bf16[3584,640]{1,0:T(8,128)(2,1)}, bf16[3584,640]{1,0:T(8,128)(2,1)}, u32[]{:S(2)}, u32[]{:S(2)}) collective-permute-start(bf16[3584,640]{1,0:T(8,128)(2,1)} %bitcast.69), channel_id=1, source_target_pairs={{0,1},{1,0},{2,3},{3,2},{4,5},{5,4},{6,7},{7,6},{8,9},{9,8},{10,11... | collective-permute-start | bytes 13762568 | tf_op jit(solution)/shard_map/ppermute | solution.py:34
  0.5 24.9 %collective-permute-start.4 = (bf16[3584,640]{1,0:T(8,128)(2,1)}, bf16[3584,640]{1,0:T(8,128)(2,1)}, u32[]{:S(2)}, u32[]{:S(2)}) collective-permute-start(bf16[3584,640]{1,0:T(8,128)(2,1)} %bitcast.71), channel_id=1, source_target_pairs={{0,1},{1,0},{2,3},{3,2},{4,5},{5,4},{6,7},{7,6},{8,9},{9,8},{10,11... | collective-permute-start | bytes 13762568 | tf_op jit(solution)/shard_map/ppermute | solution.py:34
  4.9 16.0 %collective-permute-start.2 = (bf16[1536,1280]{1,0:T(8,128)(2,1)}, bf16[1536,1280]{1,0:T(8,128)(2,1)}, u32[]{:S(2)}, u32[]{:S(2)}) collective-permute-start(bf16[1536,1280]{1,0:T(8,128)(2,1)} %shard_map.64), channel_id=1, source_target_pairs={{0,1},{1,0},{2,3},{3,2},{4,5},{5,4},{6,7},{7,6},{8,9},{9,8},{10,11... | collective-permute-start | bytes 11796488 | tf_op jit(solution)/shard_map/ppermute | solution.py:34
  16.7 26.6 %collective-permute-start.5 = (s32[4,16,128]{2,1,0:T(8,128)S(1)}, s32[4,16,128]{2,1,0:T(8,128)S(1)}, u32[]{:S(2)}, u32[]{:S(2)}) collective-permute-start(s32[4,16,128]{2,1,0:T(8,128)S(1)} %shard_map.68.refs_0_), channel_id=1, source_target_pairs={{0,8},{1,9},{2,10},{3,11},{4,12},{5,13},{6,14},{7,15},{8,0},{9,1},... | collective-permute-start | bytes 98312 | tf_op jit(solution)/shard_map/ppermute | solution.py:34
  18.3 25.0 %collective-permute-start.6 = (s32[4,16,128]{2,1,0:T(8,128)S(1)}, s32[4,16,128]{2,1,0:T(8,128)S(1)}, u32[]{:S(2)}, u32[]{:S(2)}) collective-permute-start(s32[4,16,128]{2,1,0:T(8,128)S(1)} %shard_map.68.refs_0_), channel_id=1, source_target_pairs={{0,16},{1,17},{2,18},{3,19},{4,20},{5,21},{6,22},{7,23},{8,24},{9,... | collective-permute-start | bytes 98312 | tf_op jit(solution)/shard_map/ppermute | solution.py:34
  20.9 22.4 %collective-permute-start.7 = (s32[4,16,128]{2,1,0:T(8,128)S(1)}, s32[4,16,128]{2,1,0:T(8,128)S(1)}, u32[]{:S(2)}, u32[]{:S(2)}) collective-permute-start(s32[4,16,128]{2,1,0:T(8,128)S(1)} %shard_map.68.refs_0_), channel_id=1, source_target_pairs={{0,24},{1,25},{2,26},{3,27},{4,28},{5,29},{6,30},{7,31},{8,16},{9,... | collective-permute-start | bytes 98312 | tf_op jit(solution)/shard_map/ppermute | solution.py:34
  40.2 20.5 %collective-permute-start.8 = (bf16[1,8,96,512]{3,2,1,0:T(8,128)(2,1)S(1)}, bf16[1,8,96,512]{3,2,1,0:T(8,128)(2,1)S(1)}, u32[]{:S(2)}, u32[]{:S(2)}) collective-permute-start(bf16[1,8,96,512]{3,2,1,0:T(8,128)(2,1)S(1)} %get-tuple-element.80), channel_id=1, source_target_pairs={{0,2},{1,3},{2,0},{3,1},{4,6},{5,7},{6,4},{7,5},{8,10},{9,11},{10,... | collective-permute-start | bytes 2359304 | tf_op jit(solution)/shard_map/ppermute | solution.py:34
  41.8 20.5 %collective-permute-start.9 = (bf16[1,8,96,512]{3,2,1,0:T(8,128)(2,1)S(1)}, bf16[1,8,96,512]{3,2,1,0:T(8,128)(2,1)S(1)}, u32[]{:S(2)}, u32[]{:S(2)}) collective-permute-start(bf16[1,8,96,512]{3,2,1,0:T(8,128)(2,1)S(1)} %get-tuple-element.81), channel_id=1, source_target_pairs={{0,4},{1,5},{2,6},{3,7},{4,0},{5,1},{6,2},{7,3},{8,12},{9,13},{10,... | collective-permute-start | bytes 2359304 | tf_op jit(solution)/shard_map/ppermute | solution.py:34
  52.9 22.0 %collective-permute-start.10 = (bf16[1,8,96,256]{3,2,1,0:T(8,128)(2,1)S(1)}, bf16[1,8,96,256]{3,2,1,0:T(8,128)(2,1)S(1)}, u32[]{:S(2)}, u32[]{:S(2)}) collective-permute-start(bf16[1,8,96,256]{3,2,1,0:T(8,128)(2,1)S(1)} %get-tuple-element.88), channel_id=1, source_target_pairs={{0,2},{1,3},{2,0},{3,1},{4,6},{5,7},{6,4},{7,5},{8,10},{9,11},{10,... | collective-permute-start | bytes 1179656 | tf_op jit(solution)/shard_map/ppermute | solution.py:34
  53.5 22.9 %collective-permute-start.11 = (bf16[1,8,96,256]{3,2,1,0:T(8,128)(2,1)S(1)}, bf16[1,8,96,256]{3,2,1,0:T(8,128)(2,1)S(1)}, u32[]{:S(2)}, u32[]{:S(2)}) collective-permute-start(bf16[1,8,96,256]{3,2,1,0:T(8,128)(2,1)S(1)} %get-tuple-element.89), channel_id=1, source_target_pairs={{0,4},{1,5},{2,6},{3,7},{4,0},{5,1},{6,2},{7,3},{8,12},{9,13},{10,... | collective-permute-start | bytes 1179656 | tf_op jit(solution)/shard_map/ppermute | solution.py:34
  54.0 23.4 %collective-permute-start.12 = (bf16[2,8,96,256]{3,2,1,0:T(8,128)(2,1)S(1)}, bf16[2,8,96,256]{3,2,1,0:T(8,128)(2,1)S(1)}, u32[]{:S(2)}, u32[]{:S(2)}) collective-permute-start(bf16[2,8,96,256]{3,2,1,0:T(8,128)(2,1)S(1)} %get-tuple-element.86), channel_id=1, source_target_pairs={{0,8},{1,9},{2,10},{3,11},{4,12},{5,13},{6,14},{7,15},{8,0},{9,1},... | collective-permute-start | bytes 2359304 | tf_op jit(solution)/shard_map/ppermute | solution.py:34
  63.0 18.9 %collective-permute-start.13 = (bf16[1,4,128,512]{3,2,1,0:T(8,128)(2,1)S(1)}, bf16[1,4,128,512]{3,2,1,0:T(8,128)(2,1)S(1)}, u32[]{:S(2)}, u32[]{:S(2)}) collective-permute-start(bf16[1,4,128,512]{3,2,1,0:T(8,128)(2,1)S(1)} %get-tuple-element.92), channel_id=1, source_target_pairs={{0,4},{1,5},{2,6},{3,7},{4,0},{5,1},{6,2},{7,3},{8,12},{9,13},{10,... | collective-permute-start | bytes 1572872 | tf_op jit(solution)/shard_map/ppermute | solution.py:34
  64.6 17.3 %collective-permute-start.14 = (bf16[1,4,128,512]{3,2,1,0:T(8,128)(2,1)S(1)}, bf16[1,4,128,512]{3,2,1,0:T(8,128)(2,1)S(1)}, u32[]{:S(2)}, u32[]{:S(2)}) collective-permute-start(bf16[1,4,128,512]{3,2,1,0:T(8,128)(2,1)S(1)} %get-tuple-element.93), channel_id=1, source_target_pairs={{0,2},{1,3},{2,0},{3,1},{4,6},{5,7},{6,4},{7,5},{8,10},{9,11},{10,... | collective-permute-start | bytes 1572872 | tf_op jit(solution)/shard_map/ppermute | solution.py:34
  74.9 21.2 %collective-permute-start.16 = (bf16[1,8,96,512]{3,2,1,0:T(8,128)(2,1)S(1)}, bf16[1,8,96,512]{3,2,1,0:T(8,128)(2,1)S(1)}, u32[]{:S(2)}, u32[]{:S(2)}) collective-permute-start(bf16[1,8,96,512]{3,2,1,0:T(8,128)(2,1)S(1)} %get-tuple-element.95), channel_id=1, source_target_pairs={{0,2},{1,3},{2,0},{3,1},{4,6},{5,7},{6,4},{7,5},{8,10},{9,11},{10,... | collective-permute-start | bytes 2359304 | tf_op jit(solution)/shard_map/ppermute | solution.py:34
  76.5 20.9 %collective-permute-start.17 = (bf16[1,8,96,512]{3,2,1,0:T(8,128)(2,1)S(1)}, bf16[1,8,96,512]{3,2,1,0:T(8,128)(2,1)S(1)}, u32[]{:S(2)}, u32[]{:S(2)}) collective-permute-start(bf16[1,8,96,512]{3,2,1,0:T(8,128)(2,1)S(1)} %get-tuple-element.96), channel_id=1, source_target_pairs={{0,4},{1,5},{2,6},{3,7},{4,0},{5,1},{6,2},{7,3},{8,12},{9,13},{10,... | collective-permute-start | bytes 2359304 | tf_op jit(solution)/shard_map/ppermute | solution.py:34
  77.5 17.6 %collective-permute-start.15 = (bf16[2,4,128,256]{3,2,1,0:T(8,128)(2,1)S(1)}, bf16[2,4,128,256]{3,2,1,0:T(8,128)(2,1)S(1)}, u32[]{:S(2)}, u32[]{:S(2)}) collective-permute-start(bf16[2,4,128,256]{3,2,1,0:T(8,128)(2,1)S(1)} %shard_map.75), channel_id=1, source_target_pairs={{0,8},{1,9},{2,10},{3,11},{4,12},{5,13},{6,14},{7,15},{8,0},{9,1},... | collective-permute-start | bytes 1572872 | tf_op jit(solution)/shard_map/ppermute | solution.py:34
  82.7 19.2 %collective-permute-start.18 = (bf16[2,2,128,512]{3,2,1,0:T(8,128)(2,1)S(1)}, bf16[2,2,128,512]{3,2,1,0:T(8,128)(2,1)S(1)}, u32[]{:S(2)}, u32[]{:S(2)}) collective-permute-start(bf16[2,2,128,512]{3,2,1,0:T(8,128)(2,1)S(1)} %get-tuple-element.105), channel_id=1, source_target_pairs={{0,8},{1,9},{2,10},{3,11},{4,12},{5,13},{6,14},{7,15},{8,0},{9,1},... | collective-permute-start | bytes 1572872 | tf_op jit(solution)/shard_map/ppermute | solution.py:34
  95.6 10.1 %collective-permute-start.19 = (bf16[2,2,128,256]{3,2,1,0:T(8,128)(2,1)S(1)}, bf16[2,2,128,256]{3,2,1,0:T(8,128)(2,1)S(1)}, u32[]{:S(2)}, u32[]{:S(2)}) collective-permute-start(bf16[2,2,128,256]{3,2,1,0:T(8,128)(2,1)S(1)} %get-tuple-element.108), channel_id=1, source_target_pairs={{0,16},{1,17},{2,18},{3,19},{4,20},{5,21},{6,22},{7,23},{8,24},{9,... | collective-permute-start | bytes 786440 | tf_op jit(solution)/shard_map/ppermute | solution.py:34
  98.1 14.9 %collective-permute-start.20 = (bf16[1,4,128,512]{3,2,1,0:T(8,128)(2,1)S(1)}, bf16[1,4,128,512]{3,2,1,0:T(8,128)(2,1)S(1)}, u32[]{:S(2)}, u32[]{:S(2)}) collective-permute-start(bf16[1,4,128,512]{3,2,1,0:T(8,128)(2,1)S(1)} %get-tuple-element.111), channel_id=1, source_target_pairs={{0,4},{1,5},{2,6},{3,7},{4,0},{5,1},{6,2},{7,3},{8,12},{9,13},{10,... | collective-permute-start | bytes 1572872 | tf_op jit(solution)/shard_map/ppermute | solution.py:34
  99.7 14.9 %collective-permute-start.21 = (bf16[1,4,128,512]{3,2,1,0:T(8,128)(2,1)S(1)}, bf16[1,4,128,512]{3,2,1,0:T(8,128)(2,1)S(1)}, u32[]{:S(2)}, u32[]{:S(2)}) collective-permute-start(bf16[1,4,128,512]{3,2,1,0:T(8,128)(2,1)S(1)} %get-tuple-element.112), channel_id=1, source_target_pairs={{0,2},{1,3},{2,0},{3,1},{4,6},{5,7},{6,4},{7,5},{8,10},{9,11},{10,... | collective-permute-start | bytes 1572872 | tf_op jit(solution)/shard_map/ppermute | solution.py:34
  110.6 18.6 %collective-permute-start.23 = (bf16[1,8,96,256]{3,2,1,0:T(8,128)(2,1)S(1)}, bf16[1,8,96,256]{3,2,1,0:T(8,128)(2,1)S(1)}, u32[]{:S(2)}, u32[]{:S(2)}) collective-permute-start(bf16[1,8,96,256]{3,2,1,0:T(8,128)(2,1)S(1)} %get-tuple-element.118), channel_id=1, source_target_pairs={{0,2},{1,3},{2,0},{3,1},{4,6},{5,7},{6,4},{7,5},{8,10},{9,11},{10,... | collective-permute-start | bytes 1179656 | tf_op jit(solution)/shard_map/ppermute | solution.py:34
  111.3 18.6 %collective-permute-start.24 = (bf16[1,8,96,256]{3,2,1,0:T(8,128)(2,1)S(1)}, bf16[1,8,96,256]{3,2,1,0:T(8,128)(2,1)S(1)}, u32[]{:S(2)}, u32[]{:S(2)}) collective-permute-start(bf16[1,8,96,256]{3,2,1,0:T(8,128)(2,1)S(1)} %get-tuple-element.119), channel_id=1, source_target_pairs={{0,4},{1,5},{2,6},{3,7},{4,0},{5,1},{6,2},{7,3},{8,12},{9,13},{10,... | collective-permute-start | bytes 1179656 | tf_op jit(solution)/shard_map/ppermute | solution.py:34
  112.8 15.1 %collective-permute-start.22 = (bf16[2,128,512]{2,1,0:T(8,128)(2,1)S(1)}, bf16[2,128,512]{2,1,0:T(8,128)(2,1)S(1)}, u32[]{:S(2)}, u32[]{:S(2)}) collective-permute-start(bf16[2,128,512]{2,1,0:T(8,128)(2,1)S(1)} %shard_map.80), channel_id=1, source_target_pairs={{0,16},{1,17},{2,18},{3,19},{4,20},{5,21},{6,22},{7,23},{8,24},{9,... | collective-permute-start | bytes 786440 | tf_op jit(solution)/shard_map/ppermute | solution.py:34
  115.3 16.6 %collective-permute-start.25 = (bf16[1,2,128,512]{3,2,1,0:T(8,128)(2,1)S(1)}, bf16[1,2,128,512]{3,2,1,0:T(8,128)(2,1)S(1)}, u32[]{:S(2)}, u32[]{:S(2)}) collective-permute-start(bf16[1,2,128,512]{3,2,1,0:T(8,128)(2,1)S(1)} %get-tuple-element.122), channel_id=1, source_target_pairs={{0,8},{1,9},{2,10},{3,11},{4,12},{5,13},{6,14},{7,15},{8,0},{9,1},... | collective-permute-start | bytes 786440 | tf_op jit(solution)/shard_map/ppermute | solution.py:34
  115.4 17.3 %collective-permute-start.26 = (bf16[1,2,128,512]{3,2,1,0:T(8,128)(2,1)S(1)}, bf16[1,2,128,512]{3,2,1,0:T(8,128)(2,1)S(1)}, u32[]{:S(2)}, u32[]{:S(2)}) collective-permute-start(bf16[1,2,128,512]{3,2,1,0:T(8,128)(2,1)S(1)} %get-tuple-element.123), channel_id=1, source_target_pairs={{0,16},{1,17},{2,18},{3,19},{4,20},{5,21},{6,22},{7,23},{8,24},{9,... | collective-permute-start | bytes 786440 | tf_op jit(solution)/shard_map/ppermute | solution.py:34
  127.9 8.4 %collective-permute-start.27 = (bf16[1,4,128,256]{3,2,1,0:T(8,128)(2,1)S(1)}, bf16[1,4,128,256]{3,2,1,0:T(8,128)(2,1)S(1)}, u32[]{:S(2)}, u32[]{:S(2)}) collective-permute-start(bf16[1,4,128,256]{3,2,1,0:T(8,128)(2,1)S(1)} %get-tuple-element.101), channel_id=1, source_target_pairs={{0,2},{1,3},{2,0},{3,1},{4,6},{5,7},{6,4},{7,5},{8,10},{9,11},{10,... | collective-permute-start | bytes 786440 | tf_op jit(solution)/shard_map/ppermute | solution.py:34
  130.4 8.0 %collective-permute-start.29 = (bf16[1,4,128,256]{3,2,1,0:T(8,128)(2,1)S(1)}, bf16[1,4,128,256]{3,2,1,0:T(8,128)(2,1)S(1)}, u32[]{:S(2)}, u32[]{:S(2)}) collective-permute-start(bf16[1,4,128,256]{3,2,1,0:T(8,128)(2,1)S(1)} %get-tuple-element.127), channel_id=1, source_target_pairs={{0,4},{1,5},{2,6},{3,7},{4,0},{5,1},{6,2},{7,3},{8,12},{9,13},{10,... | collective-permute-start | bytes 786440 | tf_op jit(solution)/shard_map/ppermute | solution.py:34
  132.6 20.5 %collective-permute-start.37 = (bf16[1,128,256]{2,1,0:T(8,128)(2,1)S(1)}, bf16[1,128,256]{2,1,0:T(8,128)(2,1)S(1)}, u32[]{:S(2)}, u32[]{:S(2)}) collective-permute-start(bf16[1,128,256]{2,1,0:T(8,128)(2,1)S(1)} %get-tuple-element.115), channel_id=1, source_target_pairs={{0,4},{1,5},{2,6},{3,7},{4,0},{5,1},{6,2},{7,3},{8,12},{9,13},{10,... | collective-permute-start | bytes 196616 | tf_op jit(solution)/shard_map/ppermute | solution.py:34
  138.5 8.8 %collective-permute-start.33 = (bf16[1,128,512]{2,1,0:T(8,128)(2,1)S(1)}, bf16[1,128,512]{2,1,0:T(8,128)(2,1)S(1)}, u32[]{:S(2)}, u32[]{:S(2)}) collective-permute-start(bf16[1,128,512]{2,1,0:T(8,128)(2,1)S(1)} %get-tuple-element.130), channel_id=1, source_target_pairs={{0,16},{1,17},{2,18},{3,19},{4,20},{5,21},{6,22},{7,23},{8,24},{9,... | collective-permute-start | bytes 393224 | tf_op jit(solution)/shard_map/ppermute | solution.py:34
  139.7 10.6 %collective-permute-start.35 = (bf16[2,2,128,256]{3,2,1,0:T(8,128)(2,1)S(1)}, bf16[2,2,128,256]{3,2,1,0:T(8,128)(2,1)S(1)}, u32[]{:S(2)}, u32[]{:S(2)}) collective-permute-start(bf16[2,2,128,256]{3,2,1,0:T(8,128)(2,1)S(1)} %get-tuple-element.138), channel_id=1, source_target_pairs={{0,8},{1,9},{2,10},{3,11},{4,12},{5,13},{6,14},{7,15},{8,0},{9,1},... | collective-permute-start | bytes 786440 | tf_op jit(solution)/shard_map/ppermute | solution.py:34
  141.8 11.4 %collective-permute-start.38 = (bf16[1,128,256]{2,1,0:T(8,128)(2,1)S(1)}, bf16[1,128,256]{2,1,0:T(8,128)(2,1)S(1)}, u32[]{:S(2)}, u32[]{:S(2)}) collective-permute-start(bf16[1,128,256]{2,1,0:T(8,128)(2,1)S(1)} %get-tuple-element.116), channel_id=1, source_target_pairs={{0,2},{1,3},{2,0},{3,1},{4,6},{5,7},{6,4},{7,5},{8,10},{9,11},{10,... | collective-permute-start | bytes 196616 | tf_op jit(solution)/shard_map/ppermute | solution.py:34
  142.7 7.5 %collective-permute-start.34 = (bf16[1,128,512]{2,1,0:T(8,128)(2,1)S(1)}, bf16[1,128,512]{2,1,0:T(8,128)(2,1)S(1)}, u32[]{:S(2)}, u32[]{:S(2)}) collective-permute-start(bf16[1,128,512]{2,1,0:T(8,128)(2,1)S(1)} %get-tuple-element.131), channel_id=1, source_target_pairs={{0,8},{1,9},{2,10},{3,11},{4,12},{5,13},{6,14},{7,15},{8,0},{9,1},... | collective-permute-start | bytes 393224 | tf_op jit(solution)/shard_map/ppermute | solution.py:34
  (12 other events, 87.6 us)

commit v4 on v3

--- a/solution.py
+++ b/solution.py
@@ -16,9 +16,9 @@
 BZ = (Z0, X, Z1, Y), (Z0, Y, Z1, X)
 D = (X, Z0, Y, Z1), (Y, Z0, X, Z1)
 E = (X, Z0, Z1, Y), (Y, Z0, Z1, X)
-WAVES = ((AH, 512), (BH, 256), (E, 256), (AM, 512), (AH, 256))
+WAVES = ((AH, 512), (BH, 256), (E, 256), (AM, 512), (AM, 256))
 SCHEDULE = (
-    *("A0", "S0", "A1", "S1", "S2", "B0", "S3", "B1", "B2", "C0", "B3", "C2", "C1", "D0", "D2", "C3"),
+    *("A0", "S0", "A1", "S1", "S2", "B0", "B1", "S3", "B2", "C0", "B3", "C2", "C1", "D0", "D2", "C3"),
     *("E0", "E2", "B4", "D3", "F0", "C4", "E3", "D1", "D4", "E1", "F3", "E4", "F1", "F2", "F4"),
 )
 TILE = 256

time: 158 us -> 156 us (0.987)
  waiting for transfers between devices: 65.3 us -> 45 us
  starting transfers between devices: 36.1 us -> 53.9 us
    ppermute x40 -> x42, waiting for transfers between devices: 65.3 us -> 45 us  [send(): return lax.ppermute(value, 'expert', [(i, i ^ mask) for i in range(count)])]
    ppermute x40 -> x42, starting transfers between devices: 36.1 us -> 53.9 us  [send(): return lax.ppermute(value, 'expert', [(i, i ^ mask) for i in range(count)])]
  transfers between devices with their start and end apart: 40 -> 42, of which waited for: 19 -> 16; matrix products, arithmetic and copies ran while one was open for 0% -> 0% of each run, Pallas kernels for 35% -> 26%
where the time goes in v4:
time: 156 us
  Pallas kernels  54.7 us (35%)
  starting transfers between devices  53.9 us (35%)
  waiting for transfers between devices  45 us (29%)
  local copies, waits for them, and re-layouts  1.74 us (1%)
    ppermute x42, starting transfers between devices, send(): return lax.ppermute(value, 'expert', [(i, i ^ mask) for i in range(count)])  53.9 us
    ppermute x42, waiting for transfers between devices, send(): return lax.ppermute(value, 'expert', [(i, i ^ mask) for i in range(count)])  45 us
    pallas_call x5, Pallas kernels, expert_rows(): pl.pallas_call(functools.partial(rows_kernel, orders, start // TILE, load...  39 us
    pallas_call x2, Pallas kernels, swiglu(): pl.pallas_call(functools.partial(swiglu_kernel, side), in_specs=[HBM] * 3...  8.81 us
    pallas_call x10, Pallas kernels, token_rows(): pl.pallas_call(functools.partial(spread_kernel, orders, half, counts), in...  5.89 us
  transfers between devices with their start and end apart: 42, of which 16 were waited for; matrix products, arithmetic and copies ran while one was open for 0% of the time, Pallas kernels for 26%

profile of v4, /device:TPU:0, one launch (start us, length us, event | category | flops | bytes accessed | tf_op | source)
XLA Modules:
  0.0 155.8 jit_solution(3276194500495632353)
XLA Ops:
  0.5 4.4 %shard_map.64 = bf16[1536,1280]{1,0:T(8,128)(2,1)} custom-call(bf16[4,4,2,96,640]{4,3,2,1,0:T(8,128)(2,1)} %bitcast.63, bf16[4,4,2,96,640]{4,3,2,1,0:T(8,128)(2,1)} %bitcast.65, bf16[4,4,2,96,640]{4,3,2,1,0:T(8,128)(2,1)} %bitcast.67), custom_call_target="tpu_custom_call" | custom-call | flops 19660800 | bytes 9830400 | tf_op jit(solution)/shard_map/pallas_call | solution.py:118
  6.0 2.5 %collective-permute-start = (s32[1,16,128]{2,1,0:T(8,128)S(1)}, s32[1,16,128]{2,1,0:T(8,128)S(1)}, u32[]{:S(2)}, u32[]{:S(2)}) collective-permute-start(s32[1,16,128]{2,1,0:T(8,128)S(1)} %bitcast.46), channel_id=1, source_target_pairs={{0,2},{1,3},{2,0},{3,1},{4,6},{5,7},{6,4},{7,5},{8,10},{9,11},{10,... | collective-permute-start | bytes 24584 | tf_op jit(solution)/shard_map/ppermute | solution.py:34
  8.5 4.4 %shard_map.66.refs_0_ = bf16[1536,1280]{1,0:T(8,128)(2,1)} custom-call(bf16[4,4,2,96,640]{4,3,2,1,0:T(8,128)(2,1)} %bitcast.64, bf16[4,4,2,96,640]{4,3,2,1,0:T(8,128)(2,1)} %bitcast.66, bf16[4,4,2,96,640]{4,3,2,1,0:T(8,128)(2,1)} %bitcast.68), custom_call_target="tpu_custom_call" | custom-call | flops 19660800 | bytes 9830400 | tf_op jit(solution)/shard_map/pallas_call | solution.py:118
  12.9 1.6 %collective-permute-start.1 = (s32[2,16,128]{2,1,0:T(8,128)S(1)}, s32[2,16,128]{2,1,0:T(8,128)S(1)}, u32[]{:S(2)}, u32[]{:S(2)}) collective-permute-start(s32[2,16,128]{2,1,0:T(8,128)S(1)} %shard_map.67.refs_0_), channel_id=1, source_target_pairs={{0,4},{1,5},{2,6},{3,7},{4,0},{5,1},{6,2},{7,3},{8,12},{9,13},{10,... | collective-permute-start | bytes 49160 | tf_op jit(solution)/shard_map/ppermute | solution.py:34
  14.5 2.2 %collective-permute-done.1.refs_1_ = s32[2,16,128]{2,1,0:T(8,128)S(1)} collective-permute-done((s32[2,16,128]{2,1,0:T(8,128)S(1)}, s32[2,16,128]{2,1,0:T(8,128)S(1)}, u32[]{:S(2)}, u32[]{:S(2)}) %collective-permute-start.1) | collective-permute-done | bytes 16416 | tf_op jit(solution)/shard_map/ppermute | solution.py:34
  16.7 3.6 %collective-permute-done.2.refs_1_ = bf16[1536,1280]{1,0:T(8,128)(2,1)} collective-permute-done((bf16[1536,1280]{1,0:T(8,128)(2,1)}, bf16[1536,1280]{1,0:T(8,128)(2,1)}, u32[]{:S(2)}, u32[]{:S(2)}) %collective-permute-start.2) | collective-permute-done | bytes 3932192 | tf_op jit(solution)/shard_map/ppermute | solution.py:34
  20.3 14.9 %shard_map.69 = (bf16[2,8,96,512]{3,2,1,0:T(8,128)(2,1)S(1)}, bf16[2,1536,1280]{2,1,0:T(8,128)(2,1)S(1)}, bf16[14,256,2560]{2,1,0:T(8,128)(2,1)S(1)}, bf16[1,8,9...) custom-call(s32[1,16,128]{2,1,0:T(8,128)} %bitcast.48, bf16[1536,1280]{1,0:T(8,128)(2,1)} %shard_map.66.refs_0_, ...), custom_call_target="tpu_custom_call" | custom-call | flops 8053063680 | bytes 8388608 | tf_op jit(solution)/shard_map/pallas_call | solution.py:236
  35.3 2.9 %collective-permute-start.8 = (bf16[1,8,96,512]{3,2,1,0:T(8,128)(2,1)S(1)}, bf16[1,8,96,512]{3,2,1,0:T(8,128)(2,1)S(1)}, u32[]{:S(2)}, u32[]{:S(2)}) collective-permute-start(bf16[1,8,96,512]{3,2,1,0:T(8,128)(2,1)S(1)} %get-tuple-element.83), channel_id=1, source_target_pairs={{0,2},{1,3},{2,0},{3,1},{4,6},{5,7},{6,4},{7,5},{8,10},{9,11},{10,... | collective-permute-start | bytes 2359304 | tf_op jit(solution)/shard_map/ppermute | solution.py:34
  41.3 2.6 %collective-permute-start.6 = (s32[4,16,128]{2,1,0:T(8,128)S(1)}, s32[4,16,128]{2,1,0:T(8,128)S(1)}, u32[]{:S(2)}, u32[]{:S(2)}) collective-permute-start(s32[4,16,128]{2,1,0:T(8,128)S(1)} %shard_map.68.refs_0_), channel_id=1, source_target_pairs={{0,16},{1,17},{2,18},{3,19},{4,20},{5,21},{6,22},{7,23},{8,24},{9,... | collective-permute-start | bytes 98312 | tf_op jit(solution)/shard_map/ppermute | solution.py:34
  44.1 4.8 %shard_map.70 = (bf16[2,8,96,256]{3,2,1,0:T(8,128)(2,1)S(1)}, bf16[2,8,96,256]{3,2,1,0:T(8,128)(2,1)S(1)}) custom-call(s32[1,16,128]{2,1,0:T(8,128)S(1)} %bitcast.49, bf16[2,1536,1280]{2,1,0:T(8,128)(2,1)S(1)} %get-tuple-element.86.refs_0_, bf16[14,256,2560]{2,1,0:T(8,128)(2,1)S(1)} %get-tuple-element.87.refs_1_), custom_call_target="tpu_custom_call" | custom-call | flops 4026531840 | bytes 4194304 | tf_op jit(solution)/shard_map/pallas_call | solution.py:236
  49.7 4.8 %shard_map.72 = (bf16[2,8,96,256]{3,2,1,0:T(8,128)(2,1)S(1)}, bf16[1,8,96,256]{3,2,1,0:T(8,128)(2,1)S(1)}, bf16[1,8,96,256]{3,2,1,0:T(8,128)(2,1)S(1)}) custom-call(s32[1,16,128]{2,1,0:T(8,128)S(1)} %bitcast.50, bf16[2,1536,1280]{2,1,0:T(8,128)(2,1)S(1)} %get-tuple-element.86.refs_0_, bf16[14,256,2560]{2,1,0:T(8,128)(2,1)S(1)} %get-tuple-element.87.refs_1_), custom_call_target="tpu_custom_call" | custom-call | flops 4026531840 | bytes 4194304 | tf_op jit(solution)/shard_map/pallas_call | solution.py:236
  56.4 2.2 %collective-permute-done.9.refs_1_ = bf16[1,8,96,512]{3,2,1,0:T(8,128)(2,1)S(1)} collective-permute-done((bf16[1,8,96,512]{3,2,1,0:T(8,128)(2,1)S(1)}, bf16[1,8,96,512]{3,2,1,0:T(8,128)(2,1)S(1)}, u32[]{:S(2)}, u32[]{:S(2)}) %collective-permute-start.9) | collective-permute-done | bytes 786464 | tf_op jit(solution)/shard_map/ppermute | solution.py:34
  59.4 1.6 %collective-permute-start.13 = (bf16[1,4,128,512]{3,2,1,0:T(8,128)(2,1)S(1)}, bf16[1,4,128,512]{3,2,1,0:T(8,128)(2,1)S(1)}, u32[]{:S(2)}, u32[]{:S(2)}) collective-permute-start(bf16[1,4,128,512]{3,2,1,0:T(8,128)(2,1)S(1)} %get-tuple-element.95), channel_id=1, source_target_pairs={{0,4},{1,5},{2,6},{3,7},{4,0},{5,1},{6,2},{7,3},{8,12},{9,13},{10,... | collective-permute-start | bytes 1572872 | tf_op jit(solution)/shard_map/ppermute | solution.py:34
  61.5 9.8 %shard_map.74 = (bf16[2,8,96,512]{3,2,1,0:T(8,128)(2,1)S(1)}, bf16[1,8,96,512]{3,2,1,0:T(8,128)(2,1)S(1)}, bf16[1,8,96,512]{3,2,1,0:T(8,128)(2,1)S(1)}) custom-call(s32[1,16,128]{2,1,0:T(8,128)S(1)} %bitcast.51, bf16[2,1536,1280]{2,1,0:T(8,128)(2,1)S(1)} %get-tuple-element.86.refs_0_, bf16[14,256,2560]{2,1,0:T(8,128)(2,1)S(1)} %get-tuple-element.87.refs_1_), custom_call_target="tpu_custom_call" | custom-call | flops 8053063680 | bytes 8388608 | tf_op jit(solution)/shard_map/pallas_call | solution.py:236
  73.8 1.6 %collective-permute-start.15 = (bf16[2,4,128,256]{3,2,1,0:T(8,128)(2,1)S(1)}, bf16[2,4,128,256]{3,2,1,0:T(8,128)(2,1)S(1)}, u32[]{:S(2)}, u32[]{:S(2)}) collective-permute-start(bf16[2,4,128,256]{3,2,1,0:T(8,128)(2,1)S(1)} %shard_map.75), channel_id=1, source_target_pairs={{0,8},{1,9},{2,10},{3,11},{4,12},{5,13},{6,14},{7,15},{8,0},{9,1},... | collective-permute-start | bytes 1572872 | tf_op jit(solution)/shard_map/ppermute | solution.py:34
  76.0 2.4 %collective-permute-done.13.refs_2_ = bf16[1,4,128,512]{3,2,1,0:T(8,128)(2,1)S(1)} collective-permute-done((bf16[1,4,128,512]{3,2,1,0:T(8,128)(2,1)S(1)}, bf16[1,4,128,512]{3,2,1,0:T(8,128)(2,1)S(1)}, u32[]{:S(2)}, u32[]{:S(2)}) %collective-permute-start.13) | collective-permute-done | bytes 524320 | tf_op jit(solution)/shard_map/ppermute | solution.py:34
  80.7 10.9 %collective-permute-done.15.refs_2_ = bf16[2,4,128,256]{3,2,1,0:T(8,128)(2,1)S(1)} collective-permute-done((bf16[2,4,128,256]{3,2,1,0:T(8,128)(2,1)S(1)}, bf16[2,4,128,256]{3,2,1,0:T(8,128)(2,1)S(1)}, u32[]{:S(2)}, u32[]{:S(2)}) %collective-permute-start.15) | collective-permute-done | bytes 524320 | tf_op jit(solution)/shard_map/ppermute | solution.py:34
  92.1 1.8 %collective-permute-start.19 = (bf16[2,2,128,256]{3,2,1,0:T(8,128)(2,1)S(1)}, bf16[2,2,128,256]{3,2,1,0:T(8,128)(2,1)S(1)}, u32[]{:S(2)}, u32[]{:S(2)}) collective-permute-start(bf16[2,2,128,256]{3,2,1,0:T(8,128)(2,1)S(1)} %get-tuple-element.111), channel_id=1, source_target_pairs={{0,16},{1,17},{2,18},{3,19},{4,20},{5,21},{6,22},{7,23},{8,24},{9,... | collective-permute-start | bytes 786440 | tf_op jit(solution)/shard_map/ppermute | solution.py:34
  96.9 4.2 %collective-permute-done.18.refs_0_ = bf16[2,2,128,512]{3,2,1,0:T(8,128)(2,1)S(1)} collective-permute-done((bf16[2,2,128,512]{3,2,1,0:T(8,128)(2,1)S(1)}, bf16[2,2,128,512]{3,2,1,0:T(8,128)(2,1)S(1)}, u32[]{:S(2)}, u32[]{:S(2)}) %collective-permute-start.18) | collective-permute-done | bytes 524320 | tf_op jit(solution)/shard_map/ppermute | solution.py:34
  101.1 2.5 %collective-permute-done.19.refs_0_ = bf16[2,2,128,256]{3,2,1,0:T(8,128)(2,1)S(1)} collective-permute-done((bf16[2,2,128,256]{3,2,1,0:T(8,128)(2,1)S(1)}, bf16[2,2,128,256]{3,2,1,0:T(8,128)(2,1)S(1)}, u32[]{:S(2)}, u32[]{:S(2)}) %collective-permute-start.19) | collective-permute-done | bytes 262176 | tf_op jit(solution)/shard_map/ppermute | solution.py:34
  103.7 4.8 %shard_map.82 = (bf16[2,8,96,256]{3,2,1,0:T(8,128)(2,1)S(1)}, bf16[1,8,96,256]{3,2,1,0:T(8,128)(2,1)S(1)}, bf16[1,8,96,256]{3,2,1,0:T(8,128)(2,1)S(1)}) custom-call(s32[1,16,128]{2,1,0:T(8,128)S(1)} %bitcast.54, bf16[2,1536,1280]{2,1,0:T(8,128)(2,1)S(1)} %get-tuple-element.86.refs_0_, bf16[14,256,2560]{2,1,0:T(8,128)(2,1)S(1)} %get-tuple-element.87.refs_1_), custom_call_target="tpu_custom_call" | custom-call | flops 4026531840 | bytes 4194304 | tf_op jit(solution)/shard_map/pallas_call | solution.py:236
  112.0 2.4 %collective-permute-start.25 = (bf16[1,2,128,512]{3,2,1,0:T(8,128)(2,1)S(1)}, bf16[1,2,128,512]{3,2,1,0:T(8,128)(2,1)S(1)}, u32[]{:S(2)}, u32[]{:S(2)}) collective-permute-start(bf16[1,2,128,512]{3,2,1,0:T(8,128)(2,1)S(1)} %get-tuple-element.125), channel_id=1, source_target_pairs={{0,8},{1,9},{2,10},{3,11},{4,12},{5,13},{6,14},{7,15},{8,0},{9,1},... | collective-permute-start | bytes 786440 | tf_op jit(solution)/shard_map/ppermute | solution.py:34
  114.4 1.8 %collective-permute-start.26 = (bf16[1,2,128,512]{3,2,1,0:T(8,128)(2,1)S(1)}, bf16[1,2,128,512]{3,2,1,0:T(8,128)(2,1)S(1)}, u32[]{:S(2)}, u32[]{:S(2)}) collective-permute-start(bf16[1,2,128,512]{3,2,1,0:T(8,128)(2,1)S(1)} %get-tuple-element.126), channel_id=1, source_target_pairs={{0,16},{1,17},{2,18},{3,19},{4,20},{5,21},{6,22},{7,23},{8,24},{9,... | collective-permute-start | bytes 786440 | tf_op jit(solution)/shard_map/ppermute | solution.py:34
  116.2 10.1 %collective-permute-done.22.refs_1_ = bf16[2,128,512]{2,1,0:T(8,128)(2,1)S(1)} collective-permute-done((bf16[2,128,512]{2,1,0:T(8,128)(2,1)S(1)}, bf16[2,128,512]{2,1,0:T(8,128)(2,1)S(1)}, u32[]{:S(2)}, u32[]{:S(2)}) %collective-permute-start.22) | collective-permute-done | bytes 262176 | tf_op jit(solution)/shard_map/ppermute | solution.py:34
  126.3 1.7 %collective-permute-start.28 = (bf16[1,4,128,256]{3,2,1,0:T(8,128)(2,1)S(1)}, bf16[1,4,128,256]{3,2,1,0:T(8,128)(2,1)S(1)}, u32[]{:S(2)}, u32[]{:S(2)}) collective-permute-start(bf16[1,4,128,256]{3,2,1,0:T(8,128)(2,1)S(1)} %get-tuple-element.105), channel_id=1, source_target_pairs={{0,4},{1,5},{2,6},{3,7},{4,0},{5,1},{6,2},{7,3},{8,12},{9,13},{10,... | collective-permute-start | bytes 786440 | tf_op jit(solution)/shard_map/ppermute | solution.py:34
  129.0 2.0 %collective-permute-start.30 = (bf16[1,4,128,256]{3,2,1,0:T(8,128)(2,1)S(1)}, bf16[1,4,128,256]{3,2,1,0:T(8,128)(2,1)S(1)}, u32[]{:S(2)}, u32[]{:S(2)}) collective-permute-start(bf16[1,4,128,256]{3,2,1,0:T(8,128)(2,1)S(1)} %get-tuple-element.131), channel_id=1, source_target_pairs={{0,2},{1,3},{2,0},{3,1},{4,6},{5,7},{6,4},{7,5},{8,10},{9,11},{10,... | collective-permute-start | bytes 786440 | tf_op jit(solution)/shard_map/ppermute | solution.py:34
  133.2 1.8 %collective-permute-start.31 = (bf16[1,2,128,256]{3,2,1,0:T(8,128)(2,1)S(1)}, bf16[1,2,128,256]{3,2,1,0:T(8,128)(2,1)S(1)}, u32[]{:S(2)}, u32[]{:S(2)}) collective-permute-start(bf16[1,2,128,256]{3,2,1,0:T(8,128)(2,1)S(1)} %get-tuple-element.137), channel_id=1, source_target_pairs={{0,4},{1,5},{2,6},{3,7},{4,0},{5,1},{6,2},{7,3},{8,12},{9,13},{10,... | collective-permute-start | bytes 393224 | tf_op jit(solution)/shard_map/ppermute | solution.py:34
  135.6 3.6 %collective-permute-start.34 = (bf16[1,128,512]{2,1,0:T(8,128)(2,1)S(1)}, bf16[1,128,512]{2,1,0:T(8,128)(2,1)S(1)}, u32[]{:S(2)}, u32[]{:S(2)}) collective-permute-start(bf16[1,128,512]{2,1,0:T(8,128)(2,1)S(1)} %get-tuple-element.134), channel_id=1, source_target_pairs={{0,8},{1,9},{2,10},{3,11},{4,12},{5,13},{6,14},{7,15},{8,0},{9,1},... | collective-permute-start | bytes 393224 | tf_op jit(solution)/shard_map/ppermute | solution.py:34
  141.0 1.9 %collective-permute-start.37 = (bf16[2,128,256]{2,1,0:T(8,128)(2,1)S(1)}, bf16[2,128,256]{2,1,0:T(8,128)(2,1)S(1)}, u32[]{:S(2)}, u32[]{:S(2)}) collective-permute-start(bf16[2,128,256]{2,1,0:T(8,128)(2,1)S(1)} %shard_map.89), channel_id=1, source_target_pairs={{0,16},{1,17},{2,18},{3,19},{4,20},{5,21},{6,22},{7,23},{8,24},{9,... | collective-permute-start | bytes 393224 | tf_op jit(solution)/shard_map/ppermute | solution.py:34
  145.8 1.8 %collective-permute-start.39 = (bf16[1,128,256]{2,1,0:T(8,128)(2,1)S(1)}, bf16[1,128,256]{2,1,0:T(8,128)(2,1)S(1)}, u32[]{:S(2)}, u32[]{:S(2)}) collective-permute-start(bf16[1,128,256]{2,1,0:T(8,128)(2,1)S(1)} %get-tuple-element.119), channel_id=1, source_target_pairs={{0,2},{1,3},{2,0},{3,1},{4,6},{5,7},{6,4},{7,5},{8,10},{9,11},{10,... | collective-permute-start | bytes 196616 | tf_op jit(solution)/shard_map/ppermute | solution.py:34
  149.0 2.5 %collective-permute-start.41 = (bf16[1,128,256]{2,1,0:T(8,128)(2,1)S(1)}, bf16[1,128,256]{2,1,0:T(8,128)(2,1)S(1)}, u32[]{:S(2)}, u32[]{:S(2)}) collective-permute-start(bf16[1,128,256]{2,1,0:T(8,128)(2,1)S(1)} %get-tuple-element.147), channel_id=1, source_target_pairs={{0,8},{1,9},{2,10},{3,11},{4,12},{5,13},{6,14},{7,15},{8,0},{9,1},... | collective-permute-start | bytes 196616 | tf_op jit(solution)/shard_map/ppermute | solution.py:34
  151.7 2.1 %collective-permute-done.40.refs_2_ = bf16[1,128,256]{2,1,0:T(8,128)(2,1)S(1)} collective-permute-done((bf16[1,128,256]{2,1,0:T(8,128)(2,1)S(1)}, bf16[1,128,256]{2,1,0:T(8,128)(2,1)S(1)}, u32[]{:S(2)}, u32[]{:S(2)}) %collective-permute-start.40) | collective-permute-done | bytes 65568 | tf_op jit(solution)/shard_map/ppermute | solution.py:34
  (102 shorter events, 33.1 us)
Async XLA Ops:
  0.0 20.3 %collective-permute-start.3 = (bf16[3584,640]{1,0:T(8,128)(2,1)}, bf16[3584,640]{1,0:T(8,128)(2,1)}, u32[]{:S(2)}, u32[]{:S(2)}) collective-permute-start(bf16[3584,640]{1,0:T(8,128)(2,1)} %bitcast.69), channel_id=1, source_target_pairs={{0,1},{1,0},{2,3},{3,2},{4,5},{5,4},{6,7},{7,6},{8,9},{9,8},{10,11... | collective-permute-start | bytes 13762568 | tf_op jit(solution)/shard_map/ppermute | solution.py:34
  0.5 19.9 %collective-permute-start.4 = (bf16[3584,640]{1,0:T(8,128)(2,1)}, bf16[3584,640]{1,0:T(8,128)(2,1)}, u32[]{:S(2)}, u32[]{:S(2)}) collective-permute-start(bf16[3584,640]{1,0:T(8,128)(2,1)} %bitcast.71), channel_id=1, source_target_pairs={{0,1},{1,0},{2,3},{3,2},{4,5},{5,4},{6,7},{7,6},{8,9},{9,8},{10,11... | collective-permute-start | bytes 13762568 | tf_op jit(solution)/shard_map/ppermute | solution.py:34
  4.9 15.4 %collective-permute-start.2 = (bf16[1536,1280]{1,0:T(8,128)(2,1)}, bf16[1536,1280]{1,0:T(8,128)(2,1)}, u32[]{:S(2)}, u32[]{:S(2)}) collective-permute-start(bf16[1536,1280]{1,0:T(8,128)(2,1)} %shard_map.64), channel_id=1, source_target_pairs={{0,1},{1,0},{2,3},{3,2},{4,5},{5,4},{6,7},{7,6},{8,9},{9,8},{10,11... | collective-permute-start | bytes 11796488 | tf_op jit(solution)/shard_map/ppermute | solution.py:34
  6.0 6.9 %collective-permute-start = (s32[1,16,128]{2,1,0:T(8,128)S(1)}, s32[1,16,128]{2,1,0:T(8,128)S(1)}, u32[]{:S(2)}, u32[]{:S(2)}) collective-permute-start(s32[1,16,128]{2,1,0:T(8,128)S(1)} %bitcast.46), channel_id=1, source_target_pairs={{0,2},{1,3},{2,0},{3,1},{4,6},{5,7},{6,4},{7,5},{8,10},{9,11},{10,... | collective-permute-start | bytes 24584 | tf_op jit(solution)/shard_map/ppermute | solution.py:34
  35.3 21.2 %collective-permute-start.8 = (bf16[1,8,96,512]{3,2,1,0:T(8,128)(2,1)S(1)}, bf16[1,8,96,512]{3,2,1,0:T(8,128)(2,1)S(1)}, u32[]{:S(2)}, u32[]{:S(2)}) collective-permute-start(bf16[1,8,96,512]{3,2,1,0:T(8,128)(2,1)S(1)} %get-tuple-element.83), channel_id=1, source_target_pairs={{0,2},{1,3},{2,0},{3,1},{4,6},{5,7},{6,4},{7,5},{8,10},{9,11},{10,... | collective-permute-start | bytes 2359304 | tf_op jit(solution)/shard_map/ppermute | solution.py:34
  38.2 20.4 %collective-permute-start.9 = (bf16[1,8,96,512]{3,2,1,0:T(8,128)(2,1)S(1)}, bf16[1,8,96,512]{3,2,1,0:T(8,128)(2,1)S(1)}, u32[]{:S(2)}, u32[]{:S(2)}) collective-permute-start(bf16[1,8,96,512]{3,2,1,0:T(8,128)(2,1)S(1)} %get-tuple-element.84), channel_id=1, source_target_pairs={{0,4},{1,5},{2,6},{3,7},{4,0},{5,1},{6,2},{7,3},{8,12},{9,13},{10,... | collective-permute-start | bytes 2359304 | tf_op jit(solution)/shard_map/ppermute | solution.py:34
  39.7 9.2 %collective-permute-start.5 = (s32[4,16,128]{2,1,0:T(8,128)S(1)}, s32[4,16,128]{2,1,0:T(8,128)S(1)}, u32[]{:S(2)}, u32[]{:S(2)}) collective-permute-start(s32[4,16,128]{2,1,0:T(8,128)S(1)} %shard_map.68.refs_0_), channel_id=1, source_target_pairs={{0,8},{1,9},{2,10},{3,11},{4,12},{5,13},{6,14},{7,15},{8,0},{9,1},... | collective-permute-start | bytes 98312 | tf_op jit(solution)/shard_map/ppermute | solution.py:34
  41.3 8.4 %collective-permute-start.6 = (s32[4,16,128]{2,1,0:T(8,128)S(1)}, s32[4,16,128]{2,1,0:T(8,128)S(1)}, u32[]{:S(2)}, u32[]{:S(2)}) collective-permute-start(s32[4,16,128]{2,1,0:T(8,128)S(1)} %shard_map.68.refs_0_), channel_id=1, source_target_pairs={{0,16},{1,17},{2,18},{3,19},{4,20},{5,21},{6,22},{7,23},{8,24},{9,... | collective-permute-start | bytes 98312 | tf_op jit(solution)/shard_map/ppermute | solution.py:34
  48.9 24.9 %collective-permute-start.12 = (bf16[2,8,96,256]{3,2,1,0:T(8,128)(2,1)S(1)}, bf16[2,8,96,256]{3,2,1,0:T(8,128)(2,1)S(1)}, u32[]{:S(2)}, u32[]{:S(2)}) collective-permute-start(bf16[2,8,96,256]{3,2,1,0:T(8,128)(2,1)S(1)} %get-tuple-element.88), channel_id=1, source_target_pairs={{0,8},{1,9},{2,10},{3,11},{4,12},{5,13},{6,14},{7,15},{8,0},{9,1},... | collective-permute-start | bytes 2359304 | tf_op jit(solution)/shard_map/ppermute | solution.py:34
  54.5 16.8 %collective-permute-start.10 = (bf16[1,8,96,256]{3,2,1,0:T(8,128)(2,1)S(1)}, bf16[1,8,96,256]{3,2,1,0:T(8,128)(2,1)S(1)}, u32[]{:S(2)}, u32[]{:S(2)}) collective-permute-start(bf16[1,8,96,256]{3,2,1,0:T(8,128)(2,1)S(1)} %get-tuple-element.91), channel_id=1, source_target_pairs={{0,2},{1,3},{2,0},{3,1},{4,6},{5,7},{6,4},{7,5},{8,10},{9,11},{10,... | collective-permute-start | bytes 1179656 | tf_op jit(solution)/shard_map/ppermute | solution.py:34
  55.1 17.8 %collective-permute-start.11 = (bf16[1,8,96,256]{3,2,1,0:T(8,128)(2,1)S(1)}, bf16[1,8,96,256]{3,2,1,0:T(8,128)(2,1)S(1)}, u32[]{:S(2)}, u32[]{:S(2)}) collective-permute-start(bf16[1,8,96,256]{3,2,1,0:T(8,128)(2,1)S(1)} %get-tuple-element.92), channel_id=1, source_target_pairs={{0,4},{1,5},{2,6},{3,7},{4,0},{5,1},{6,2},{7,3},{8,12},{9,13},{10,... | collective-permute-start | bytes 1179656 | tf_op jit(solution)/shard_map/ppermute | solution.py:34
  59.4 19.0 %collective-permute-start.13 = (bf16[1,4,128,512]{3,2,1,0:T(8,128)(2,1)S(1)}, bf16[1,4,128,512]{3,2,1,0:T(8,128)(2,1)S(1)}, u32[]{:S(2)}, u32[]{:S(2)}) collective-permute-start(bf16[1,4,128,512]{3,2,1,0:T(8,128)(2,1)S(1)} %get-tuple-element.95), channel_id=1, source_target_pairs={{0,4},{1,5},{2,6},{3,7},{4,0},{5,1},{6,2},{7,3},{8,12},{9,13},{10,... | collective-permute-start | bytes 1572872 | tf_op jit(solution)/shard_map/ppermute | solution.py:34
  61.0 17.4 %collective-permute-start.14 = (bf16[1,4,128,512]{3,2,1,0:T(8,128)(2,1)S(1)}, bf16[1,4,128,512]{3,2,1,0:T(8,128)(2,1)S(1)}, u32[]{:S(2)}, u32[]{:S(2)}) collective-permute-start(bf16[1,4,128,512]{3,2,1,0:T(8,128)(2,1)S(1)} %get-tuple-element.96), channel_id=1, source_target_pairs={{0,2},{1,3},{2,0},{3,1},{4,6},{5,7},{6,4},{7,5},{8,10},{9,11},{10,... | collective-permute-start | bytes 1572872 | tf_op jit(solution)/shard_map/ppermute | solution.py:34
  71.3 22.6 %collective-permute-start.16 = (bf16[1,8,96,512]{3,2,1,0:T(8,128)(2,1)S(1)}, bf16[1,8,96,512]{3,2,1,0:T(8,128)(2,1)S(1)}, u32[]{:S(2)}, u32[]{:S(2)}) collective-permute-start(bf16[1,8,96,512]{3,2,1,0:T(8,128)(2,1)S(1)} %get-tuple-element.98), channel_id=1, source_target_pairs={{0,2},{1,3},{2,0},{3,1},{4,6},{5,7},{6,4},{7,5},{8,10},{9,11},{10,... | collective-permute-start | bytes 2359304 | tf_op jit(solution)/shard_map/ppermute | solution.py:34
  72.8 21.2 %collective-permute-start.17 = (bf16[1,8,96,512]{3,2,1,0:T(8,128)(2,1)S(1)}, bf16[1,8,96,512]{3,2,1,0:T(8,128)(2,1)S(1)}, u32[]{:S(2)}, u32[]{:S(2)}) collective-permute-start(bf16[1,8,96,512]{3,2,1,0:T(8,128)(2,1)S(1)} %get-tuple-element.99), channel_id=1, source_target_pairs={{0,4},{1,5},{2,6},{3,7},{4,0},{5,1},{6,2},{7,3},{8,12},{9,13},{10,... | collective-permute-start | bytes 2359304 | tf_op jit(solution)/shard_map/ppermute | solution.py:34
  73.8 17.7 %collective-permute-start.15 = (bf16[2,4,128,256]{3,2,1,0:T(8,128)(2,1)S(1)}, bf16[2,4,128,256]{3,2,1,0:T(8,128)(2,1)S(1)}, u32[]{:S(2)}, u32[]{:S(2)}) collective-permute-start(bf16[2,4,128,256]{3,2,1,0:T(8,128)(2,1)S(1)} %shard_map.75), channel_id=1, source_target_pairs={{0,8},{1,9},{2,10},{3,11},{4,12},{5,13},{6,14},{7,15},{8,0},{9,1},... | collective-permute-start | bytes 1572872 | tf_op jit(solution)/shard_map/ppermute | solution.py:34
  79.1 21.9 %collective-permute-start.18 = (bf16[2,2,128,512]{3,2,1,0:T(8,128)(2,1)S(1)}, bf16[2,2,128,512]{3,2,1,0:T(8,128)(2,1)S(1)}, u32[]{:S(2)}, u32[]{:S(2)}) collective-permute-start(bf16[2,2,128,512]{3,2,1,0:T(8,128)(2,1)S(1)} %get-tuple-element.108), channel_id=1, source_target_pairs={{0,8},{1,9},{2,10},{3,11},{4,12},{5,13},{6,14},{7,15},{8,0},{9,1},... | collective-permute-start | bytes 1572872 | tf_op jit(solution)/shard_map/ppermute | solution.py:34
  92.1 11.6 %collective-permute-start.19 = (bf16[2,2,128,256]{3,2,1,0:T(8,128)(2,1)S(1)}, bf16[2,2,128,256]{3,2,1,0:T(8,128)(2,1)S(1)}, u32[]{:S(2)}, u32[]{:S(2)}) collective-permute-start(bf16[2,2,128,256]{3,2,1,0:T(8,128)(2,1)S(1)} %get-tuple-element.111), channel_id=1, source_target_pairs={{0,16},{1,17},{2,18},{3,19},{4,20},{5,21},{6,22},{7,23},{8,24},{9,... | collective-permute-start | bytes 786440 | tf_op jit(solution)/shard_map/ppermute | solution.py:34
  94.8 16.2 %collective-permute-start.20 = (bf16[1,4,128,512]{3,2,1,0:T(8,128)(2,1)S(1)}, bf16[1,4,128,512]{3,2,1,0:T(8,128)(2,1)S(1)}, u32[]{:S(2)}, u32[]{:S(2)}) collective-permute-start(bf16[1,4,128,512]{3,2,1,0:T(8,128)(2,1)S(1)} %get-tuple-element.114), channel_id=1, source_target_pairs={{0,4},{1,5},{2,6},{3,7},{4,0},{5,1},{6,2},{7,3},{8,12},{9,13},{10,... | collective-permute-start | bytes 1572872 | tf_op jit(solution)/shard_map/ppermute | solution.py:34
  96.3 14.9 %collective-permute-start.21 = (bf16[1,4,128,512]{3,2,1,0:T(8,128)(2,1)S(1)}, bf16[1,4,128,512]{3,2,1,0:T(8,128)(2,1)S(1)}, u32[]{:S(2)}, u32[]{:S(2)}) collective-permute-start(bf16[1,4,128,512]{3,2,1,0:T(8,128)(2,1)S(1)} %get-tuple-element.115), channel_id=1, source_target_pairs={{0,2},{1,3},{2,0},{3,1},{4,6},{5,7},{6,4},{7,5},{8,10},{9,11},{10,... | collective-permute-start | bytes 1572872 | tf_op jit(solution)/shard_map/ppermute | solution.py:34
  108.5 17.8 %collective-permute-start.23 = (bf16[1,8,96,256]{3,2,1,0:T(8,128)(2,1)S(1)}, bf16[1,8,96,256]{3,2,1,0:T(8,128)(2,1)S(1)}, u32[]{:S(2)}, u32[]{:S(2)}) collective-permute-start(bf16[1,8,96,256]{3,2,1,0:T(8,128)(2,1)S(1)} %get-tuple-element.121), channel_id=1, source_target_pairs={{0,2},{1,3},{2,0},{3,1},{4,6},{5,7},{6,4},{7,5},{8,10},{9,11},{10,... | collective-permute-start | bytes 1179656 | tf_op jit(solution)/shard_map/ppermute | solution.py:34
  109.0 17.3 %collective-permute-start.22 = (bf16[2,128,512]{2,1,0:T(8,128)(2,1)S(1)}, bf16[2,128,512]{2,1,0:T(8,128)(2,1)S(1)}, u32[]{:S(2)}, u32[]{:S(2)}) collective-permute-start(bf16[2,128,512]{2,1,0:T(8,128)(2,1)S(1)} %shard_map.80), channel_id=1, source_target_pairs={{0,16},{1,17},{2,18},{3,19},{4,20},{5,21},{6,22},{7,23},{8,24},{9,... | collective-permute-start | bytes 786440 | tf_op jit(solution)/shard_map/ppermute | solution.py:34
  109.4 18.8 %collective-permute-start.24 = (bf16[1,8,96,256]{3,2,1,0:T(8,128)(2,1)S(1)}, bf16[1,8,96,256]{3,2,1,0:T(8,128)(2,1)S(1)}, u32[]{:S(2)}, u32[]{:S(2)}) collective-permute-start(bf16[1,8,96,256]{3,2,1,0:T(8,128)(2,1)S(1)} %get-tuple-element.122), channel_id=1, source_target_pairs={{0,4},{1,5},{2,6},{3,7},{4,0},{5,1},{6,2},{7,3},{8,12},{9,13},{10,... | collective-permute-start | bytes 1179656 | tf_op jit(solution)/shard_map/ppermute | solution.py:34
  112.0 17.1 %collective-permute-start.25 = (bf16[1,2,128,512]{3,2,1,0:T(8,128)(2,1)S(1)}, bf16[1,2,128,512]{3,2,1,0:T(8,128)(2,1)S(1)}, u32[]{:S(2)}, u32[]{:S(2)}) collective-permute-start(bf16[1,2,128,512]{3,2,1,0:T(8,128)(2,1)S(1)} %get-tuple-element.125), channel_id=1, source_target_pairs={{0,8},{1,9},{2,10},{3,11},{4,12},{5,13},{6,14},{7,15},{8,0},{9,1},... | collective-permute-start | bytes 786440 | tf_op jit(solution)/shard_map/ppermute | solution.py:34
  114.4 16.7 %collective-permute-start.26 = (bf16[1,2,128,512]{3,2,1,0:T(8,128)(2,1)S(1)}, bf16[1,2,128,512]{3,2,1,0:T(8,128)(2,1)S(1)}, u32[]{:S(2)}, u32[]{:S(2)}) collective-permute-start(bf16[1,2,128,512]{3,2,1,0:T(8,128)(2,1)S(1)} %get-tuple-element.126), channel_id=1, source_target_pairs={{0,16},{1,17},{2,18},{3,19},{4,20},{5,21},{6,22},{7,23},{8,24},{9,... | collective-permute-start | bytes 786440 | tf_op jit(solution)/shard_map/ppermute | solution.py:34
  129.0 10.2 %collective-permute-start.30 = (bf16[1,4,128,256]{3,2,1,0:T(8,128)(2,1)S(1)}, bf16[1,4,128,256]{3,2,1,0:T(8,128)(2,1)S(1)}, u32[]{:S(2)}, u32[]{:S(2)}) collective-permute-start(bf16[1,4,128,256]{3,2,1,0:T(8,128)(2,1)S(1)} %get-tuple-element.131), channel_id=1, source_target_pairs={{0,2},{1,3},{2,0},{3,1},{4,6},{5,7},{6,4},{7,5},{8,10},{9,11},{10,... | collective-permute-start | bytes 786440 | tf_op jit(solution)/shard_map/ppermute | solution.py:34
  135.4 8.8 %collective-permute-start.33 = (bf16[1,128,512]{2,1,0:T(8,128)(2,1)S(1)}, bf16[1,128,512]{2,1,0:T(8,128)(2,1)S(1)}, u32[]{:S(2)}, u32[]{:S(2)}) collective-permute-start(bf16[1,128,512]{2,1,0:T(8,128)(2,1)S(1)} %get-tuple-element.133), channel_id=1, source_target_pairs={{0,16},{1,17},{2,18},{3,19},{4,20},{5,21},{6,22},{7,23},{8,24},{9,... | collective-permute-start | bytes 393224 | tf_op jit(solution)/shard_map/ppermute | solution.py:34
  135.6 10.2 %collective-permute-start.34 = (bf16[1,128,512]{2,1,0:T(8,128)(2,1)S(1)}, bf16[1,128,512]{2,1,0:T(8,128)(2,1)S(1)}, u32[]{:S(2)}, u32[]{:S(2)}) collective-permute-start(bf16[1,128,512]{2,1,0:T(8,128)(2,1)S(1)} %get-tuple-element.134), channel_id=1, source_target_pairs={{0,8},{1,9},{2,10},{3,11},{4,12},{5,13},{6,14},{7,15},{8,0},{9,1},... | collective-permute-start | bytes 393224 | tf_op jit(solution)/shard_map/ppermute | solution.py:34
  139.7 8.0 %collective-permute-start.35 = (bf16[1,2,128,256]{3,2,1,0:T(8,128)(2,1)S(1)}, bf16[1,2,128,256]{3,2,1,0:T(8,128)(2,1)S(1)}, u32[]{:S(2)}, u32[]{:S(2)}) collective-permute-start(bf16[1,2,128,256]{3,2,1,0:T(8,128)(2,1)S(1)} %get-tuple-element.141), channel_id=1, source_target_pairs={{0,8},{1,9},{2,10},{3,11},{4,12},{5,13},{6,14},{7,15},{8,0},{9,1},... | collective-permute-start | bytes 393224 | tf_op jit(solution)/shard_map/ppermute | solution.py:34
  139.8 7.9 %collective-permute-start.36 = (bf16[1,2,128,256]{3,2,1,0:T(8,128)(2,1)S(1)}, bf16[1,2,128,256]{3,2,1,0:T(8,128)(2,1)S(1)}, u32[]{:S(2)}, u32[]{:S(2)}) collective-permute-start(bf16[1,2,128,256]{3,2,1,0:T(8,128)(2,1)S(1)} %get-tuple-element.142), channel_id=1, source_target_pairs={{0,16},{1,17},{2,18},{3,19},{4,20},{5,21},{6,22},{7,23},{8,24},{9,... | collective-permute-start | bytes 393224 | tf_op jit(solution)/shard_map/ppermute | solution.py:34
  141.0 10.5 %collective-permute-start.37 = (bf16[2,128,256]{2,1,0:T(8,128)(2,1)S(1)}, bf16[2,128,256]{2,1,0:T(8,128)(2,1)S(1)}, u32[]{:S(2)}, u32[]{:S(2)}) collective-permute-start(bf16[2,128,256]{2,1,0:T(8,128)(2,1)S(1)} %shard_map.89), channel_id=1, source_target_pairs={{0,16},{1,17},{2,18},{3,19},{4,20},{5,21},{6,22},{7,23},{8,24},{9,... | collective-permute-start | bytes 393224 | tf_op jit(solution)/shard_map/ppermute | solution.py:34
  144.2 7.3 %collective-permute-start.38 = (bf16[1,128,256]{2,1,0:T(8,128)(2,1)S(1)}, bf16[1,128,256]{2,1,0:T(8,128)(2,1)S(1)}, u32[]{:S(2)}, u32[]{:S(2)}) collective-permute-start(bf16[1,128,256]{2,1,0:T(8,128)(2,1)S(1)} %get-tuple-element.118), channel_id=1, source_target_pairs={{0,4},{1,5},{2,6},{3,7},{4,0},{5,1},{6,2},{7,3},{8,12},{9,13},{10,... | collective-permute-start | bytes 196616 | tf_op jit(solution)/shard_map/ppermute | solution.py:34
  (14 other events, 98.9 us)
